TPU v7x, 32 devices: a whole 2x2x4 slice. The times are simulated.
32 devices in a mesh: seq: 4 (over x, core), ctx: 8 (over z, y).
Axes of the slice: x: 2, y: 2, z: 4, core: 2. Of those that a mesh axis runs over, the one named last changes fastest.
Arguments:
- tokens: bfloat16 [4, 1024, 1024], P('seq', 'ctx'), may hold values from -6 to 6
- encoder_states: bfloat16 [4, 256, 1024], P('seq', 'ctx'), may hold values from -6 to 6
- cotangent: bfloat16 [4, 1024, 1024], P('seq', 'ctx'), may hold values from -6 to 6
- target_lengths: int32 [4], P('seq'), may hold values from 512 to 1024, as said below
- source_lengths: int32 [4], P('seq'), may hold values from 225 to 256, as said below
- block_table: int32 [8, 2], replicated, may hold values from 0 to 15, as said below
- self_qkv: bfloat16 [1024, 3072], P('seq'), may hold values from -0.1875 to 0.1875
- self_out: bfloat16 [1024, 1024], P('seq'), may hold values from -3 to 3
- cross_q: bfloat16 [1024, 1024], P('seq'), may hold values from -0.1875 to 0.1875
- cross_kv: bfloat16 [1024, 2048], P('seq'), may hold values from -0.1875 to 0.1875
- cross_out: bfloat16 [1024, 1024], P('seq'), may hold values from -3 to 3
- mlp_up: bfloat16 [1024, 8192], P('seq'), may hold values from -0.1875 to 0.1875
- mlp_down: bfloat16 [8192, 1024], P('seq'), may hold values from -0.0625 to 0.0625
- norm_gain: float32 [3, 1024], replicated, may hold values from 0.1 to 1.9
- norm_bias: float32 [3, 1024], replicated, may hold values from -1.5 to 1.5
- clip_limit: float32 [2, 16], replicated, may hold values from 2 to 16
Outputs:
- output: bfloat16 [4, 1024, 1024], P('seq', 'ctx')
- grad_tokens: float32 [4, 1024, 1024], P('seq', 'ctx')
- grad_encoder: float32 [4, 256, 1024], P('seq', 'ctx')
- grad_self_qkv: float32 [1024, 3072], P(('seq', 'ctx'))
- grad_self_out: float32 [1024, 1024], P(('seq', 'ctx'))
- grad_cross_q: float32 [1024, 1024], P(('seq', 'ctx'))
- grad_cross_kv: float32 [1024, 2048], P(('seq', 'ctx'))
- grad_cross_out: float32 [1024, 1024], P(('seq', 'ctx'))
- grad_mlp_up: float32 [1024, 8192], P(('seq', 'ctx'))
- grad_mlp_down: float32 [8192, 1024], P(('seq', 'ctx'))
- grad_norm_gain: float32 [3, 1024], P(None, ('seq', 'ctx'))
- grad_norm_bias: float32 [3, 1024], P(None, ('seq', 'ctx'))
- clipped_self: bfloat16 [1024, 2048], P('seq')
- clipped_cross: bfloat16 [1024, 2048], P('seq')
- head_peaks: float32 [2, 16], replicated
Inputs may be any that keep to these rules, and one draw needn't show every extreme that they name: `block_table`: row j names the two blocks of 64 positions held by device j of ctx; they are b and 15 - b for some b, and every block is named once. `target_lengths`: in every draw one slot is 1024 long. `source_lengths`: in every draw one sequence has all 256 states.
All inputs are finite; a program needn't handle non-finite values.
Results may differ from a plain program's by a relative error of at most 0.025.
Values may be sent and summed in bfloat16 or wider, within the bound.
A program may use at most 384 MiB of HBM per device.

v0:
```python
import jax
import jax.numpy as jnp
from jax import lax
from jax.sharding import PartitionSpec as P

H = 16
HD = 64


masked_score = -1000000000.0
norm_eps = 1e-05


def block_size(count):
    return max((step for step in range(1, min(count, 512) + 1) if count % step == 0))


def layer_norm(values, gain, bias):
    centered = values - jnp.mean(values, axis=-1, keepdims=True)
    spread = jnp.mean(centered * centered, axis=-1, keepdims=True)
    return centered * lax.rsqrt(spread + norm_eps) * gain + bias


def allowed_pairs(query_pos, key_pos, key_limit, causal):
    allowed = jnp.broadcast_to(
        (key_pos < key_limit)[None, :], (query_pos.shape[0], key_pos.shape[0])
    )
    if causal:
        allowed = allowed & (key_pos[None, :] <= query_pos[:, None])
    return allowed


def head_scores(query_heads, key_rows):
    key_heads = key_rows.reshape(key_rows.shape[0], H, HD)
    return jnp.einsum(
        "qhd,khd->hqk", query_heads, key_heads, preferred_element_type=jnp.float32
    ) * HD ** (-0.5)


def softmax_stats(query_heads, kv_rows, key_pos, query_pos, query_ok, key_limit, causal):
    count = kv_rows.shape[0]
    step = block_size(count)
    width = H * HD
    rows = query_heads.shape[0]

    def softmax_visit(carry, block):
        top, total, peak = carry
        block_rows, block_pos = block
        allowed = allowed_pairs(query_pos, block_pos, key_limit, causal)
        scores = jnp.where(
            allowed[None], head_scores(query_heads, block_rows[:, :width]), masked_score
        )
        new_top = jnp.maximum(top, jnp.max(scores, axis=-1))
        total = total * jnp.exp(top - new_top) + jnp.sum(
            jnp.exp(scores - new_top[..., None]), axis=-1
        )
        counted = jnp.where((allowed & query_ok[:, None])[None], scores, masked_score)
        peak = jnp.maximum(peak, jnp.max(counted, axis=(1, 2)))
        return ((new_top, total, peak), None)

    start = (
        jnp.full((H, rows), -jnp.inf, jnp.float32),
        jnp.zeros((H, rows), jnp.float32),
        jnp.full((H,), masked_score, jnp.float32),
    )
    blocks = (kv_rows.reshape(count // step, step, 2 * width), key_pos.reshape(count // step, step))
    return lax.scan(softmax_visit, start, blocks)[0]


def attend_values(query_heads, kv_rows, key_pos, query_pos, key_limit, causal, top, total):
    count = kv_rows.shape[0]
    step = block_size(count)
    width = H * HD
    rows = query_heads.shape[0]

    def attend_visit(acc, block):
        block_rows, block_pos = block
        allowed = allowed_pairs(query_pos, block_pos, key_limit, causal)
        scores = jnp.where(
            allowed[None], head_scores(query_heads, block_rows[:, :width]), masked_score
        )
        weights = (jnp.exp(scores - top[..., None]) / total[..., None]).astype(jnp.bfloat16)
        value_heads = block_rows[:, width:].reshape(step, H, HD)
        return (
            acc
            + jnp.einsum("hqk,khd->qhd", weights, value_heads, preferred_element_type=jnp.float32),
            None,
        )

    blocks = (kv_rows.reshape(count // step, step, 2 * width), key_pos.reshape(count // step, step))
    acc = lax.scan(attend_visit, jnp.zeros((rows, H, HD), jnp.float32), blocks)[0]
    return acc.reshape(rows, width)


def query_grads(
    query_heads, kv_rows, key_pos, query_pos, key_limit, causal, top, total, grad_heads, delta
):
    count = kv_rows.shape[0]
    step = block_size(count)
    width = H * HD
    rows = query_heads.shape[0]

    def query_visit(acc, block):
        block_rows, block_pos = block
        allowed = allowed_pairs(query_pos, block_pos, key_limit, causal)
        scores = jnp.where(
            allowed[None], head_scores(query_heads, block_rows[:, :width]), masked_score
        )
        probs = jnp.exp(scores - top[..., None]) / total[..., None]
        value_heads = block_rows[:, width:].reshape(step, H, HD)
        dprobs = jnp.einsum(
            "qhd,khd->hqk", grad_heads, value_heads, preferred_element_type=jnp.float32
        )
        dscores = (probs * (dprobs - delta[..., None])).astype(jnp.bfloat16)
        key_heads = block_rows[:, :width].reshape(step, H, HD)
        return (
            acc
            + jnp.einsum("hqk,khd->qhd", dscores, key_heads, preferred_element_type=jnp.float32),
            None,
        )

    blocks = (kv_rows.reshape(count // step, step, 2 * width), key_pos.reshape(count // step, step))
    acc = lax.scan(query_visit, jnp.zeros((rows, H, HD), jnp.float32), blocks)[0]
    return acc.reshape(rows, width) * HD ** (-0.5)


def key_grads(
    query_heads,
    kv_rows,
    key_pos,
    query_pos,
    key_limit,
    causal,
    top,
    total,
    grad_heads,
    delta,
    start,
    count,
):
    step = block_size(count)
    width = H * HD

    def piece(index):
        offset = start + index * step
        block_rows = lax.dynamic_slice_in_dim(kv_rows, offset, step, 0)
        block_pos = lax.dynamic_slice_in_dim(key_pos, offset, step, 0)
        allowed = allowed_pairs(query_pos, block_pos, key_limit, causal)
        scores = jnp.where(
            allowed[None], head_scores(query_heads, block_rows[:, :width]), masked_score
        )
        probs = jnp.exp(scores - top[..., None]) / total[..., None]
        value_heads = block_rows[:, width:].reshape(step, H, HD)
        dprobs = jnp.einsum(
            "qhd,khd->hqk", grad_heads, value_heads, preferred_element_type=jnp.float32
        )
        dscores = (probs * (dprobs - delta[..., None])).astype(jnp.bfloat16)
        dkeys = jnp.einsum(
            "hqk,qhd->khd", dscores, query_heads, preferred_element_type=jnp.float32
        ).reshape(step, width) * HD ** (-0.5)
        dvalues = jnp.einsum(
            "hqk,qhd->khd",
            probs.astype(jnp.bfloat16),
            grad_heads,
            preferred_element_type=jnp.float32,
        ).reshape(step, width)
        return jnp.concatenate([dkeys, dvalues], axis=1)

    return lax.map(piece, jnp.arange(count // step, dtype=jnp.int32)).reshape(count, 2 * width)


def split_rows(grad, seq_count, ctx_count):
    return grad.reshape(
        (seq_count, ctx_count, grad.shape[0] // (seq_count * ctx_count)) + grad.shape[1:]
    )


def join_rows(grad):
    return grad.reshape((grad.shape[2],) + grad.shape[3:])


def on_device(
    tokens,
    encoder_states,
    cotangent,
    target_lengths,
    source_lengths,
    block_table,
    self_qkv,
    self_out,
    cross_q,
    cross_kv,
    cross_out,
    mlp_up,
    mlp_down,
    norm_gain,
    norm_bias,
    clip_limit,
):
    rows = tokens.shape[1]
    width = H * HD
    half = rows // 2
    source_rows = encoder_states.shape[1]
    seq_count = lax.axis_size("seq")
    ctx_count = lax.axis_size("ctx")
    all_positions = (
        block_table[:, :, None] * half + jnp.arange(half, dtype=jnp.int32)[None, None, :]
    ).reshape(-1)
    own_positions = lax.dynamic_slice_in_dim(all_positions, lax.axis_index("ctx") * rows, rows, 0)
    length = target_lengths[0]
    source_length = source_lengths[0]
    query_ok = own_positions < length
    valid_rows = query_ok[:, None]
    source_positions = jnp.arange(source_rows * ctx_count, dtype=jnp.int32)
    w_qkv, w_out, w_cq, w_ckv, w_co = (
        lax.all_gather(self_qkv, "seq", axis=0, tiled=True),
        lax.all_gather(self_out, "seq", axis=0, tiled=True),
        lax.all_gather(cross_q, "seq", axis=0, tiled=True),
        lax.all_gather(cross_kv, "seq", axis=0, tiled=True),
        lax.all_gather(cross_out, "seq", axis=0, tiled=True),
    )
    inputs = tokens[0].astype(jnp.float32)
    first_norm, first_back = jax.vjp(layer_norm, inputs, norm_gain[0], norm_bias[0])
    first_low = first_norm.astype(jnp.bfloat16)
    projected = jnp.dot(first_low, w_qkv, preferred_element_type=jnp.float32).astype(jnp.bfloat16)
    self_query = projected[:, :width].reshape(rows, H, HD)
    source_kv = jnp.dot(encoder_states[0], w_ckv, preferred_element_type=jnp.float32).astype(
        jnp.bfloat16
    )
    self_kv, cross_kvs = (
        lax.all_gather(projected[:, width:], "ctx", axis=0, tiled=True),
        lax.all_gather(source_kv, "ctx", axis=0, tiled=True),
    )
    self_top, self_total, self_peak = softmax_stats(
        self_query, self_kv, all_positions, own_positions, query_ok, length, True
    )
    self_mix = attend_values(
        self_query, self_kv, all_positions, own_positions, length, True, self_top, self_total
    )
    self_low = self_mix.astype(jnp.bfloat16)
    first_sum = inputs + jnp.dot(self_low, w_out, preferred_element_type=jnp.float32)
    second_norm, second_back = jax.vjp(layer_norm, first_sum, norm_gain[1], norm_bias[1])
    second_low = second_norm.astype(jnp.bfloat16)
    cross_rows = jnp.dot(second_low, w_cq, preferred_element_type=jnp.float32).astype(jnp.bfloat16)
    cross_query = cross_rows.reshape(rows, H, HD)
    cross_top, cross_total, cross_peak = softmax_stats(
        cross_query, cross_kvs, source_positions, own_positions, query_ok, source_length, False
    )
    cross_mix = attend_values(
        cross_query,
        cross_kvs,
        source_positions,
        own_positions,
        source_length,
        False,
        cross_top,
        cross_total,
    )
    cross_low = cross_mix.astype(jnp.bfloat16)
    second_sum = first_sum + jnp.dot(cross_low, w_co, preferred_element_type=jnp.float32)
    third_norm, third_back = jax.vjp(layer_norm, second_sum, norm_gain[2], norm_bias[2])
    third_low = third_norm.astype(jnp.bfloat16)
    w_up, w_down = (
        lax.all_gather(mlp_up, "seq", axis=0, tiled=True),
        lax.all_gather(mlp_down, "seq", axis=0, tiled=True),
    )
    hidden_pre = jnp.dot(third_low, w_up, preferred_element_type=jnp.float32)
    hidden_act, gelu_back = jax.vjp(jax.nn.gelu, hidden_pre)
    hidden_low = hidden_act.astype(jnp.bfloat16)
    third_sum = second_sum + jnp.dot(hidden_low, w_down, preferred_element_type=jnp.float32)
    output_rows = jnp.where(valid_rows, third_sum, 0.0).astype(jnp.bfloat16)
    peaks = lax.pmax(jnp.stack([self_peak, cross_peak]), ("seq", "ctx"))
    grad_rows = jnp.where(valid_rows, cotangent[0].astype(jnp.float32), 0.0)
    mlp_branch = grad_rows.astype(jnp.bfloat16)
    grad_down = jnp.einsum("rf,rd->fd", hidden_low, mlp_branch, preferred_element_type=jnp.float32)
    grad_act = jnp.einsum("rd,fd->rf", mlp_branch, w_down, preferred_element_type=jnp.float32)
    grad_pre = gelu_back(grad_act)[0].astype(jnp.bfloat16)
    grad_up = jnp.einsum("rd,rf->df", third_low, grad_pre, preferred_element_type=jnp.float32)
    back_third, gain_three, bias_three = third_back(
        jnp.einsum("rf,df->rd", grad_pre, w_up, preferred_element_type=jnp.float32)
    )
    up_part, down_part = (
        lax.psum_scatter(
            split_rows(grad_up, seq_count, ctx_count).astype(jnp.bfloat16),
            "ctx",
            scatter_dimension=1,
            tiled=True,
        ).astype(jnp.float32),
        lax.psum_scatter(
            split_rows(grad_down, seq_count, ctx_count).astype(jnp.bfloat16),
            "ctx",
            scatter_dimension=1,
            tiled=True,
        ).astype(jnp.float32),
    )
    up_shard, down_shard = (
        lax.psum_scatter(
            up_part.astype(jnp.bfloat16), "seq", scatter_dimension=0, tiled=True
        ).astype(jnp.float32),
        lax.psum_scatter(
            down_part.astype(jnp.bfloat16), "seq", scatter_dimension=0, tiled=True
        ).astype(jnp.float32),
    )
    grad_second = grad_rows + back_third
    cross_branch = grad_second.astype(jnp.bfloat16)
    grad_co = jnp.einsum("rd,re->de", cross_low, cross_branch, preferred_element_type=jnp.float32)
    cross_heads_grad = (
        jnp.einsum("re,de->rd", cross_branch, w_co, preferred_element_type=jnp.float32)
        .astype(jnp.bfloat16)
        .reshape(rows, H, HD)
    )
    cross_delta = jnp.einsum(
        "qhd,qhd->hq", cross_heads_grad.astype(jnp.float32), cross_mix.reshape(rows, H, HD)
    )
    grad_cross_rows = query_grads(
        cross_query,
        cross_kvs,
        source_positions,
        own_positions,
        source_length,
        False,
        cross_top,
        cross_total,
        cross_heads_grad,
        cross_delta,
    ).astype(jnp.bfloat16)
    grad_source_kv = lax.psum_scatter(
        key_grads(
            cross_query,
            cross_kvs,
            source_positions,
            own_positions,
            source_length,
            False,
            cross_top,
            cross_total,
            cross_heads_grad,
            cross_delta,
            jnp.int32(0),
            source_rows * lax.axis_size("ctx"),
        ).astype(jnp.bfloat16),
        "ctx",
        scatter_dimension=0,
        tiled=True,
    )
    grad_cq = jnp.einsum(
        "rd,re->de", second_low, grad_cross_rows, preferred_element_type=jnp.float32
    )
    grad_ckv = jnp.einsum(
        "sd,se->de", encoder_states[0], grad_source_kv, preferred_element_type=jnp.float32
    )
    grad_source = jnp.einsum("se,de->sd", grad_source_kv, w_ckv, preferred_element_type=jnp.float32)
    back_second, gain_two, bias_two = second_back(
        jnp.einsum("re,de->rd", grad_cross_rows, w_cq, preferred_element_type=jnp.float32)
    )
    grad_first = grad_second + back_second
    self_branch = grad_first.astype(jnp.bfloat16)
    grad_so = jnp.einsum("rd,re->de", self_low, self_branch, preferred_element_type=jnp.float32)
    self_heads_grad = (
        jnp.einsum("re,de->rd", self_branch, w_out, preferred_element_type=jnp.float32)
        .astype(jnp.bfloat16)
        .reshape(rows, H, HD)
    )
    self_delta = jnp.einsum(
        "qhd,qhd->hq", self_heads_grad.astype(jnp.float32), self_mix.reshape(rows, H, HD)
    )
    grad_query = query_grads(
        self_query,
        self_kv,
        all_positions,
        own_positions,
        length,
        True,
        self_top,
        self_total,
        self_heads_grad,
        self_delta,
    ).astype(jnp.bfloat16)
    grad_kv = lax.psum_scatter(
        key_grads(
            self_query,
            self_kv,
            all_positions,
            own_positions,
            length,
            True,
            self_top,
            self_total,
            self_heads_grad,
            self_delta,
            jnp.int32(0),
            rows * lax.axis_size("ctx"),
        ).astype(jnp.bfloat16),
        "ctx",
        scatter_dimension=0,
        tiled=True,
    )
    grad_projected = jnp.concatenate([grad_query, grad_kv], axis=1)
    grad_qkv = jnp.einsum(
        "rd,re->de", first_low, grad_projected, preferred_element_type=jnp.float32
    )
    back_first, gain_one, bias_one = first_back(
        jnp.einsum("re,de->rd", grad_projected, w_qkv, preferred_element_type=jnp.float32)
    )
    grad_inputs = grad_first + back_first
    norm_terms = jnp.stack([gain_one, gain_two, gain_three, bias_one, bias_two, bias_three], axis=1)
    qkv_part, out_part, cq_part, ckv_part, co_part, norm_part = (
        lax.psum_scatter(
            split_rows(grad_qkv, seq_count, ctx_count).astype(jnp.bfloat16),
            "ctx",
            scatter_dimension=1,
            tiled=True,
        ).astype(jnp.float32),
        lax.psum_scatter(
            split_rows(grad_so, seq_count, ctx_count).astype(jnp.bfloat16),
            "ctx",
            scatter_dimension=1,
            tiled=True,
        ).astype(jnp.float32),
        lax.psum_scatter(
            split_rows(grad_cq, seq_count, ctx_count).astype(jnp.bfloat16),
            "ctx",
            scatter_dimension=1,
            tiled=True,
        ).astype(jnp.float32),
        lax.psum_scatter(
            split_rows(grad_ckv, seq_count, ctx_count).astype(jnp.bfloat16),
            "ctx",
            scatter_dimension=1,
            tiled=True,
        ).astype(jnp.float32),
        lax.psum_scatter(
            split_rows(grad_co, seq_count, ctx_count).astype(jnp.bfloat16),
            "ctx",
            scatter_dimension=1,
            tiled=True,
        ).astype(jnp.float32),
        lax.psum_scatter(
            split_rows(norm_terms, seq_count, ctx_count).astype(jnp.bfloat16),
            "ctx",
            scatter_dimension=1,
            tiled=True,
        ).astype(jnp.float32),
    )
    qkv_shard, out_shard, cq_shard, ckv_shard, co_shard, norm_shard = (
        lax.psum_scatter(
            qkv_part.astype(jnp.bfloat16), "seq", scatter_dimension=0, tiled=True
        ).astype(jnp.float32),
        lax.psum_scatter(
            out_part.astype(jnp.bfloat16), "seq", scatter_dimension=0, tiled=True
        ).astype(jnp.float32),
        lax.psum_scatter(
            cq_part.astype(jnp.bfloat16), "seq", scatter_dimension=0, tiled=True
        ).astype(jnp.float32),
        lax.psum_scatter(
            ckv_part.astype(jnp.bfloat16), "seq", scatter_dimension=0, tiled=True
        ).astype(jnp.float32),
        lax.psum_scatter(
            co_part.astype(jnp.bfloat16), "seq", scatter_dimension=0, tiled=True
        ).astype(jnp.float32),
        lax.psum_scatter(
            norm_part.astype(jnp.bfloat16), "seq", scatter_dimension=0, tiled=True
        ).astype(jnp.float32),
    )
    norm_shard = join_rows(norm_shard)
    factors = jnp.sqrt(clip_limit / jnp.maximum(peaks, clip_limit))
    columns = jnp.repeat(factors, HD, axis=1)
    qkv_wide = self_qkv.astype(jnp.float32)
    clipped_self = jnp.concatenate(
        [qkv_wide[:, :width] * columns[0], qkv_wide[:, width : 2 * width] * columns[0]], axis=1
    ).astype(jnp.bfloat16)
    clipped_cross = jnp.concatenate(
        [
            cross_q.astype(jnp.float32) * columns[1],
            cross_kv[:, :width].astype(jnp.float32) * columns[1],
        ],
        axis=1,
    ).astype(jnp.bfloat16)
    return (
        output_rows[None],
        grad_inputs[None],
        grad_source[None],
        join_rows(qkv_shard),
        join_rows(out_shard),
        join_rows(cq_shard),
        join_rows(ckv_shard),
        join_rows(co_shard),
        join_rows(up_shard),
        join_rows(down_shard),
        norm_shard[:, :3].T,
        norm_shard[:, 3:].T,
        clipped_self,
        clipped_cross,
        peaks,
    )


def solution(mesh):
    return jax.shard_map(
        on_device,
        mesh=mesh,
        in_specs=(
            P("seq", "ctx", None),
            P("seq", "ctx", None),
            P("seq", "ctx", None),
            P("seq"),
            P("seq"),
            P(),
            P("seq", None),
            P("seq", None),
            P("seq", None),
            P("seq", None),
            P("seq", None),
            P("seq", None),
            P("seq", None),
            P(),
            P(),
            P(),
        ),
        out_specs=(
            P("seq", "ctx", None),
            P("seq", "ctx", None),
            P("seq", "ctx", None),
            P(("seq", "ctx"), None),
            P(("seq", "ctx"), None),
            P(("seq", "ctx"), None),
            P(("seq", "ctx"), None),
            P(("seq", "ctx"), None),
            P(("seq", "ctx"), None),
            P(("seq", "ctx"), None),
            P(None, ("seq", "ctx")),
            P(None, ("seq", "ctx")),
            P("seq", None),
            P("seq", None),
            P(),
        ),
        check_vma=False,
    )
```

profile of v0, /device:TPU:29, one launch (start us, length us, event | category | flops | bytes accessed | tf_op | source)
XLA Modules:
  0.0 2391.3 jit_solution(9368792390208723148)
XLA Ops:
  8.8 36.7 %all-gather.16.cloned.1.call-done = bf16[1024,2048]{1,0:T(8,128)(2,1)} async-done(((bf16[256,2048]{1,0:T(8,128)(2,1)}), bf16[1024,2048]{1,0:T(8,128)(2,1)}) %all-gather.16.cloned.1.call-update) | async-done | bytes 4194320 | tf_op jit(solution)/shard_map/all_gather | solution.py:219
  45.5 3.7 convolution_convert_fusion.5
  50.7 42.7 %all-gather.10.cloned.1.call-done = bf16[1024,3072]{1,0:T(8,128)(2,1)} async-done(((bf16[256,3072]{1,0:T(8,128)(2,1)}), bf16[1024,3072]{1,0:T(8,128)(2,1)}) %all-gather.10.cloned.1.call-update) | async-done | bytes 6291472 | tf_op jit(solution)/shard_map/all_gather | solution.py:216
  93.5 3.9 convolution_convert_fusion.4
  103.7 28.3 %all-gather.18.cloned.1.call-done = bf16[256,2048]{1,0:T(8,128)(2,1)} async-done(((bf16[32,2048]{1,0:T(8,128)(2,1)}), bf16[256,2048]{1,0:T(8,128)(2,1)}) %all-gather.18.cloned.1.call-update) | async-done | bytes 1048592 | tf_op jit(solution)/shard_map/all_gather | solution.py:232
  135.5 72.7 %all-gather.12.cloned.1.call-done = bf16[1024,2048]{1,0:T(8,128)(2,1)} async-done(((bf16[128,2048]{1,0:T(8,128)(2,1)}), bf16[1024,2048]{1,0:T(8,128)(2,1)}) %all-gather.12.cloned.1.call-update) | async-done | bytes 4194320 | tf_op jit(solution)/shard_map/all_gather | solution.py:231
  208.1 6.2 copy.84
  214.3 19.4 while.12
  217.0 3.0 fusion.230
  220.0 4.0 select_reduce_fusion.3
  226.8 3.0 fusion.230
  229.7 4.0 select_reduce_fusion.3
  234.4 9.1 while.13
  246.7 10.7 all-gather.20.cloned.1.call-done
  266.1 15.5 all-gather.22.cloned.1.call-done
  284.1 105.1 %all-gather.24.cloned.1.call-done = bf16[1024,8192]{1,0:T(8,128)(2,1)} async-done(((bf16[256,8192]{1,0:T(8,128)(2,1)}), bf16[1024,8192]{1,0:T(8,128)(2,1)}) %all-gather.24.cloned.1.call-update) | async-done | bytes 16777232 | tf_op jit(solution)/shard_map/all_gather | solution.py:264
  389.2 12.7 fusion.44
  401.9 94.8 %all-gather.26.cloned.1.call-done = bf16[8192,1024]{1,0:T(8,128)(2,1)} async-done(((bf16[2048,1024]{1,0:T(8,128)(2,1)}), bf16[8192,1024]{1,0:T(8,128)(2,1)}) %all-gather.26.cloned.1.call-update) | async-done | bytes 16777232 | tf_op jit(solution)/shard_map/all_gather | solution.py:265
  496.8 12.5 fusion.36
  509.3 13.5 multiply_reduce_fusion
  525.9 3.2 convolution_convert_fusion.11
  543.4 33.4 %while.11 = (s32[]{:T(128)}, bf16[2,512,2048]{1,2,0:T(8,128)(2,1)}, s32[2]{0:T(128)S(1)}, s32[1024]{0:T(1024)S(1)}, s32[]{:T(128)}, /*index=5*/s32[128]{0:T(128)...) while((s32[]{:T(128)}, bf16[2,512,2048]{1,2,0:T(8,128)(2,1)}, ...), condition=%wide.region_22.23_spmd, body=%wide.region_21.22_spmd.sunk | while | flops 550633984 | bytes 49446740 | solution.py:169
  554.8 3.9 fusion.226
  571.4 3.9 fusion.226
  576.7 6.3 copy.92
  583.1 21.2 while.14
  585.0 2.8 fusion.244
  588.7 5.0 fusion.245
  599.2 5.1 fusion.245
  607.2 3.3 copy.126
  610.5 3.1 convolution_convert_fusion.6
  613.6 3.1 convolution_convert_fusion.7
  618.7 10.0 convolution_convert_fusion
  628.6 8.6 convolution_convert_fusion.1
  637.4 4.3 convolution_convert_fusion.3
  641.7 55.1 %reduce-scatter.33.cloned.1.call-done = bf16[128,2048]{1,0:T(8,128)(2,1)} async-done(((bf16[1024,2048]{1,0:T(8,128)(2,1)}), bf16[128,2048]{1,0:T(8,128)(2,1)}) %reduce-scatter.33.cloned.1.call-update) | async-done | bytes 524304 | tf_op jit(solution)/shard_map/reduce_scatter | solution.py:379
  696.7 5.3 fusion.117
  703.7 4.5 convolution_convert_fusion.2
  709.4 1484.2 %all-reduce.12.cloned.1.call-done = (bf16[4,8,32,3072]{3,2,1,0:T(8,128)(2,1)}, bf16[4,8,32,1024]{3,2,1,0:T(8,128)(2,1)}, bf16[4,8,32,1024]{3,2,1,0:T(8,128)(2,1)...) async-done(((bf16[4,8,32,3072]{3,2,1,0:T(8,128)(2,1)}, ...) | async-done | bytes 50331664
  2203.5 2.8 constant_dynamic-slice_fusion.12
  2206.4 3.8 constant_dynamic-slice_fusion.7
  2212.9 39.4 %pmax.7 = f32[2,16]{1,0:T(2,128)S(1)} all-reduce(f32[2,16]{1,0:T(2,128)S(1)} %pad_maximum_fusion.6), channel_id=1, replica_groups=mesh['seq'=4,'ctx'=8] {'seq','ctx'}, use_global_device_ids=true, to_apply=%region_50.51 | all-reduce | flops 32 | bytes 256 | tf_op jit(solution)/shard_map/pmax | solution.py:272
  2257.6 10.9 fusion.57
  2270.7 3.8 constant_dynamic-slice_fusion.6
  2274.6 26.5 %all-reduce.7 = bf16[4,8,32,6]{2,0,3,1:T(4,128)(2,1)S(1)} all-reduce(bf16[4,8,32,6]{2,0,3,1:T(4,128)(2,1)S(1)} %copy.98), channel_id=18, replica_groups=mesh['seq'=4,'ctx'=8] {'ctx'}, use_global_device_ids=true, to_apply=%region_47.48.clone | all-reduce | flops 6144 | bytes 24576
  2301.8 14.0 all-reduce.8
  2324.9 23.5 reduce-scatter.45.cloned.1.call-done
  2350.5 31.9 %reduce-scatter.47.cloned.1.call-done = bf16[1,1,256,1024]{3,2,1,0:T(8,128)(2,1)} async-done(((bf16[4,1,256,1024]{3,2,1,0:T(8,128)(2,1)}), bf16[1,1,256,1024]{3,2,1,0:T(8,128)(2,1)}) %reduce-scatter.47.cloned.1.call-update) | async-done | bytes 524304 | tf_op jit(solution)/shard_map/reduce_scatter | solution.py:300
  (371 shorter events, 131.8 us)
Async XLA Ops:
  7.2 38.3 %copy-start = (bf16[1,32,1024]{2,1,0:T(8,128)(2,1)S(1)}, bf16[1,32,1024]{2,1,0:T(8,128)(2,1)}, u32[]{:S(2)}) copy-start(bf16[1,32,1024]{2,1,0:T(8,128)(2,1)} %param.25) | copy-start | bytes 196612
  7.2 42.0 %copy-start.7 = (bf16[1,128,1024]{2,1,0:T(8,128)(2,1)S(1)}, bf16[1,128,1024]{2,1,0:T(8,128)(2,1)}, u32[]{:S(2)}) copy-start(bf16[1,128,1024]{2,1,0:T(8,128)(2,1)} %param.24) | copy-start | bytes 786436
  7.2 42.9 %copy-start.51 = (f32[3,1024]{1,0:T(4,128)S(1)}, f32[3,1024]{1,0:T(4,128)}, u32[]{:S(2)}) copy-start(f32[3,1024]{1,0:T(4,128)} %param.38) | copy-start | bytes 36868
  7.2 43.5 %copy-start.52 = (f32[3,1024]{1,0:T(4,128)S(1)}, f32[3,1024]{1,0:T(4,128)}, u32[]{:S(2)}) copy-start(f32[3,1024]{1,0:T(4,128)} %param.37) | copy-start | bytes 36868
  7.2 38.3 %all-gather.16.cloned.1.call-start = ((), (), s32[]{:S(2)}) async-start(), calls=%async_computation.12 | async-start | bytes 5242880 | tf_op jit(solution)/shard_map/all_gather | solution.py:219
  8.0 85.5 %all-gather.10.cloned.1.call-start = ((), (), s32[]{:S(2)}) async-start(), calls=%async_computation.9 | async-start | bytes 7864320 | tf_op jit(solution)/shard_map/all_gather | solution.py:216
  8.7 123.3 %all-gather.18.cloned.1.call-start = ((), (), s32[]{:S(2)}) async-start(), calls=%async_computation.13 | async-start | bytes 1179648 | tf_op jit(solution)/shard_map/all_gather | solution.py:232
  49.2 159.0 %all-gather.12.cloned.1.call-start = ((), (), s32[]{:S(2)}) async-start(), calls=%async_computation.10 | async-start | bytes 4718592 | tf_op jit(solution)/shard_map/all_gather | solution.py:231
  49.4 48.0 %copy-start.49 = (f32[128]{0:T(128)}, f32[128]{0:T(128)S(1)}, u32[]{:S(2)}) copy-start(f32[128]{0:T(128)S(1)} %broadcast_multiply_fusion.3) | copy-start | bytes 1540
  50.1 47.2 %copy-start.53 = (f32[128]{0:T(128)}, f32[128]{0:T(128)S(1)}, u32[]{:S(2)}) copy-start(f32[128]{0:T(128)S(1)} %fusion.101) | copy-start | bytes 1540
  50.7 46.6 %copy-start.39 = (f32[1,1024]{1,0:T(1,128)}, f32[1,1024]{1,0:T(1,128)S(1)}, u32[]{:S(2)}) copy-start(f32[1,1024]{1,0:T(1,128)S(1)} %get-tuple-element.717) | copy-start | bytes 12292
  50.7 338.5 %copy-start.41 = (f32[1,1024]{1,0:T(1,128)}, f32[1,1024]{1,0:T(1,128)S(1)}, u32[]{:S(2)}) copy-start(f32[1,1024]{1,0:T(1,128)S(1)} %get-tuple-element.716) | copy-start | bytes 12292
  50.7 46.6 %copy-start.37 = (f32[1,1024]{1,0:T(1,128)}, f32[1,1024]{1,0:T(1,128)S(1)}, u32[]{:S(2)}) copy-start(f32[1,1024]{1,0:T(1,128)S(1)} %get-tuple-element.714) | copy-start | bytes 12292
  98.2 145.4 %all-gather.14.cloned.1.call-start = ((), (), s32[]{:S(2)}) async-start(), calls=%async_computation.11 | async-start | bytes 2621440 | tf_op jit(solution)/shard_map/all_gather | solution.py:217
  98.8 158.6 %all-gather.20.cloned.1.call-start = ((), (), s32[]{:S(2)}) async-start(), calls=%async_computation.14 | async-start | bytes 2621440 | tf_op jit(solution)/shard_map/all_gather | solution.py:218
  99.4 182.2 %all-gather.22.cloned.1.call-start = ((), (), s32[]{:S(2)}) async-start(), calls=%async_computation.15 | async-start | bytes 2621440 | tf_op jit(solution)/shard_map/all_gather | solution.py:220
  100.2 289.1 %all-gather.24.cloned.1.call-start = ((), (), s32[]{:S(2)}) async-start(), calls=%async_computation.16 | async-start | bytes 20971520 | tf_op jit(solution)/shard_map/all_gather | solution.py:264
  100.9 395.8 %all-gather.26.cloned.1.call-start = ((), (), s32[]{:S(2)}) async-start(), calls=%async_computation.17 | async-start | bytes 20971520 | tf_op jit(solution)/shard_map/all_gather | solution.py:265
  101.6 535.7 %reduce-scatter.49.cloned.1.call-start = ((), (), s32[]{:S(2)}) async-start(), calls=%async_computation.26 | async-start | bytes 1179648
  103.5 110.8 %copy-start.64 = (pred[256]{0:T(512)(128)(4,1)}, pred[256]{0:T(512)(128)(4,1)S(1)}, u32[]{:S(2)}) copy-start(pred[256]{0:T(512)(128)(4,1)S(1)} %iota_compare_fusion) | copy-start | bytes 772
  243.5 13.9 copy-start.45
  243.6 17.9 copy-start.26
  246.5 13.3 copy-start.57
  246.7 10.8 copy-start.72
  246.7 10.7 copy-start.61
  283.9 238.9 %copy-start.5 = (f32[128,1024]{1,0:T(8,128)}, f32[128,1024]{1,0:T(8,128)S(1)}, u32[]{:S(2)}) copy-start(f32[128,1024]{1,0:T(8,128)S(1)} %get-tuple-element.732) | copy-start | bytes 1572868
  389.2 107.5 %copy-start.44 = (pred[128]{0:T(512)(128)(4,1)S(1)}, pred[128]{0:T(512)(128)(4,1)}, u32[]{:S(2)}) copy-start(pred[128]{0:T(512)(128)(4,1)} %copy-done.43) | copy-start | bytes 388
  543.3 153.4 %reduce-scatter.33.cloned.1.call-start = ((), (), s32[]{:S(2)}) async-start(), calls=%async_computation.18 | async-start | bytes 4718592 | tf_op jit(solution)/shard_map/reduce_scatter | solution.py:379
  583.0 1610.6 %all-reduce.12.cloned.1.call-start = ((), (), s32[]{:S(2)}) async-start(), calls=%async_computation.27 | async-start | bytes 100663296
  583.1 23.3 copy-start.34
  637.3 59.4 %copy-start.8 = (bf16[1,128,1024]{2,1,0:T(8,128)(2,1)S(1)}, bf16[1,128,1024]{2,1,0:T(8,128)(2,1)}, u32[]{:S(2)}) copy-start(bf16[1,128,1024]{2,1,0:T(8,128)(2,1)} %param.24) | copy-start | bytes 786436
  637.3 59.4 %copy-start.35 = (bf16[128,1024]{1,0:T(8,128)(2,1)S(1)}, bf16[128,1024]{1,0:T(8,128)(2,1)}, u32[]{:S(2)}) copy-start(bf16[128,1024]{1,0:T(8,128)(2,1)} %copy.93) | copy-start | bytes 786436
  637.3 59.4 %copy-start.38 = (f32[1,1024]{1,0:T(1,128)S(1)}, f32[1,1024]{1,0:T(1,128)}, u32[]{:S(2)}) copy-start(f32[1,1024]{1,0:T(1,128)} %copy-done.37) | copy-start | bytes 12292
  637.3 59.4 %copy-start.50 = (f32[128]{0:T(128)S(1)}, f32[128]{0:T(128)}, u32[]{:S(2)}) copy-start(f32[128]{0:T(128)} %copy-done.49) | copy-start | bytes 1540
  641.7 60.4 %copy-start.70 = (f32[128]{0:T(128)S(1)}, f32[128]{0:T(128)}, u32[]{:S(2)}) copy-start(f32[128]{0:T(128)} %copy-done.69) | copy-start | bytes 1540
  641.7 60.4 %copy-start.54 = (f32[128]{0:T(128)S(1)}, f32[128]{0:T(128)}, u32[]{:S(2)}) copy-start(f32[128]{0:T(128)} %copy-done.53) | copy-start | bytes 1540
  641.7 60.8 %copy-start.40 = (f32[1,1024]{1,0:T(1,128)S(1)}, f32[1,1024]{1,0:T(1,128)}, u32[]{:S(2)}) copy-start(f32[1,1024]{1,0:T(1,128)} %copy-done.39) | copy-start | bytes 12292
  708.2 1608.8 %reduce-scatter.37.cloned.1.call-start = ((), (), s32[]{:S(2)}) async-start(), calls=%async_computation.20 | async-start | bytes 327680 | tf_op jit(solution)/shard_map/reduce_scatter | solution.py:449
  2196.0 122.6 %reduce-scatter.39.cloned.1.call-start = ((), (), s32[]{:S(2)}) async-start(), calls=%async_computation.21 | async-start | bytes 327680 | tf_op jit(solution)/shard_map/reduce_scatter | solution.py:452
  2198.4 121.7 %reduce-scatter.43.cloned.1.call-start = ((), (), s32[]{:S(2)}) async-start(), calls=%async_computation.23 | async-start | bytes 327680 | tf_op jit(solution)/shard_map/reduce_scatter | solution.py:458
  2200.8 120.8 %reduce-scatter.41.cloned.1.call-start = ((), (), s32[]{:S(2)}) async-start(), calls=%async_computation.22 | async-start | bytes 655360 | tf_op jit(solution)/shard_map/reduce_scatter | solution.py:455
  2203.4 119.8 %reduce-scatter.35.cloned.1.call-start = ((), (), s32[]{:S(2)}) async-start(), calls=%async_computation.19 | async-start | bytes 983040 | tf_op jit(solution)/shard_map/reduce_scatter | solution.py:446
  2206.3 142.1 %reduce-scatter.45.cloned.1.call-start = ((), (), s32[]{:S(2)}) async-start(), calls=%async_computation.24 | async-start | bytes 2621440 | tf_op jit(solution)/shard_map/reduce_scatter | solution.py:297
  2210.2 42.2 %copy-start.67 = (f32[2,16]{1,0:T(2,128)S(1)}, f32[2,16]{1,0:T(2,128)}, u32[]{:S(2)}) copy-start(f32[2,16]{1,0:T(2,128)} %param.39) | copy-start | bytes 388
  2210.2 42.5 %copy-start.31 = (bf16[256,1024]{1,0:T(8,128)(2,1)S(1)}, bf16[256,1024]{1,0:T(8,128)(2,1)}, u32[]{:S(2)}) copy-start(bf16[256,1024]{1,0:T(8,128)(2,1)} %param.32) | copy-start | bytes 1572868
  2210.2 172.2 %reduce-scatter.47.cloned.1.call-start = ((), (), s32[]{:S(2)}) async-start(), calls=%async_computation.25 | async-start | bytes 2621440 | tf_op jit(solution)/shard_map/reduce_scatter | solution.py:300
  2257.6 10.9 copy-start.4
  2257.6 10.9 copy-start.33
  (50 other events, 184.9 us)
Sparse Core Ops, SparseCore 0:
  9.6 35.8 all-gather.15
  47.0 46.3 all-gather.9
  96.2 35.7 all-gather.17
  134.6 73.5 all-gather.11
  209.5 23.8 all-gather.13
  234.8 22.5 all-gather.19
  259.0 22.5 all-gather.21
  283.2 105.9 all-gather.23
  390.8 105.9 all-gather.25
  543.4 59.4 reduce-scatter.48
  607.0 89.7 reduce-scatter.32
  708.3 1485.2 all-reduce.11
  2196.7 21.0 reduce-scatter.36
  2220.8 19.9 reduce-scatter.38
  2243.2 20.0 reduce-scatter.42
  2266.4 21.7 reduce-scatter.40
  2291.1 23.2 reduce-scatter.34
  2317.0 31.3 reduce-scatter.44
  2350.9 31.4 reduce-scatter.46
where the time goes:
time: 2400 us; the launch traced here: 2390 us
  waiting for transfers between devices  2010 us (84%)
  matrix products  160 us (7%)
  blocking collectives  79.9 us (3%)
  local copies, waits for them, and re-layouts  77.6 us (3%)
  other arithmetic  48.3 us (2%)
    unnamed x21, waiting for transfers between devices  1490 us
    all_gather x1, waiting for transfers between devices, on_device(): lax.all_gather(mlp_up, 'seq', axis=0, tiled=True)  105 us
    all_gather x1, waiting for transfers between devices, on_device(): lax.all_gather(mlp_down, 'seq', axis=0, tiled=True)  94.8 us
    all_gather x1, waiting for transfers between devices, on_device(): lax.all_gather(projected[:, width:], 'ctx', axis=0, tiled=True)  72.7 us
    reduce_scatter x1, waiting for transfers between devices, on_device(): lax.psum_scatter(key_grads(self_query, self_kv, all_positions, own_positi...  55.1 us
  transfers between devices with their start and end apart: 19, of which 12 were waited for; matrix products, arithmetic and copies ran while one was open for 9% of the time, Pallas kernels for 0%

commit v1 on v0

--- a/solution.py
+++ b/solution.py
@@ -1,6 +1,10 @@
+import functools
+
 import jax
 import jax.numpy as jnp
 from jax import lax
+from jax.experimental import pallas as pl
+from jax.experimental.pallas import tpu as pltpu
 from jax.sharding import PartitionSpec as P
 
 H = 16
@@ -179,7 +183,7 @@
     return grad.reshape((grad.shape[2],) + grad.shape[3:])
 
 
-def on_device(
+def general_device(
     tokens,
     encoder_states,
     cotangent,
@@ -495,9 +499,476 @@
     )
 
 
+F32 = jnp.float32
+BF16 = jnp.bfloat16
+SCALE = HD**-0.5
+
+
+def fast_fits(mesh):
+    seq_count, ctx_count = mesh.shape["seq"], mesh.shape["ctx"]
+    if H % seq_count or H % ctx_count:
+        return False
+    held, pair = H // seq_count, H // ctx_count
+    return held % pair == 0 and seq_count * (held // pair) == ctx_count and pair * HD == 128
+
+
+def dot(left, right, contract=((1,), (0,))):
+    return lax.dot_general(left, right, (contract, ((), ())), preferred_element_type=F32)
+
+
+NT = ((1,), (1,))
+TN = ((0,), (0,))
+
+
+def norm_forward(values, gain, bias):
+    centered = values - jnp.mean(values, axis=-1, keepdims=True)
+    spread = jnp.mean(centered * centered, axis=-1, keepdims=True)
+    inverse = lax.rsqrt(spread + norm_eps)
+    hat = centered * inverse
+    return hat, inverse, (hat * gain + bias).astype(BF16)
+
+
+def norm_backward(grad, hat, inverse, gain):
+    scaled = grad * gain
+    inner = jnp.mean(scaled, axis=-1, keepdims=True)
+    outer = jnp.mean(scaled * hat, axis=-1, keepdims=True)
+    return (
+        (scaled - inner - hat * outer) * inverse,
+        jnp.sum(grad * hat, axis=0),
+        jnp.sum(grad, axis=0),
+    )
+
+
+def self_forward_kernel(length_ref, row_ref, col_ref, q_ref, kv_ref, mix_ref, peak_ref):
+    length = length_ref[0]
+    row_pos = row_ref[...]
+    col_pos = col_ref[...]
+    allowed = (col_pos <= row_pos) & (col_pos < length)
+    valid = row_pos < length
+
+    @pl.when(pl.program_id(0) == 0)
+    def _():
+        peak_ref[...] = jnp.full_like(peak_ref, masked_score)
+
+    for head in range(q_ref.shape[-1] // HD):
+        cut = slice(head * HD, (head + 1) * HD)
+        scores = dot(q_ref[0, :, cut], kv_ref[0, :, cut], NT) * SCALE
+        scores = jnp.where(allowed, scores, masked_score)
+        top = jnp.max(scores, axis=-1, keepdims=True)
+        expos = jnp.exp(scores - top)
+        probs = expos * (1.0 / jnp.sum(expos, axis=-1, keepdims=True))
+        mix_ref[:, cut] = dot(probs.astype(BF16), kv_ref[1, :, cut]).astype(BF16)
+        peak = jnp.max(jnp.where(valid, top, masked_score), axis=0, keepdims=True)
+        peak_ref[head : head + 1, :] = jnp.maximum(
+            peak_ref[head : head + 1, :], jnp.broadcast_to(peak, (1, 128))
+        )
+
+
+def self_forward(qkv, positions, length):
+    count, width = qkv.shape[1:]
+    step = min(256, count)
+    return pl.pallas_call(
+        self_forward_kernel,
+        grid=(count // step,),
+        in_specs=[
+            pl.BlockSpec(memory_space=pltpu.SMEM),
+            pl.BlockSpec((step, 1), lambda i: (i, 0)),
+            pl.BlockSpec((1, count), lambda i: (0, 0)),
+            pl.BlockSpec((1, step, width), lambda i: (0, i, 0)),
+            pl.BlockSpec((2, count, width), lambda i: (0, 0, 0)),
+        ],
+        out_specs=[
+            pl.BlockSpec((step, width), lambda i: (i, 0)),
+            pl.BlockSpec((8, 128), lambda i: (0, 0)),
+        ],
+        out_shape=[
+            jax.ShapeDtypeStruct((count, width), BF16),
+            jax.ShapeDtypeStruct((8, 128), F32),
+        ],
+        compiler_params=pltpu.CompilerParams(vmem_limit_bytes=48 * 2**20),
+        name="self_forward",
+    )(length, positions[:, None], positions[None, :], qkv[0][None], qkv[1:])
+
+
+def self_backward_kernel(length_ref, row_ref, col_ref, q_ref, kv_ref, g_ref, dq_ref, dkv_ref, acc):
+    length = length_ref[0]
+    row_pos = row_ref[...]
+    col_pos = col_ref[...]
+    allowed = (col_pos <= row_pos) & (col_pos < length)
+
+    @pl.when(pl.program_id(0) == 0)
+    def _():
+        acc[...] = jnp.zeros_like(acc)
+
+    for head in range(q_ref.shape[-1] // HD):
+        cut = slice(head * HD, (head + 1) * HD)
+        query, grad = q_ref[0, :, cut], g_ref[:, cut]
+        scores = dot(query, kv_ref[0, :, cut], NT) * SCALE
+        scores = jnp.where(allowed, scores, masked_score)
+        top = jnp.max(scores, axis=-1, keepdims=True)
+        expos = jnp.exp(scores - top)
+        probs = expos * (1.0 / jnp.sum(expos, axis=-1, keepdims=True))
+        dprobs = dot(grad, kv_ref[1, :, cut], NT)
+        delta = jnp.sum(probs * dprobs, axis=-1, keepdims=True)
+        dscores = (probs * (dprobs - delta)).astype(BF16)
+        dq_ref[:, cut] = (dot(dscores, kv_ref[0, :, cut]) * SCALE).astype(BF16)
+        acc[0, :, cut] += dot(dscores, query, TN)
+        acc[1, :, cut] += dot(probs.astype(BF16), grad, TN)
+
+    @pl.when(pl.program_id(0) == pl.num_programs(0) - 1)
+    def _():
+        dkv_ref[0] = (acc[0] * SCALE).astype(BF16)
+        dkv_ref[1] = acc[1].astype(BF16)
+
+
+def self_backward(qkv, positions, length, grad):
+    count, width = qkv.shape[1:]
+    step = min(256, count)
+    dq, dkv = pl.pallas_call(
+        self_backward_kernel,
+        grid=(count // step,),
+        in_specs=[
+            pl.BlockSpec(memory_space=pltpu.SMEM),
+            pl.BlockSpec((step, 1), lambda i: (i, 0)),
+            pl.BlockSpec((1, count), lambda i: (0, 0)),
+            pl.BlockSpec((1, step, width), lambda i: (0, i, 0)),
+            pl.BlockSpec((2, count, width), lambda i: (0, 0, 0)),
+            pl.BlockSpec((step, width), lambda i: (i, 0)),
+        ],
+        out_specs=[
+            pl.BlockSpec((step, width), lambda i: (i, 0)),
+            pl.BlockSpec((2, count, width), lambda i: (0, 0, 0)),
+        ],
+        out_shape=[
+            jax.ShapeDtypeStruct((count, width), BF16),
+            jax.ShapeDtypeStruct((2, count, width), BF16),
+        ],
+        scratch_shapes=[pltpu.VMEM((2, count, width), F32)],
+        compiler_params=pltpu.CompilerParams(vmem_limit_bytes=48 * 2**20),
+        name="self_backward",
+    )(length, positions[:, None], positions[None, :], qkv[0][None], qkv[1:], grad)
+    return jnp.concatenate([dq[None], dkv], axis=0)
+
+
+def cross_forward_kernel(limit_ref, target_ref, row_ref, q_ref, kv_ref, mix_ref, peak_ref):
+    slot = pl.program_id(0)
+    width = q_ref.shape[-1]
+    keys = kv_ref.shape[1]
+    live = lax.broadcasted_iota(jnp.int32, (1, keys), 1) < limit_ref[slot]
+    valid = row_ref[...] < target_ref[slot]
+
+    @pl.when(slot == 0)
+    def _():
+        peak_ref[...] = jnp.full_like(peak_ref, masked_score)
+
+    for head in range(width // HD):
+        cut = slice(head * HD, (head + 1) * HD)
+        vcut = slice(width + head * HD, width + (head + 1) * HD)
+        scores = dot(q_ref[0, :, cut], kv_ref[0, :, cut], NT) * SCALE
+        scores = jnp.where(live, scores, masked_score)
+        top = jnp.max(scores, axis=-1, keepdims=True)
+        expos = jnp.exp(scores - top)
+        probs = expos * (1.0 / jnp.sum(expos, axis=-1, keepdims=True))
+        mix_ref[0, :, cut] = dot(probs.astype(BF16), kv_ref[0, :, vcut]).astype(BF16)
+        peak = jnp.max(jnp.where(valid, top, masked_score), axis=0, keepdims=True)
+        peak_ref[head : head + 1, :] = jnp.maximum(
+            peak_ref[head : head + 1, :], jnp.broadcast_to(peak, (1, 128))
+        )
+
+
+def cross_forward(query, kv, own_positions, target_lengths, source_lengths):
+    slots, rows, width = query.shape
+    keys = kv.shape[1]
+    return pl.pallas_call(
+        cross_forward_kernel,
+        grid=(slots,),
+        in_specs=[
+            pl.BlockSpec(memory_space=pltpu.SMEM),
+            pl.BlockSpec(memory_space=pltpu.SMEM),
+            pl.BlockSpec((rows, 1), lambda i: (0, 0)),
+            pl.BlockSpec((1, rows, width), lambda i: (i, 0, 0)),
+            pl.BlockSpec((1, keys, 2 * width), lambda i: (i, 0, 0)),
+        ],
+        out_specs=[
+            pl.BlockSpec((1, rows, width), lambda i: (i, 0, 0)),
+            pl.BlockSpec((8, 128), lambda i: (0, 0)),
+        ],
+        out_shape=[
+            jax.ShapeDtypeStruct((slots, rows, width), BF16),
+            jax.ShapeDtypeStruct((8, 128), F32),
+        ],
+        compiler_params=pltpu.CompilerParams(vmem_limit_bytes=48 * 2**20),
+        name="cross_forward",
+    )(source_lengths, target_lengths, own_positions[:, None], query, kv)
+
+
+def cross_backward_kernel(limit_ref, q_ref, kv_ref, g_ref, dq_ref, dkv_ref):
+    slot = pl.program_id(0)
+    width = q_ref.shape[-1]
+    keys = kv_ref.shape[1]
+    live = lax.broadcasted_iota(jnp.int32, (1, keys), 1) < limit_ref[slot]
+    for head in range(width // HD):
+        cut = slice(head * HD, (head + 1) * HD)
+        vcut = slice(width + head * HD, width + (head + 1) * HD)
+        query, grad = q_ref[0, :, cut], g_ref[0, :, cut]
+        scores = dot(query, kv_ref[0, :, cut], NT) * SCALE
+        scores = jnp.where(live, scores, masked_score)
+        top = jnp.max(scores, axis=-1, keepdims=True)
+        expos = jnp.exp(scores - top)
+        probs = expos * (1.0 / jnp.sum(expos, axis=-1, keepdims=True))
+        dprobs = dot(grad, kv_ref[0, :, vcut], NT)
+        delta = jnp.sum(probs * dprobs, axis=-1, keepdims=True)
+        dscores = (probs * (dprobs - delta)).astype(BF16)
+        dq_ref[0, :, cut] = (dot(dscores, kv_ref[0, :, cut]) * SCALE).astype(BF16)
+        dkv_ref[0, :, cut] = (dot(dscores, query, TN) * SCALE).astype(BF16)
+        dkv_ref[0, :, vcut] = dot(probs.astype(BF16), grad, TN).astype(BF16)
+
+
+def cross_backward(query, kv, source_lengths, grad):
+    slots, rows, width = query.shape
+    keys = kv.shape[1]
+    return pl.pallas_call(
+        cross_backward_kernel,
+        grid=(slots,),
+        in_specs=[
+            pl.BlockSpec(memory_space=pltpu.SMEM),
+            pl.BlockSpec((1, rows, width), lambda i: (i, 0, 0)),
+            pl.BlockSpec((1, keys, 2 * width), lambda i: (i, 0, 0)),
+            pl.BlockSpec((1, rows, width), lambda i: (i, 0, 0)),
+        ],
+        out_specs=[
+            pl.BlockSpec((1, rows, width), lambda i: (i, 0, 0)),
+            pl.BlockSpec((1, keys, 2 * width), lambda i: (i, 0, 0)),
+        ],
+        out_shape=[
+            jax.ShapeDtypeStruct((slots, rows, width), BF16),
+            jax.ShapeDtypeStruct((slots, keys, 2 * width), BF16),
+        ],
+        compiler_params=pltpu.CompilerParams(vmem_limit_bytes=48 * 2**20),
+        name="cross_backward",
+    )(source_lengths, query, kv, grad)
+
+
+def gather_seq(rows):
+    return lax.all_gather(rows, "seq", axis=0, tiled=True)
+
+
+def scatter_seq(partial):
+    return lax.psum_scatter(
+        partial.astype(BF16), "seq", scatter_dimension=0, tiled=True
+    ).astype(F32)
+
+
+def swap(blocks, axis):
+    return lax.all_to_all(blocks, axis, split_axis=0, concat_axis=0, tiled=True)
+
+
+def columns_of(weight, parts):
+    seq_count = lax.axis_size("seq")
+    rows, columns = weight.shape
+    width = columns // (parts * seq_count)
+    blocks = weight.reshape(rows, parts, seq_count, width).transpose(2, 0, 1, 3)
+    return swap(blocks.reshape(seq_count, rows, parts * width), "seq").reshape(
+        seq_count * rows, parts * width
+    )
+
+
+def finish_rows(grad):
+    return lax.psum_scatter(grad.astype(BF16), "ctx", scatter_dimension=0, tiled=True).astype(F32)
+
+
+def finish_columns(grad, parts):
+    seq_count, ctx_count = lax.axis_size("seq"), lax.axis_size("ctx")
+    rows, columns = grad.shape
+    share = rows // (seq_count * ctx_count)
+    blocks = grad.astype(BF16).reshape(seq_count, ctx_count, share, columns).transpose(1, 0, 2, 3)
+    own = lax.psum_scatter(
+        blocks.reshape(ctx_count * seq_count * share, columns),
+        "ctx",
+        scatter_dimension=0,
+        tiled=True,
+    ).reshape(seq_count, share, columns)
+    taken = swap(own, "seq").reshape(seq_count, share, parts, columns // parts)
+    return taken.transpose(1, 2, 0, 3).reshape(share, seq_count * columns).astype(F32)
+
+
+def fast_device(
+    tokens,
+    encoder_states,
+    cotangent,
+    target_lengths,
+    source_lengths,
+    block_table,
+    self_qkv,
+    self_out,
+    cross_q,
+    cross_kv,
+    cross_out,
+    mlp_up,
+    mlp_down,
+    norm_gain,
+    norm_bias,
+    clip_limit,
+):
+    rows = tokens.shape[1]
+    source_rows = encoder_states.shape[1]
+    seq_count, ctx_count = lax.axis_size("seq"), lax.axis_size("ctx")
+    seq_index, ctx_index = lax.axis_index("seq"), lax.axis_index("ctx")
+    held, pair = H // seq_count, H // ctx_count
+    groups = held // pair
+    own_width, pair_width = held * HD, pair * HD
+    width = H * HD
+    half = rows // 2
+    all_positions = (
+        block_table[:, :, None] * half + jnp.arange(half, dtype=jnp.int32)[None, None, :]
+    ).reshape(-1)
+    own_positions = lax.dynamic_slice_in_dim(all_positions, ctx_index * rows, rows, 0)
+    valid_rows = (own_positions < target_lengths[0])[:, None]
+    targets, sources = gather_seq(target_lengths), gather_seq(source_lengths)
+    my_slot = ctx_index // groups
+    my_length = lax.dynamic_slice_in_dim(targets, my_slot, 1, 0)
+
+    w_qkv, w_cq, w_ckv = columns_of(self_qkv, 3), columns_of(cross_q, 1), columns_of(cross_kv, 2)
+    w_up = columns_of(mlp_up, 1)
+
+    inputs = tokens[0].astype(F32)
+    hat_one, inverse_one, first_own = norm_forward(inputs, norm_gain[0], norm_bias[0])
+    first_low = gather_seq(first_own)
+    source_low = gather_seq(encoder_states[0])
+    grad_rows = jnp.where(valid_rows, cotangent[0].astype(F32), 0.0)
+    mlp_branch = gather_seq(grad_rows.astype(BF16))
+
+    def to_heads(blocks, parts):
+        blocks = blocks.reshape(seq_count, rows, parts, groups, pair_width)
+        blocks = blocks.transpose(0, 3, 2, 1, 4).reshape(ctx_count, parts * rows, pair_width)
+        taken = swap(blocks, "ctx").reshape(ctx_count, parts, rows, pair_width)
+        return taken.transpose(1, 0, 2, 3).reshape(parts, ctx_count * rows, pair_width)
+
+    def to_rows(heads):
+        parts = heads.shape[0]
+        blocks = heads.reshape(parts, ctx_count, rows, pair_width).transpose(1, 0, 2, 3)
+        taken = swap(blocks.reshape(ctx_count, parts * rows, pair_width), "ctx")
+        taken = taken.reshape(seq_count, groups, parts, rows, pair_width).transpose(0, 3, 2, 1, 4)
+        return taken.reshape(seq_count * rows, parts * own_width)
+
+    projected = dot(first_low, w_qkv).astype(BF16)
+    qkv = to_heads(projected, 3)
+    self_mix, self_peak = self_forward(qkv, all_positions, my_length)
+    self_low = to_rows(self_mix[None])
+
+    source_kv = dot(source_low, w_ckv).astype(BF16)
+    cross_kvs = lax.all_gather(source_kv, "ctx", axis=0, tiled=True)
+    cross_kvs = (
+        cross_kvs.reshape(ctx_count, seq_count, source_rows, 2 * own_width)
+        .transpose(1, 0, 2, 3)
+        .reshape(seq_count, ctx_count * source_rows, 2 * own_width)
+    )
+
+    first_sum = inputs + scatter_seq(dot(self_low, self_out))
+    hat_two, inverse_two, second_own = norm_forward(first_sum, norm_gain[1], norm_bias[1])
+    second_low = gather_seq(second_own)
+    cross_query = dot(second_low, w_cq).astype(BF16).reshape(seq_count, rows, own_width)
+    cross_mix, cross_peak = cross_forward(cross_query, cross_kvs, own_positions, targets, sources)
+    cross_low = cross_mix.reshape(seq_count * rows, own_width)
+    second_sum = first_sum + scatter_seq(dot(cross_low, cross_out))
+    hat_three, inverse_three, third_own = norm_forward(second_sum, norm_gain[2], norm_bias[2])
+    third_low = gather_seq(third_own)
+
+    hidden_pre = dot(third_low, w_up)
+    hidden_act, gelu_back = jax.vjp(jax.nn.gelu, hidden_pre)
+    hidden_low = hidden_act.astype(BF16)
+    third_sum = second_sum + scatter_seq(dot(hidden_low, mlp_down))
+    output_rows = jnp.where(valid_rows, third_sum, 0.0).astype(BF16)
+
+    peak_self = lax.dynamic_update_slice_in_dim(
+        jnp.full((H,), masked_score, F32),
+        self_peak[:pair, 0],
+        seq_index * held + (ctx_index % groups) * pair,
+        0,
+    )
+    peak_cross = lax.dynamic_update_slice_in_dim(
+        jnp.full((H,), masked_score, F32), cross_peak[:held, 0], seq_index * held, 0
+    )
+    peaks = lax.pmax(jnp.stack([peak_self, peak_cross]), ("seq", "ctx"))
+
+    grad_down = dot(hidden_low, mlp_branch, TN)
+    grad_pre = gelu_back(dot(mlp_branch, mlp_down, NT))[0].astype(BF16)
+    grad_up = dot(third_low, grad_pre, TN)
+    back_three, gain_three, bias_three = norm_backward(
+        scatter_seq(dot(grad_pre, w_up, NT)), hat_three, inverse_three, norm_gain[2]
+    )
+    up_shard, down_shard = finish_columns(grad_up, 1), finish_rows(grad_down)
+
+    grad_second = grad_rows + back_three
+    cross_branch = gather_seq(grad_second.astype(BF16))
+    grad_co = dot(cross_low, cross_branch, TN)
+    cross_grad = dot(cross_branch, cross_out, NT).astype(BF16)
+    dquery, dkv = cross_backward(
+        cross_query, cross_kvs, sources, cross_grad.reshape(seq_count, rows, own_width)
+    )
+    dquery = dquery.reshape(seq_count * rows, own_width)
+    dkv = (
+        dkv.reshape(seq_count, ctx_count, source_rows, 2 * own_width)
+        .transpose(1, 0, 2, 3)
+        .reshape(ctx_count * seq_count * source_rows, 2 * own_width)
+    )
+    grad_source_kv = lax.psum_scatter(dkv, "ctx", scatter_dimension=0, tiled=True)
+    grad_cq = dot(second_low, dquery, TN)
+    grad_ckv = dot(source_low, grad_source_kv, TN)
+    grad_source = scatter_seq(dot(grad_source_kv, w_ckv, NT))
+    back_two, gain_two, bias_two = norm_backward(
+        scatter_seq(dot(dquery, w_cq, NT)), hat_two, inverse_two, norm_gain[1]
+    )
+    grad_first = grad_second + back_two
+    self_branch = gather_seq(grad_first.astype(BF16))
+    grad_so = dot(self_low, self_branch, TN)
+    self_grad = to_heads(dot(self_branch, self_out, NT).astype(BF16), 1)[0]
+    grad_projected = to_rows(self_backward(qkv, all_positions, my_length, self_grad))
+    grad_qkv = dot(first_low, grad_projected, TN)
+    back_one, gain_one, bias_one = norm_backward(
+        scatter_seq(dot(grad_projected, w_qkv, NT)), hat_one, inverse_one, norm_gain[0]
+    )
+    grad_inputs = grad_first + back_one
+
+    norm_terms = jnp.stack([gain_one, gain_two, gain_three, bias_one, bias_two, bias_three])
+    norm_sum = lax.psum(norm_terms, ("seq", "ctx"))
+    norm_share = width // (seq_count * ctx_count)
+    norm_shard = lax.dynamic_slice_in_dim(
+        norm_sum, (seq_index * ctx_count + ctx_index) * norm_share, norm_share, 1
+    )
+
+    factors = jnp.sqrt(clip_limit / jnp.maximum(peaks, clip_limit))
+    columns = jnp.repeat(factors, HD, axis=1)
+    qkv_wide = self_qkv.astype(F32)
+    clipped_self = jnp.concatenate(
+        [qkv_wide[:, :width] * columns[0], qkv_wide[:, width : 2 * width] * columns[0]], axis=1
+    ).astype(BF16)
+    clipped_cross = jnp.concatenate(
+        [cross_q.astype(F32) * columns[1], cross_kv[:, :width].astype(F32) * columns[1]], axis=1
+    ).astype(BF16)
+    return (
+        output_rows[None],
+        grad_inputs[None],
+        grad_source[None],
+        finish_columns(grad_qkv, 3),
+        finish_rows(grad_so),
+        finish_columns(grad_cq, 1),
+        finish_columns(grad_ckv, 2),
+        finish_rows(grad_co),
+        up_shard,
+        down_shard,
+        norm_shard[:3],
+        norm_shard[3:],
+        clipped_self,
+        clipped_cross,
+        peaks,
+    )
+
+
 def solution(mesh):
+    body = fast_device if fast_fits(mesh) else general_device
     return jax.shard_map(
-        on_device,
+        body,
         mesh=mesh,
         in_specs=(
             P("seq", "ctx", None),

time: 2400 us -> 1070 us (0.45)
  waiting for transfers between devices: 2010 us -> 636 us
  matrix products: 160 us -> 67.3 us
  blocking collectives: 79.9 us -> 153 us
  starting transfers between devices: 0.93 us -> 46.4 us
  Pallas kernels: 0 us -> 33.9 us
    unnamed x21 -> x22, waiting for transfers between devices: 1490 us -> 0.36 us
    reduce_scatter x8 -> x15, waiting for transfers between devices: 110 us -> 506 us  [the longest x3 205 us: finish_rows(): lax.psum_scatter(grad.astype(BF16), 'ctx', scatter_dimension=0, tiled=True)]
    all_gather x9 -> x7, waiting for transfers between devices: 407 us -> 61.9 us  [the longest x6 46.2 us: gather_seq(): return lax.all_gather(rows, 'seq', axis=0, tiled=True)]
    dot_general x41 -> x21, matrix products: 160 us -> 67.3 us  [dot(): lax.dot_general(left, right, (contract, ((), ())), preferred_element_type...]
    all_to_all x0 -> x9, waiting for transfers between devices: none -> 67 us  [swap(): return lax.all_to_all(blocks, axis, split_axis=0, concat_axis=0, tiled=True)]
    all_to_all x0 -> x3, blocking collectives: none -> 50 us  [swap(): return lax.all_to_all(blocks, axis, split_axis=0, concat_axis=0, tiled=True)]
    all_to_all x0 -> x9, starting transfers between devices: none -> 45 us  [swap(): return lax.all_to_all(blocks, axis, split_axis=0, concat_axis=0, tiled=True)]
    psum x0 -> x1, blocking collectives: none -> 38.6 us  [fast_device(): norm_sum = lax.psum(norm_terms, ('seq', 'ctx'))]
  transfers between devices with their start and end apart: 19 -> 31, of which waited for: 12 -> 22; matrix products, arithmetic and copies ran while one was open for 9% -> 12% of each run, Pallas kernels for 0% -> 1%
where the time goes in v1:
time: 1070 us; the launch traced here: 1050 us
  waiting for transfers between devices  636 us (59%)
  blocking collectives  153 us (14%)
  matrix products  67.3 us (6%)
  local copies, waits for them, and re-layouts  59.9 us (6%)
  starting transfers between devices  46.4 us (4%)
  other arithmetic  36.5 us (3%)
  Pallas kernels  33.9 us (3%)
  between operations  17.8 us (2%)
    reduce_scatter x3, waiting for transfers between devices, finish_rows(): lax.psum_scatter(grad.astype(BF16), 'ctx', scatter_dimension=0, tiled=True)  205 us
    reduce_scatter x7, waiting for transfers between devices, scatter_seq(): lax.psum_scatter(partial.astype(BF16), 'seq', scatter_dimension=0, tiled=...  129 us
    reduce_scatter x4, waiting for transfers between devices, finish_columns(): lax.psum_scatter(blocks.reshape(ctx_count * seq_count * share, columns),...  115 us
    dot_general x21, matrix products, dot(): lax.dot_general(left, right, (contract, ((), ())), preferred_element_type...  67.3 us
    all_to_all x9, waiting for transfers between devices, swap(): return lax.all_to_all(blocks, axis, split_axis=0, concat_axis=0, tiled=True)  67 us
    reduce_scatter x1, waiting for transfers between devices, fast_device(): lax.psum_scatter(dkv, 'ctx', scatter_dimension=0, tiled=True)  58.1 us
    all_to_all x3, blocking collectives, swap(): return lax.all_to_all(blocks, axis, split_axis=0, concat_axis=0, tiled=True)  50 us
    all_gather x6, waiting for transfers between devices, gather_seq(): return lax.all_gather(rows, 'seq', axis=0, tiled=True)  46.2 us
  transfers between devices with their start and end apart: 31, of which 22 were waited for; matrix products, arithmetic and copies ran while one was open for 12% of the time, Pallas kernels for 1%

profile of v1, /device:TPU:29, one launch (start us, length us, event | category | flops | bytes accessed | tf_op | source)
XLA Modules:
  0.0 1050.4 jit_solution(6771244353499337787)
XLA Ops:
  15.8 27.9 %all_to_all.60 = bf16[4,256,768]{1,2,0:T(8,128)(2,1)S(1)} all-to-all(bf16[4,256,768]{1,2,0:T(8,128)(2,1)S(1)} %bitcast.263), channel_id=1, replica_groups=mesh['seq'=4,'ctx'=8] {'seq'}, dimensions={0} | all-to-all | bytes 3145728 | tf_op jit(solution)/shard_map/all_to_all | solution.py:763
  49.2 5.4 all-to-all-start.1
  58.1 4.3 all-reduce.2
  63.7 9.4 all-to-all-done.1
  73.3 7.7 self_forward.1
  81.0 12.0 %all_to_all.61 = bf16[8,128,128]{2,1,0:T(8,128)(2,1)S(1)} all-to-all(bf16[8,128,128]{2,1,0:T(8,128)(2,1)S(1)} %bitcast.255), channel_id=1, replica_groups=mesh['seq'=4,'ctx'=8] {'ctx'}, dimensions={0} | all-to-all | bytes 524288 | tf_op jit(solution)/shard_map/all_to_all | solution.py:763
  97.3 5.2 all-to-all-start.4
  102.5 20.6 %all-gather = bf16[1,128,1024]{2,1,0:T(8,128)(2,1)S(1)} all-gather(bf16[1,32,1024]{2,1,0:T(8,128)(2,1)} %param.17), channel_id=2, replica_groups=mesh['seq'=4,'ctx'=8] {'seq'}, dimensions={1}, use_global_device_ids=true | all-gather | bytes 327680 | tf_op jit(solution)/shard_map/all_gather | solution.py:753
  132.0 4.3 all-to-all-start.3
  136.5 7.8 all-to-all-done.3
  146.4 15.7 %all-gather.13.cloned.1.call-done = bf16[1024,512]{1,0:T(8,128)(2,1)} async-done(((bf16[128,512]{1,0:T(8,128)(2,1)}), bf16[1024,512]{1,0:T(8,128)(2,1)}) %all-gather.13.cloned.1.call-update) | async-done | bytes 1048592 | tf_op jit(solution)/shard_map/all_gather | solution.py:860
  163.4 20.5 %all-gather.11.cloned.1.call-done = bf16[512,1024]{1,0:T(8,128)(2,1)} async-done(((bf16[128,1024]{1,0:T(8,128)(2,1)}), bf16[512,1024]{1,0:T(8,128)(2,1)}) %all-gather.11.cloned.1.call-update) | async-done | bytes 1048592 | tf_op jit(solution)/shard_map/all_gather | solution.py:753
  185.7 4.7 cross_forward.1
  191.9 6.4 copy.67
  198.3 5.1 all-to-all-start.5
  205.4 17.0 %reduce-scatter.18.cloned.1.call-done = bf16[128,1024]{1,0:T(8,128)(2,1)} async-done(((bf16[512,1024]{1,0:T(8,128)(2,1)}), bf16[128,1024]{1,0:T(8,128)(2,1)}) %reduce-scatter.18.cloned.1.call-update) | async-done | bytes 262160 | tf_op jit(solution)/shard_map/reduce_scatter | solution.py:757
  225.9 8.5 all-gather.17.cloned.1.call-done
  234.4 6.9 fusion.62
  241.2 26.5 %all-to-all-done.5 = bf16[4,256,2048]{1,2,0:T(8,128)(2,1)} async-done(((bf16[4,256,2048]{1,2,0:T(8,128)(2,1)}), bf16[4,256,2048]{1,2,0:T(8,128)(2,1)}, u32[]{:S(2)}, u32[]{:S(2)}) %all-to-all-start.5) | async-done | bytes 4194336 | tf_op jit(solution)/shard_map/all_to_all | solution.py:763
  267.7 6.3 copy.68
  274.0 10.5 %fusion.6 = (bf16[512,2048]{1,0:T(8,128)(2,1)S(1)}, f32[512,2048]{1,0:T(8,128)}) fusion(f32[512,2048]{1,0:T(8,128)} %fusion.62, bf16[512,1024]{1,0:T(8,128)(2,1)} %all-gather.15.cloned.1.call-done, bf16[1024,2048]{1,0:T(8,128)(2,1)} %bitcast.265), kind=kOutput, calls=%fused_computation.8 | convolution fusion | flops 2168455168 | bytes 15728640 | tf_op jit(solution)/shard_map/dot_general | solution.py:516
  289.3 7.1 convolution_convert_fusion.9
  296.5 17.8 %reduce-scatter.22.cloned.1.call-done = bf16[128,1024]{1,0:T(8,128)(2,1)} async-done(((bf16[512,1024]{1,0:T(8,128)(2,1)}), bf16[128,1024]{1,0:T(8,128)(2,1)}) %reduce-scatter.22.cloned.1.call-update) | async-done | bytes 262160 | tf_op jit(solution)/shard_map/reduce_scatter | solution.py:757
  315.7 26.7 %reduce-scatter.20.cloned.1.call-done = bf16[128,1024]{1,0:T(8,128)(2,1)} async-done(((bf16[512,1024]{1,0:T(8,128)(2,1)}), bf16[128,1024]{1,0:T(8,128)(2,1)}) %reduce-scatter.20.cloned.1.call-update) | async-done | bytes 262160 | tf_op jit(solution)/shard_map/reduce_scatter | solution.py:757
  345.2 17.2 %all-gather.19.cloned.1.call-done = bf16[512,1024]{1,0:T(8,128)(2,1)} async-done(((bf16[128,1024]{1,0:T(8,128)(2,1)}), bf16[512,1024]{1,0:T(8,128)(2,1)}) %all-gather.19.cloned.1.call-update) | async-done | bytes 1048592 | tf_op jit(solution)/shard_map/all_gather | solution.py:753
  364.1 9.3 cross_backward.1
  379.4 22.2 %reduce-scatter.24.cloned.1.call-done = bf16[128,1024]{1,0:T(8,128)(2,1)} async-done(((bf16[512,1024]{1,0:T(8,128)(2,1)}), bf16[128,1024]{1,0:T(8,128)(2,1)}) %reduce-scatter.24.cloned.1.call-update) | async-done | bytes 262160 | tf_op jit(solution)/shard_map/reduce_scatter | solution.py:757
  407.9 58.1 %reduce-scatter.28.cloned.1.call-done = bf16[128,512]{1,0:T(8,128)(2,1)} async-done(((bf16[1024,512]{1,0:T(8,128)(2,1)}), bf16[128,512]{1,0:T(8,128)(2,1)}) %reduce-scatter.28.cloned.1.call-update) | async-done | bytes 131088 | tf_op jit(solution)/shard_map/reduce_scatter | solution.py:915
  473.7 4.0 convolution_convert_fusion.1
  482.4 7.4 convolution_convert_fusion
  492.8 10.1 all_to_all.62
  502.9 12.1 %self_backward.1 = (bf16[1024,128]{1,0:T(8,128)(2,1)S(1)}, bf16[2,1024,128]{2,1,0:T(8,128)(2,1)S(1)}) custom-call(s32[1]{0:T(128)} %dynamic_slice.10.length_ref, s32[1024,1]{1,0:T(8,128)S(1)} %add.212.row_ref, s32[1,1024]{1,0:T(1,128)S(1)} %add.181.col_ref, bf16[1,1024,128]{2,1,0:T(8,128)(2,1)S(1)} %bitcast.245, bf16[2,1024,128]{2,1,0:T(8,128)(2,1)S(1)} %bitcast.243, ...), custom_call_target="tpu_custom_call" | custom-call | tf_op jit(solution)/shard_map/self_backward/pallas_call | solution.py:627
  516.0 6.1 all-to-all-start.7
  523.5 17.9 %all-to-all-done.7 = bf16[8,384,128]{2,1,0:T(8,128)(2,1)S(1)} async-done(((bf16[8,384,128]{2,1,0:T(8,128)(2,1)}), bf16[8,384,128]{2,1,0:T(8,128)(2,1)S(1)}, u32[]{:S(2)}, u32[]{:S(2)}) %all-to-all-start.7) | async-done | bytes 786464 | tf_op jit(solution)/shard_map/all_to_all | solution.py:763
  551.8 39.4 %pmax.7 = f32[2,16]{1,0:T(2,128)S(1)} all-reduce(f32[2,16]{1,0:T(2,128)S(1)} %pad_maximum_fusion.3), channel_id=1, replica_groups=mesh['seq'=4,'ctx'=8] {'seq','ctx'}, use_global_device_ids=true, to_apply=%region_34.35 | all-reduce | flops 32 | bytes 256 | tf_op jit(solution)/shard_map/pmax | solution.py:892
  595.7 5.1 all-to-all-start.9
  604.1 4.2 all-to-all-start.10
  609.8 55.4 %reduce-scatter.40.cloned.1.call-done = bf16[32,1024]{1,0:T(8,128)(2,1)} async-done(((bf16[256,1024]{1,0:T(8,128)(2,1)}), bf16[32,1024]{1,0:T(8,128)(2,1)}) %reduce-scatter.40.cloned.1.call-update) | async-done | bytes 65552 | tf_op jit(solution)/shard_map/reduce_scatter | solution.py:777
  666.7 92.1 %reduce-scatter.42.cloned.1.call-done = bf16[128,2048]{1,0:T(8,128)(2,1)} async-done(((bf16[1024,2048]{1,0:T(8,128)(2,1)}), bf16[128,2048]{1,0:T(8,128)(2,1)}) %reduce-scatter.42.cloned.1.call-update) | async-done | bytes 524304 | tf_op jit(solution)/shard_map/reduce_scatter | solution.py:785
  758.8 4.1 all-to-all-start.11
  763.7 18.7 %reduce-scatter.30.cloned.1.call-done = bf16[32,1024]{1,0:T(8,128)(2,1)} async-done(((bf16[128,1024]{1,0:T(8,128)(2,1)}), bf16[32,1024]{1,0:T(8,128)(2,1)}) %reduce-scatter.30.cloned.1.call-update) | async-done | bytes 65552 | tf_op jit(solution)/shard_map/reduce_scatter | solution.py:757
  785.1 88.4 %reduce-scatter.44.cloned.1.call-done = bf16[256,1024]{1,0:T(8,128)(2,1)} async-done(((bf16[2048,1024]{1,0:T(8,128)(2,1)}), bf16[256,1024]{1,0:T(8,128)(2,1)}) %reduce-scatter.44.cloned.1.call-update) | async-done | bytes 524304 | tf_op jit(solution)/shard_map/reduce_scatter | solution.py:777
  875.6 60.8 %reduce-scatter.34.cloned.1.call-done = bf16[32,1024]{1,0:T(8,128)(2,1)} async-done(((bf16[256,1024]{1,0:T(8,128)(2,1)}), bf16[32,1024]{1,0:T(8,128)(2,1)}) %reduce-scatter.34.cloned.1.call-update) | async-done | bytes 65552 | tf_op jit(solution)/shard_map/reduce_scatter | solution.py:777
  940.3 26.1 %reduce-scatter.26.cloned.1.call-done = bf16[128,1024]{1,0:T(8,128)(2,1)} async-done(((bf16[512,1024]{1,0:T(8,128)(2,1)}), bf16[128,1024]{1,0:T(8,128)(2,1)}) %reduce-scatter.26.cloned.1.call-update) | async-done | bytes 262160 | tf_op jit(solution)/shard_map/reduce_scatter | solution.py:757
  967.7 38.6 %psum.7 = f32[6,1024]{1,0:T(8,128)S(1)} all-reduce(f32[6,1024]{1,0:T(8,128)S(1)} %stack.38), channel_id=1, replica_groups=mesh['seq'=4,'ctx'=8] {'seq','ctx'}, use_global_device_ids=true, to_apply=%region_33.34 | all-reduce | flops 6144 | bytes 49152 | tf_op jit(solution)/shard_map/psum | solution.py:934
  1008.5 23.0 %reduce-scatter.32.cloned.1.call-done = bf16[128,768]{1,0:T(8,128)(2,1)} async-done(((bf16[1024,768]{1,0:T(8,128)(2,1)}), bf16[128,768]{1,0:T(8,128)(2,1)}) %reduce-scatter.32.cloned.1.call-update) | async-done | bytes 196624 | tf_op jit(solution)/shard_map/reduce_scatter | solution.py:785
  1031.5 5.5 all-to-all-start.8
  1037.5 3.9 all-to-all-done.8
  (236 shorter events, 118.4 us)
Async XLA Ops:
  8.0 182.4 %copy-start = (bf16[256,1024]{1,0:T(8,128)(2,1)S(1)}, bf16[256,1024]{1,0:T(8,128)(2,1)}, u32[]{:S(2)}) copy-start(bf16[256,1024]{1,0:T(8,128)(2,1)} %param.26) | copy-start | bytes 1572868
  8.0 37.2 %all-gather.9.cloned.1.call-start = ((), (), s32[]{:S(2)}) async-start(), calls=%async_computation.27 | async-start | bytes 1310720 | tf_op jit(solution)/shard_map/all_gather | solution.py:753
  48.0 8.0 copy-start.28
  48.0 14.4 %copy-start.26 = (s32[8,2]{0,1:T(2,128)S(1)}, s32[8,2]{0,1:T(2,128)}, u32[]{:S(2)}) copy-start(s32[8,2]{0,1:T(2,128)} %param.21) | copy-start | bytes 196
  48.2 45.1 %copy-start.21 = (bf16[256,1024]{1,0:T(8,128)(2,1)S(1)}, bf16[256,1024]{1,0:T(8,128)(2,1)}, u32[]{:S(2)}) copy-start(bf16[256,1024]{1,0:T(8,128)(2,1)} %param.23) | copy-start | bytes 1572868
  49.2 23.9 %all-to-all-start.1 = ((bf16[8,384,128]{2,1,0:T(8,128)(2,1)}), bf16[8,384,128]{2,1,0:T(8,128)(2,1)S(1)}, u32[]{:S(2)}, u32[]{:S(2)}) async-start(bf16[8,384,128]{2,1,0:T(8,128)(2,1)} %bitcast.10), calls=%async_computation.1 | async-start | bytes 1572864 | tf_op jit(solution)/shard_map/all_to_all | solution.py:763
  54.7 71.2 %reduce-scatter.16.cloned.1.call-start = ((), (), s32[]{:S(2)}) async-start(), calls=%async_computation.28 | async-start | bytes 1310720 | tf_op jit(solution)/shard_map/reduce_scatter | solution.py:757
  96.2 29.6 %copy-start.3 = (bf16[1,128,1024]{2,1,0:T(8,128)(2,1)S(1)}, bf16[1,128,1024]{2,1,0:T(8,128)(2,1)}, u32[]{:S(2)}) copy-start(bf16[1,128,1024]{2,1,0:T(8,128)(2,1)} %param.16) | copy-start | bytes 786436
  97.3 25.9 %all-to-all-start.4 = ((bf16[4,256,512]{1,2,0:T(8,128)(2,1)}), bf16[4,256,512]{1,2,0:T(8,128)(2,1)}, u32[]{:S(2)}, u32[]{:S(2)}) async-start(bf16[4,256,512]{1,2,0:T(8,128)(2,1)} %bitcast.30), calls=%async_computation.5 | async-start | bytes 2097152 | tf_op jit(solution)/shard_map/all_to_all | solution.py:763
  102.5 59.6 %all-gather.13.cloned.1.call-start = ((), (), s32[]{:S(2)}) async-start(), calls=%async_computation.30 | async-start | bytes 1179648 | tf_op jit(solution)/shard_map/all_gather | solution.py:860
  123.1 23.3 %copy-start.15 = (bf16[1,128,1024]{2,1,0:T(8,128)(2,1)}, bf16[1,128,1024]{2,1,0:T(8,128)(2,1)S(1)}, u32[]{:S(2)}) copy-start(bf16[1,128,1024]{2,1,0:T(8,128)(2,1)S(1)} %all-gather) | copy-start | bytes 786436
  124.7 37.4 %copy-start.8 = (bf16[4,256,512]{2,1,0:T(8,128)(2,1)}, bf16[4,256,512]{2,1,0:T(8,128)(2,1)S(1)}, u32[]{:S(2)}) copy-start(bf16[4,256,512]{2,1,0:T(8,128)(2,1)S(1)} %copy.64) | copy-start | bytes 3145732
  125.8 58.2 %all-gather.11.cloned.1.call-start = ((), (), s32[]{:S(2)}) async-start(), calls=%async_computation.29 | async-start | bytes 1310720 | tf_op jit(solution)/shard_map/all_gather | solution.py:753
  132.0 12.4 %all-to-all-start.3 = ((bf16[4,256,256]{1,2,0:T(8,128)(2,1)}), bf16[4,256,256]{1,2,0:T(8,128)(2,1)}, u32[]{:S(2)}, u32[]{:S(2)}) async-start(bf16[4,256,256]{1,2,0:T(8,128)(2,1)} %bitcast.283), calls=%async_computation.4 | async-start | bytes 1048576 | tf_op jit(solution)/shard_map/all_to_all | solution.py:763
  136.3 86.1 %reduce-scatter.18.cloned.1.call-start = ((), (), s32[]{:S(2)}) async-start(), calls=%async_computation.31 | async-start | bytes 1310720 | tf_op jit(solution)/shard_map/reduce_scatter | solution.py:757
  198.3 69.4 %all-to-all-start.5 = ((bf16[4,256,2048]{1,2,0:T(8,128)(2,1)}), bf16[4,256,2048]{1,2,0:T(8,128)(2,1)}, u32[]{:S(2)}, u32[]{:S(2)}) async-start(bf16[4,256,2048]{1,2,0:T(8,128)(2,1)} %bitcast.259), calls=%async_computation.7 | async-start | bytes 8388608 | tf_op jit(solution)/shard_map/all_to_all | solution.py:763
  203.4 30.9 %all-gather.17.cloned.1.call-start = ((), (), s32[]{:S(2)}) async-start(), calls=%async_computation.34 | async-start | bytes 1310720 | tf_op jit(solution)/shard_map/all_gather | solution.py:753
  205.3 68.7 %all-gather.15.cloned.1.call-start = ((), (), s32[]{:S(2)}) async-start(), calls=%async_computation.32 | async-start | bytes 1310720 | tf_op jit(solution)/shard_map/all_gather | solution.py:753
  225.4 88.9 %reduce-scatter.22.cloned.1.call-start = ((), (), s32[]{:S(2)}) async-start(), calls=%async_computation.35 | async-start | bytes 1310720 | tf_op jit(solution)/shard_map/reduce_scatter | solution.py:757
  274.0 11.9 %copy-start.11 = (bf16[4,256,2048]{2,1,0:T(8,128)(2,1)S(1)}, bf16[4,256,2048]{2,1,0:T(8,128)(2,1)}, u32[]{:S(2)}) copy-start(bf16[4,256,2048]{2,1,0:T(8,128)(2,1)} %copy.68) | copy-start | bytes 12582916
  289.3 53.2 %reduce-scatter.20.cloned.1.call-start = ((), (), s32[]{:S(2)}) async-start(), calls=%async_computation.33 | async-start | bytes 1310720 | tf_op jit(solution)/shard_map/reduce_scatter | solution.py:757
  296.4 66.0 %all-gather.19.cloned.1.call-start = ((), (), s32[]{:S(2)}) async-start(), calls=%async_computation.36 | async-start | bytes 1310720 | tf_op jit(solution)/shard_map/all_gather | solution.py:753
  345.0 56.7 %reduce-scatter.24.cloned.1.call-start = ((), (), s32[]{:S(2)}) async-start(), calls=%async_computation.37 | async-start | bytes 1310720 | tf_op jit(solution)/shard_map/reduce_scatter | solution.py:757
  364.1 37.6 %copy-start.4 = (bf16[1,128,1024]{2,1,0:T(8,128)(2,1)S(1)}, bf16[1,128,1024]{2,1,0:T(8,128)(2,1)}, u32[]{:S(2)}) copy-start(bf16[1,128,1024]{2,1,0:T(8,128)(2,1)} %param.16) | copy-start | bytes 786436
  374.4 28.6 %copy-start.7 = (bf16[128,1024]{1,0:T(8,128)(2,1)S(1)}, bf16[128,1024]{1,0:T(8,128)(2,1)}, u32[]{:S(2)}) copy-start(bf16[128,1024]{1,0:T(8,128)(2,1)} %reduce-scatter.16.cloned.1.call-done) | copy-start | bytes 786436
  374.4 28.6 %copy-start.18 = (f32[128,1024]{1,0:T(8,128)S(1)}, f32[128,1024]{1,0:T(8,128)}, u32[]{:S(2)}) copy-start(f32[128,1024]{1,0:T(8,128)} %get-tuple-element.48) | copy-start | bytes 1572868
  377.0 88.9 %reduce-scatter.28.cloned.1.call-start = ((), (), s32[]{:S(2)}) async-start(), calls=%async_computation.40 | async-start | bytes 1179648 | tf_op jit(solution)/shard_map/reduce_scatter | solution.py:915
  379.4 86.6 %copy-start.16 = (bf16[1,128,1024]{2,1,0:T(8,128)(2,1)S(1)}, bf16[1,128,1024]{2,1,0:T(8,128)(2,1)}, u32[]{:S(2)}) copy-start(bf16[1,128,1024]{2,1,0:T(8,128)(2,1)} %copy-done.15) | copy-start | bytes 786436
  379.4 110.5 %all-gather.21.cloned.1.call-start = ((), (), s32[]{:S(2)}) async-start(), calls=%async_computation.38 | async-start | bytes 1310720 | tf_op jit(solution)/shard_map/all_gather | solution.py:753
  405.2 190.5 %reduce-scatter.36.cloned.1.call-start = ((), (), s32[]{:S(2)}) async-start(), calls=%async_computation.44 | async-start | bytes 589824 | tf_op jit(solution)/shard_map/reduce_scatter | solution.py:785
  407.8 196.3 %reduce-scatter.38.cloned.1.call-start = ((), (), s32[]{:S(2)}) async-start(), calls=%async_computation.45 | async-start | bytes 1179648 | tf_op jit(solution)/shard_map/reduce_scatter | solution.py:785
  471.0 194.1 %reduce-scatter.40.cloned.1.call-start = ((), (), s32[]{:S(2)}) async-start(), calls=%async_computation.46 | async-start | bytes 589824 | tf_op jit(solution)/shard_map/reduce_scatter | solution.py:777
  473.6 285.2 %reduce-scatter.42.cloned.1.call-start = ((), (), s32[]{:S(2)}) async-start(), calls=%async_computation.47 | async-start | bytes 4718592 | tf_op jit(solution)/shard_map/reduce_scatter | solution.py:785
  479.9 302.4 %reduce-scatter.30.cloned.1.call-start = ((), (), s32[]{:S(2)}) async-start(), calls=%async_computation.41 | async-start | bytes 327680 | tf_op jit(solution)/shard_map/reduce_scatter | solution.py:757
  482.3 391.1 %reduce-scatter.44.cloned.1.call-start = ((), (), s32[]{:S(2)}) async-start(), calls=%async_computation.48 | async-start | bytes 4718592 | tf_op jit(solution)/shard_map/reduce_scatter | solution.py:777
  489.8 32.3 %copy-start.13 = (bf16[4,128,1,2,128]{4,3,1,0,2:T(2,128)(2,1)S(1)}, bf16[4,128,1,2,128]{4,3,1,0,2:T(2,128)(2,1)}, u32[]{:S(2)}) copy-start(bf16[4,128,1,2,128]{4,3,1,0,2:T(2,128)(2,1)} %copy-done.12) | copy-start | bytes 786436
  490.8 31.3 %copy-start.20 = (bf16[512,1024]{1,0:T(8,128)(2,1)S(1)}, bf16[512,1024]{1,0:T(8,128)(2,1)}, u32[]{:S(2)}) copy-start(bf16[512,1024]{1,0:T(8,128)(2,1)} %all-gather.21.cloned.1.call-done) | copy-start | bytes 3145732
  516.0 25.4 %all-to-all-start.7 = ((bf16[8,384,128]{2,1,0:T(8,128)(2,1)}), bf16[8,384,128]{2,1,0:T(8,128)(2,1)S(1)}, u32[]{:S(2)}, u32[]{:S(2)}) async-start(bf16[8,384,128]{2,1,0:T(8,128)(2,1)} %bitcast.54), calls=%async_computation.12 | async-start | bytes 1572864 | tf_op jit(solution)/shard_map/all_to_all | solution.py:763
  522.1 414.3 %reduce-scatter.34.cloned.1.call-start = ((), (), s32[]{:S(2)}) async-start(), calls=%async_computation.43 | async-start | bytes 589824 | tf_op jit(solution)/shard_map/reduce_scatter | solution.py:777
  523.4 443.0 %reduce-scatter.26.cloned.1.call-start = ((), (), s32[]{:S(2)}) async-start(), calls=%async_computation.39 | async-start | bytes 1310720 | tf_op jit(solution)/shard_map/reduce_scatter | solution.py:757
  549.0 482.5 %reduce-scatter.32.cloned.1.call-start = ((), (), s32[]{:S(2)}) async-start(), calls=%async_computation.42 | async-start | bytes 1769472 | tf_op jit(solution)/shard_map/reduce_scatter | solution.py:785
  595.7 8.3 all-to-all-start.9
  604.1 62.6 %all-to-all-start.10 = ((bf16[4,32,512]{2,1,0:T(8,128)(2,1)}), bf16[4,32,512]{2,1,0:T(8,128)(2,1)S(1)}, u32[]{:S(2)}, u32[]{:S(2)}) async-start(bf16[4,32,512]{2,1,0:T(8,128)(2,1)} %bitcast.297), calls=%async_computation.22 | async-start | bytes 262144 | tf_op jit(solution)/shard_map/all_to_all | solution.py:763
  758.8 179.1 %all-to-all-start.11 = ((bf16[4,32,2048]{2,1,0:T(8,128)(2,1)}), bf16[4,32,2048]{2,1,0:T(8,128)(2,1)S(1)}, u32[]{:S(2)}, u32[]{:S(2)}) async-start(bf16[4,32,2048]{2,1,0:T(8,128)(2,1)} %bitcast.293), calls=%async_computation.25 | async-start | bytes 1048576 | tf_op jit(solution)/shard_map/all_to_all | solution.py:763
  784.0 182.4 %copy-start.5 = (bf16[1,128,1024]{2,1,0:T(8,128)(2,1)S(1)}, bf16[1,128,1024]{2,1,0:T(8,128)(2,1)}, u32[]{:S(2)}) copy-start(bf16[1,128,1024]{2,1,0:T(8,128)(2,1)} %param.16) | copy-start | bytes 786436
  785.1 221.4 %copy-start.17 = (f32[128,1024]{1,0:T(8,128)S(1)}, f32[128,1024]{1,0:T(8,128)}, u32[]{:S(2)}) copy-start(f32[128,1024]{1,0:T(8,128)} %get-tuple-element.46) | copy-start | bytes 1572868
  937.9 104.9 %copy-start.1 = (bf16[256,1024]{1,0:T(8,128)(2,1)S(1)}, bf16[256,1024]{1,0:T(8,128)(2,1)}, u32[]{:S(2)}) copy-start(bf16[256,1024]{1,0:T(8,128)(2,1)} %param.26) | copy-start | bytes 1572868
  1031.5 10.0 all-to-all-start.8
  (13 other events, 29.6 us)
Sparse Core Ops, SparseCore 0:
  14.1 23.7 all-gather.8
  94.8 29.6 reduce-scatter.15
  206.4 27.9 all-gather.16
  236.4 22.4 all-gather.14
  345.1 17.2 all-gather.18
  377.1 24.4 reduce-scatter.23
  406.0 59.8 reduce-scatter.27
  469.3 64.2 reduce-scatter.35
  537.9 62.3 reduce-scatter.37
  604.1 61.0 reduce-scatter.39
  669.2 89.5 reduce-scatter.41
  761.7 20.6 reduce-scatter.29
  786.4 86.9 reduce-scatter.43
  877.3 59.1 reduce-scatter.33
  939.0 27.4 reduce-scatter.25
  969.7 61.7 reduce-scatter.31
Sparse Core Ops, SparseCore 1:
  125.8 36.2 all-gather.12
  164.2 19.7 all-gather.10
  192.0 30.4 reduce-scatter.17
  289.3 24.9 reduce-scatter.21
  317.6 24.8 reduce-scatter.19
  405.3 16.9 all-gather.20

commit v2 on v1

--- a/solution.py
+++ b/solution.py
@@ -749,6 +749,605 @@
     )(source_lengths, query, kv, grad)
 
 
+MESH = pl.DeviceIdType.MESH
+
+
+class Links:
+    def __init__(self, send, recv, local):
+        self.send, self.recv, self.local = send, recv, local
+        self.count, self.local_count = 0, 0
+        self.sends, self.saves = [], []
+
+    def slots(self, count):
+        start = self.count
+        self.count += count
+        return start
+
+    def copy(self, index, src, dst, device):
+        return pltpu.make_async_remote_copy(
+            src_ref=src,
+            dst_ref=dst,
+            send_sem=self.send.at[index],
+            recv_sem=self.recv.at[index],
+            device_id=device,
+            device_id_type=MESH,
+        )
+
+    def push(self, index, src, dst, device, when=None):
+        made = self.copy(index, src, dst, device)
+        if when is None:
+            made.start()
+        else:
+            pl.when(when)(made.start)
+        self.sends.append((made, when))
+
+    def take(self, index, dst, device, when=None):
+        made = self.copy(index, dst, dst, device)
+        if when is None:
+            made.wait_recv()
+        else:
+            pl.when(when)(made.wait_recv)
+
+    def save(self, src, dst):
+        made = pltpu.make_async_copy(src, dst, self.local.at[self.local_count])
+        self.local_count += 1
+        made.start()
+        self.saves.append(made)
+        return made
+
+    def finish(self):
+        for made, when in self.sends:
+            if when is None:
+                made.wait_send()
+            else:
+                pl.when(when)(made.wait_send)
+        for made in self.saves:
+            made.wait()
+        self.sends, self.saves = [], []
+
+
+class Place:
+    def __init__(self):
+        self.s, self.c = lax.axis_index("seq"), lax.axis_index("ctx")
+        self.k, self.x = lax.rem(self.s, 2), lax.div(self.s, 2)
+        self.y, self.z = lax.rem(self.c, 2), lax.div(self.c, 2)
+        self.sib = self.s + 1 - 2 * self.k
+        self.far = lax.rem(self.s + 2, 4)
+        self.opp = lax.rem(self.sib + 2, 4)
+        self.pair = self.c + 1 - 2 * self.y
+
+    def greet(self):
+        barrier = pltpu.get_barrier_semaphore()
+        for other in (self.sib, self.far, self.opp):
+            pl.semaphore_signal(barrier, inc=1, device_id=(other, self.c), device_id_type=MESH)
+        for step in range(1, 8):
+            pl.semaphore_signal(
+                barrier,
+                inc=1,
+                device_id=(self.s, lax.rem(self.c + step, 8)),
+                device_id_type=MESH,
+            )
+        pl.semaphore_wait(barrier, 10)
+
+
+def rows_at(start, count):
+    return pl.ds(pl.multiple_of(start, 16), count)
+
+
+def lanes_at(start, count):
+    return pl.ds(pl.multiple_of(start, 128), count)
+
+
+class Columns:
+    def __init__(self, links, place, weight, dest, parts, pieces=1):
+        self.links, self.place, self.weight, self.dest = links, place, weight, dest
+        rows, columns = weight.shape
+        self.rows, self.whole, self.width = rows, columns // parts, columns // (4 * parts)
+        self.step = rows // pieces
+        self.jobs = [(part, piece) for piece in range(pieces) for part in range(parts)]
+        self.base = {job: links.slots(5) for job in self.jobs}
+        self.mine = place.k == place.y
+
+    def source(self, job, target):
+        part, piece = job
+        return self.weight.at[
+            pl.ds(piece * self.step, self.step),
+            lanes_at(part * self.whole + target * self.width, self.width),
+        ]
+
+    def land(self, job, owner):
+        part, piece = job
+        return self.dest.at[
+            rows_at(owner * self.rows + piece * self.step, self.step),
+            pl.ds(part * self.width, self.width),
+        ]
+
+    def start(self, jobs=None):
+        p = self.place
+        for job in self.jobs if jobs is None else jobs:
+            base = self.base[job]
+            land = self.land(job, p.s)
+            self.links.push(base, self.source(job, p.far), land, (p.far, p.c), self.mine)
+            self.links.push(base + 1, self.source(job, p.opp), land, (p.opp, p.c), self.mine)
+            self.links.push(base + 2, self.source(job, p.sib), land, (p.sib, p.c))
+            self.links.save(self.source(job, p.s), land)
+
+    def relay(self, jobs=None):
+        p = self.place
+        came = lax.rem(p.x + 1, 2) * 2 + p.y
+        for job in self.jobs if jobs is None else jobs:
+            base = self.base[job]
+            land = self.land(job, came)
+            self.links.take(base, land, (p.far, p.c), p.k == p.y)
+            self.links.take(base + 1, land, (p.opp, p.c), p.k != p.y)
+            self.links.push(base + 3, land, land, (p.s, p.pair))
+
+    def finish(self):
+        p = self.place
+        for job in self.jobs:
+            base = self.base[job]
+            self.links.take(base + 2, self.land(job, p.sib), (p.sib, p.c))
+            self.links.take(
+                base + 3,
+                self.land(job, lax.rem(p.x + 1, 2) * 2 + 1 - p.y),
+                (p.s, p.pair),
+            )
+
+
+class Gather:
+    def __init__(self, links, place, dest, rows, pieces=1):
+        self.links, self.place, self.dest, self.rows = links, place, dest, rows
+        self.step = rows // pieces
+        self.base = [links.slots(3) for _ in range(pieces)]
+
+    def land(self, piece, owner):
+        return self.dest.at[rows_at(owner * self.rows + piece * self.step, self.step)]
+
+    def start(self, piece=0):
+        p, base = self.place, self.base[piece]
+        land = self.land(piece, p.s)
+        self.links.push(base, land, land, (p.far, p.c))
+        self.links.push(base + 1, land, land, (p.sib, p.c))
+
+    def forward(self, piece=0):
+        p, base = self.place, self.base[piece]
+        land = self.land(piece, p.far)
+        self.links.take(base, land, (p.far, p.c))
+        self.links.push(base + 2, land, land, (p.sib, p.c))
+
+    def finish(self, piece=0):
+        p, base = self.place, self.base[piece]
+        self.links.take(base + 1, self.land(piece, p.sib), (p.sib, p.c))
+        self.links.take(base + 2, self.land(piece, p.opp), (p.sib, p.c))
+
+    def all(self):
+        for piece in range(len(self.base)):
+            self.start(piece)
+        for piece in range(len(self.base)):
+            self.forward(piece)
+        for piece in range(len(self.base)):
+            self.finish(piece)
+
+
+class Reduce:
+    def __init__(self, links, place, out, into, rows, pieces=1):
+        self.links, self.place, self.out, self.into = links, place, out, into
+        self.step = rows // pieces
+        self.base = [links.slots(3) for _ in range(pieces)]
+
+    def run(self, partial, then):
+        p, links, out, into = self.place, self.links, self.out, self.into
+        count, step = len(self.base), self.step
+        cut = [pl.ds(piece * step, step) for piece in range(count)]
+        here = (p.sib, p.c)
+        for piece, base in enumerate(self.base):
+            out[0, cut[piece]] = partial(p.opp, piece).astype(BF16)
+            links.push(base, out.at[0, cut[piece]], into.at[0, cut[piece]], here)
+        for piece, base in enumerate(self.base):
+            held = partial(p.far, piece)
+            links.take(base, into.at[0, cut[piece]], here)
+            out[2, cut[piece]] = (held + into[0, cut[piece]].astype(F32)).astype(BF16)
+            links.push(base + 1, out.at[2, cut[piece]], into.at[2, cut[piece]], (p.far, p.c))
+        for piece, base in enumerate(self.base):
+            out[1, cut[piece]] = partial(p.sib, piece).astype(BF16)
+            links.push(base + 2, out.at[1, cut[piece]], into.at[1, cut[piece]], here)
+        for piece, base in enumerate(self.base):
+            held = partial(p.s, piece)
+            links.take(base + 2, into.at[1, cut[piece]], here)
+            held = held + into[1, cut[piece]].astype(F32)
+            links.take(base + 1, into.at[2, cut[piece]], (p.far, p.c))
+            then(piece, held + into[2, cut[piece]].astype(F32))
+
+
+def row_positions(table_ref, owner, half):
+    place = lax.broadcasted_iota(jnp.int32, (2 * half, 1), 0)
+    first, second = table_ref[owner, 0] * half, table_ref[owner, 1] * half - half
+    return place + jnp.where(place < half, first, second)
+
+
+def column_positions(table_ref, owner, half):
+    place = lax.broadcasted_iota(jnp.int32, (1, 2 * half), 1)
+    first, second = table_ref[owner, 0] * half, table_ref[owner, 1] * half - half
+    return place + jnp.where(place < half, first, second)
+
+
+def softmax_rows(scores):
+    top = jnp.max(scores, axis=-1, keepdims=True)
+    expos = jnp.exp(scores - top)
+    return expos * (1.0 / jnp.sum(expos, axis=-1, keepdims=True)), top
+
+
+PIECES = 2
+STEPS = 8
+
+
+def forward_kernel(
+    table_ref,
+    target_ref,
+    source_ref,
+    tokens_ref,
+    encoder_ref,
+    cotangent_ref,
+    qkv_ref,
+    out_ref,
+    cq_ref,
+    ckv_ref,
+    co_ref,
+    up_ref,
+    gain_ref,
+    bias_ref,
+    first_out,
+    second_out,
+    third_out,
+    branch_out,
+    source_out,
+    w_qkv_out,
+    w_cq_out,
+    w_ckv_out,
+    w_up_out,
+    heads_out,
+    mix_out,
+    query_out,
+    kvs_out,
+    cross_out_ref,
+    sums_out,
+    peak_out,
+    lens_out,
+    first,
+    second,
+    third,
+    branch,
+    source,
+    w_qkv,
+    w_cq,
+    w_ckv,
+    sent,
+    heads,
+    mix_own,
+    mix,
+    query,
+    kv_own,
+    kvs,
+    cross,
+    sums,
+    columns,
+    lens,
+    rs_out,
+    rs_in,
+    send_sem,
+    recv_sem,
+    local_sem,
+):
+    place, links = Place(), Links(send_sem, recv_sem, local_sem)
+    p = place
+    rows = tokens_ref.shape[1]
+    source_rows = encoder_ref.shape[1]
+    half = rows // 2
+    width = w_cq.shape[1]
+    pair_width = heads.shape[2]
+    held = width // HD
+    groups = width // pair_width
+    place.greet()
+
+    get_qkv = Columns(links, place, qkv_ref, w_qkv, 3)
+    get_qkv.start()
+
+    own = rows_at(p.s * rows, rows)
+    inputs = tokens_ref[0].astype(F32)
+    first[own] = norm_forward(inputs, gain_ref[0:1], bias_ref[0:1])[2]
+    get_first = Gather(links, place, first, rows)
+    get_first.start()
+    source[rows_at(p.s * source_rows, source_rows)] = encoder_ref[0]
+    get_source = Gather(links, place, source, source_rows)
+    get_source.start()
+    place_lens = links.slots(3)
+    line = lax.broadcasted_iota(jnp.int32, (8, 128), 0)
+    lens[pl.ds(p.s, 1)] = jnp.where(line < 4, target_ref[0], source_ref[0])[None]
+    own_lens = lens.at[pl.ds(p.s, 1)]
+    for step, other in enumerate((p.far, p.opp, p.sib)):
+        links.push(place_lens + step, own_lens, own_lens, (other, p.c))
+    for owner in range(STEPS):
+        columns[:, owner * rows : (owner + 1) * rows] = column_positions(table_ref, owner, half)
+    own_rows = row_positions(table_ref, p.c, half)
+    valid = own_rows < target_ref[0]
+    branch[own] = jnp.where(valid, cotangent_ref[0].astype(F32), 0.0).astype(BF16)
+    get_cq = Columns(links, place, cq_ref, w_cq, 1)
+    get_ckv = Columns(links, place, ckv_ref, w_ckv, 2)
+    get_up = Columns(links, place, up_ref, w_up_out, 1, 4)
+
+    get_qkv.relay()
+    get_first.forward()
+    get_source.forward()
+    get_first.finish()
+    get_source.finish()
+    for made in links.saves:
+        made.wait()
+    links.saves = []
+    get_qkv.finish()
+    links.save(first, first_out)
+    links.save(w_qkv, w_qkv_out)
+    links.save(source, source_out)
+    for step, other in enumerate((p.far, p.opp, p.sib)):
+        links.take(place_lens + step, lens.at[pl.ds(other, 1)], (other, p.c))
+    links.save(lens, lens_out)
+
+    def project(block, carry):
+        value = dot(first[rows_at(block * rows, rows)], w_qkv[...]).astype(BF16)
+        for group in range(groups):
+            for part in range(3):
+                at = part * width + group * pair_width
+                sent[block * groups + group, part] = value[:, at : at + pair_width]
+        return carry
+
+    lax.fori_loop(0, 4, project, 0)
+    a2a = links.slots(STEPS)
+    mine = rows_at(p.c * rows, rows)
+    for step in range(1, STEPS):
+        other = lax.rem(p.c + step, STEPS)
+        links.push(a2a + step, sent.at[other], heads.at[:, mine], (p.s, other))
+    keep = pltpu.make_async_copy(sent.at[p.c], heads.at[:, mine], local_sem.at[STEPS * 8 - 1])
+    keep.start()
+    get_cq.start()
+    get_ckv.start()
+    get_up.start(get_up.jobs[:2])
+    get_branch = Gather(links, place, branch, rows)
+    get_branch.start()
+    keep.wait()
+    get_cq.relay()
+    get_ckv.relay()
+    for step in range(1, STEPS):
+        other = lax.rem(p.c + STEPS - step, STEPS)
+        links.take(a2a + step, heads.at[:, rows_at(other * rows, rows)], (p.s, other))
+    links.save(heads, heads_out)
+
+    my_slot = lax.div(p.c, groups)
+    my_group = lax.rem(p.c, groups)
+    length = lens[pl.ds(my_slot, 1)][0, 0:1, 0:1]
+    back = links.slots(STEPS)
+    slot_rows = rows_at(my_slot * rows, rows)
+    group_lanes = lanes_at(my_group * pair_width, pair_width)
+
+    def back_copy(owner):
+        return links.copy(
+            back + p.c, mix_own.at[rows_at(owner * rows, rows)], mix.at[slot_rows, group_lanes], (p.s, owner)
+        )
+
+    def attend(block, peaks):
+        at = rows_at(block * 2 * rows, 2 * rows)
+        row_pos = jnp.concatenate(
+            [row_positions(table_ref, 2 * block, half), row_positions(table_ref, 2 * block + 1, half)], axis=0
+        )
+        col_pos = columns[...]
+        allowed = (col_pos <= row_pos) & (col_pos < length)
+        ok = row_pos < length
+        tops = []
+        for head in range(pair_width // HD):
+            cut = slice(head * HD, (head + 1) * HD)
+            scores = dot(heads[0, at, cut], heads[1, :, cut], NT) * SCALE
+            probs, top = softmax_rows(jnp.where(allowed, scores, masked_score))
+            mix_own[at, cut] = dot(probs.astype(BF16), heads[2, :, cut]).astype(BF16)
+            peak = jnp.max(jnp.where(ok, top, masked_score), axis=0, keepdims=True)
+            tops.append(jnp.maximum(peaks[head], peak))
+        return tuple(tops)
+
+    low = jnp.full((1, 1), masked_score, F32)
+    peaks = (low, low)
+    for block in range(STEPS // 2):
+        peaks = attend(block, peaks)
+        for owner in (2 * block, 2 * block + 1):
+            pl.when(p.c != owner)(back_copy(owner).start)
+    for head in range(2):
+        peak_out[head : head + 1] = jnp.broadcast_to(peaks[head], (1, 128))
+    mix[slot_rows, group_lanes] = mix_own[mine]
+
+    get_cq.finish()
+    get_ckv.finish()
+    for made in links.saves:
+        made.wait()
+    links.saves = []
+    links.save(w_cq, w_cq_out)
+    links.save(w_ckv, w_ckv_out)
+    value = dot(source[...], w_ckv[...]).astype(BF16)
+    for slot in range(4):
+        kv_own[slot] = value[slot * source_rows : (slot + 1) * source_rows]
+    own_keys = rows_at(p.c * source_rows, source_rows)
+    kvs[:, own_keys] = kv_own[...]
+    along, across = links.slots(4), links.slots(4)
+    links.push(across, kv_own, kvs.at[:, own_keys], (p.s, p.pair))
+    for step in range(1, 4):
+        other = lax.rem(p.z + step, 4) * 2 + p.y
+        links.push(along + step, kv_own, kvs.at[:, own_keys], (p.s, other))
+    get_up.relay(get_up.jobs[:2])
+    get_branch.forward()
+
+    for owner in range(STEPS):
+
+        @pl.when(p.c != owner)
+        def _():
+            lane = lanes_at((owner % groups) * pair_width, pair_width)
+            links.take(
+                back + owner, mix.at[pl.ds((owner // groups) * rows, rows), lane], (p.s, owner)
+            )
+
+    links.save(mix, mix_out)
+
+    def boundary(index, left, weight, base, gather, store):
+        def partial(block, piece):
+            step = rows // PIECES
+            return dot(left[rows_at(block * rows + piece * step, step)], weight[...])
+
+        def then(piece, total):
+            step = rows // PIECES
+            cut = pl.ds(piece * step, step)
+            value = base(piece) + total
+            sums[index, cut] = value
+            store[rows_at(p.s * rows + piece * step, step)] = norm_forward(
+                value, gain_ref[index + 1 : index + 2], bias_ref[index + 1 : index + 2]
+            )[2]
+            gather.start(piece)
+
+        Reduce(links, place, rs_out.at[index], rs_in.at[index], rows, PIECES).run(partial, then)
+
+    step = rows // PIECES
+    get_second = Gather(links, place, second, rows, PIECES)
+    boundary(
+        0,
+        mix,
+        out_ref,
+        lambda piece: tokens_ref[0, piece * step : (piece + 1) * step].astype(F32),
+        get_second,
+        second,
+    )
+    for hop in range(1, 4):
+        other = lax.rem(p.z + 4 - hop, 4) * 2 + p.y
+        land = kvs.at[:, rows_at(other * source_rows, source_rows)]
+        links.take(along + hop, land, (p.s, other))
+        links.push(across + hop, land, land, (p.s, p.pair))
+    get_up.start(get_up.jobs[2:])
+    for piece in range(PIECES):
+        get_second.forward(piece)
+    for piece in range(PIECES):
+        get_second.finish(piece)
+    links.save(second, second_out)
+    for hop in range(4):
+        other = lax.rem(p.z + 4 - hop, 4) * 2 + 1 - p.y
+        land = kvs.at[:, rows_at(other * source_rows, source_rows)]
+        links.take(across + hop, land, (p.s, p.pair))
+    links.save(kvs, kvs_out)
+
+    keys = kvs.shape[1]
+
+    def cross_attend(slot, peaks):
+        at = rows_at(slot * rows, rows)
+        asked = dot(second[at], w_cq[...]).astype(BF16)
+        query[at] = asked
+        limits = lens[pl.ds(slot, 1)]
+        live = lax.broadcasted_iota(jnp.int32, (1, keys), 1) < limits[0, 4:5, 0:1]
+        ok = own_rows < limits[0, 0:1, 0:1]
+        tops = []
+        for head in range(held):
+            cut = slice(head * HD, (head + 1) * HD)
+            vcut = slice(width + head * HD, width + (head + 1) * HD)
+            scores = dot(asked[:, cut], kvs[slot, :, cut], NT) * SCALE
+            probs, top = softmax_rows(jnp.where(live, scores, masked_score))
+            cross[at, cut] = dot(probs.astype(BF16), kvs[slot, :, vcut]).astype(BF16)
+            peak = jnp.max(jnp.where(ok, top, masked_score), axis=0, keepdims=True)
+            tops.append(jnp.maximum(peaks[head], peak))
+        return tuple(tops)
+
+    peaks = lax.fori_loop(0, 4, cross_attend, (low,) * held)
+    for head in range(held):
+        peak_out[2 + head : 3 + head] = jnp.broadcast_to(peaks[head], (1, 128))
+    links.save(query, query_out)
+    links.save(cross, cross_out_ref)
+    get_up.relay(get_up.jobs[2:])
+    get_branch.finish()
+    links.save(branch, branch_out)
+    get_third = Gather(links, place, third, rows, PIECES)
+    boundary(
+        1, cross, co_ref, lambda piece: sums[0, piece * step : (piece + 1) * step], get_third, third
+    )
+    links.save(sums, sums_out)
+    for piece in range(PIECES):
+        get_third.forward(piece)
+    for piece in range(PIECES):
+        get_third.finish(piece)
+    links.save(third, third_out)
+    get_up.finish()
+    for owner in range(STEPS):
+        pl.when(p.c != owner)(back_copy(owner).wait_send)
+    links.finish()
+
+
+def forward_call(
+    table, targets, sources, tokens, encoder, cotangent, qkv, out, cq, ckv, co, up, gain, bias
+):
+    rows, width = tokens.shape[1], out.shape[0]
+    source_rows = encoder.shape[1]
+    depth = tokens.shape[2]
+    keys = 8 * source_rows
+    any_space = pl.BlockSpec(memory_space=pl.ANY)
+    vmem = pl.BlockSpec(memory_space=pltpu.VMEM)
+    smem = pl.BlockSpec(memory_space=pltpu.SMEM)
+    shapes = dict(
+        first=((4 * rows, depth), BF16),
+        second=((4 * rows, depth), BF16),
+        third=((4 * rows, depth), BF16),
+        branch=((4 * rows, depth), BF16),
+        source=((4 * source_rows, depth), BF16),
+        w_qkv=((depth, 3 * width), BF16),
+        w_cq=((depth, width), BF16),
+        w_ckv=((depth, 2 * width), BF16),
+        w_up=((depth, up.shape[1] // 4), BF16),
+        heads=((3, 8 * rows, 128), BF16),
+        mix=((4 * rows, width), BF16),
+        query=((4 * rows, width), BF16),
+        kvs=((4, keys, 2 * width), BF16),
+        cross=((4 * rows, width), BF16),
+        sums=((2, rows, depth), F32),
+        peak=((8, 128), F32),
+        lens=((4, 8, 128), jnp.int32),
+    )
+    scratch = [
+        shapes[name]
+        for name in ("first", "second", "third", "branch", "source", "w_qkv", "w_cq", "w_ckv")
+    ] + [
+        ((8, 3, rows, 128), BF16),
+        shapes["heads"],
+        ((8 * rows, 128), BF16),
+        shapes["mix"],
+        shapes["query"],
+        ((4, source_rows, 2 * width), BF16),
+        shapes["kvs"],
+        shapes["cross"],
+        shapes["sums"],
+        ((1, 8 * rows), jnp.int32),
+        shapes["lens"],
+        ((2, 3, rows, depth), BF16),
+        ((2, 3, rows, depth), BF16),
+    ]
+    made = pl.pallas_call(
+        forward_kernel,
+        in_specs=[smem] * 3
+        + [vmem] * 3
+        + [any_space, vmem, any_space, any_space, vmem, any_space]
+        + [vmem] * 2,
+        out_specs=[vmem if name == "peak" else any_space for name in shapes],
+        out_shape=[jax.ShapeDtypeStruct(*shape) for shape in shapes.values()],
+        scratch_shapes=[pltpu.VMEM(*shape) for shape in scratch]
+        + [
+            pltpu.SemaphoreType.DMA((128,)),
+            pltpu.SemaphoreType.DMA((128,)),
+            pltpu.SemaphoreType.DMA((64,)),
+        ],
+        compiler_params=pltpu.CompilerParams(
+            collective_id=0, has_side_effects=True, vmem_limit_bytes=48 * 2**20
+        ),
+        name="forward",
+    )(table, targets, sources, tokens, encoder, cotangent, qkv, out, cq, ckv, co, up, gain, bias)
+    return dict(zip(shapes, made))
+
+
 def gather_seq(rows):
     return lax.all_gather(rows, "seq", axis=0, tiled=True)
 
@@ -824,19 +1423,11 @@
     ).reshape(-1)
     own_positions = lax.dynamic_slice_in_dim(all_positions, ctx_index * rows, rows, 0)
     valid_rows = (own_positions < target_lengths[0])[:, None]
-    targets, sources = gather_seq(target_lengths), gather_seq(source_lengths)
     my_slot = ctx_index // groups
-    my_length = lax.dynamic_slice_in_dim(targets, my_slot, 1, 0)
-
-    w_qkv, w_cq, w_ckv = columns_of(self_qkv, 3), columns_of(cross_q, 1), columns_of(cross_kv, 2)
-    w_up = columns_of(mlp_up, 1)
 
     inputs = tokens[0].astype(F32)
-    hat_one, inverse_one, first_own = norm_forward(inputs, norm_gain[0], norm_bias[0])
-    first_low = gather_seq(first_own)
-    source_low = gather_seq(encoder_states[0])
+    hat_one, inverse_one, _ = norm_forward(inputs, norm_gain[0], norm_bias[0])
     grad_rows = jnp.where(valid_rows, cotangent[0].astype(F32), 0.0)
-    mlp_branch = gather_seq(grad_rows.astype(BF16))
 
     def to_heads(blocks, parts):
         blocks = blocks.reshape(seq_count, rows, parts, groups, pair_width)
@@ -851,28 +1442,33 @@
         taken = taken.reshape(seq_count, groups, parts, rows, pair_width).transpose(0, 3, 2, 1, 4)
         return taken.reshape(seq_count * rows, parts * own_width)
 
-    projected = dot(first_low, w_qkv).astype(BF16)
-    qkv = to_heads(projected, 3)
-    self_mix, self_peak = self_forward(qkv, all_positions, my_length)
-    self_low = to_rows(self_mix[None])
-
-    source_kv = dot(source_low, w_ckv).astype(BF16)
-    cross_kvs = lax.all_gather(source_kv, "ctx", axis=0, tiled=True)
-    cross_kvs = (
-        cross_kvs.reshape(ctx_count, seq_count, source_rows, 2 * own_width)
-        .transpose(1, 0, 2, 3)
-        .reshape(seq_count, ctx_count * source_rows, 2 * own_width)
-    )
-
-    first_sum = inputs + scatter_seq(dot(self_low, self_out))
-    hat_two, inverse_two, second_own = norm_forward(first_sum, norm_gain[1], norm_bias[1])
-    second_low = gather_seq(second_own)
-    cross_query = dot(second_low, w_cq).astype(BF16).reshape(seq_count, rows, own_width)
-    cross_mix, cross_peak = cross_forward(cross_query, cross_kvs, own_positions, targets, sources)
-    cross_low = cross_mix.reshape(seq_count * rows, own_width)
-    second_sum = first_sum + scatter_seq(dot(cross_low, cross_out))
-    hat_three, inverse_three, third_own = norm_forward(second_sum, norm_gain[2], norm_bias[2])
-    third_low = gather_seq(third_own)
+    kept = forward_call(
+        block_table,
+        target_lengths,
+        source_lengths,
+        tokens,
+        encoder_states,
+        cotangent,
+        self_qkv,
+        self_out,
+        cross_q,
+        cross_kv,
+        cross_out,
+        mlp_up,
+        norm_gain,
+        norm_bias,
+    )
+    first_low, second_low, third_low = kept["first"], kept["second"], kept["third"]
+    mlp_branch, source_low = kept["branch"], kept["source"]
+    w_qkv, w_cq, w_ckv, w_up = kept["w_qkv"], kept["w_cq"], kept["w_ckv"], kept["w_up"]
+    qkv, self_low, cross_kvs, cross_low = kept["heads"], kept["mix"], kept["kvs"], kept["cross"]
+    cross_query = kept["query"].reshape(seq_count, rows, own_width)
+    first_sum, second_sum = kept["sums"][0], kept["sums"][1]
+    self_peak, cross_peak = kept["peak"], kept["peak"][2:]
+    targets, sources = kept["lens"][:, 0, 0], kept["lens"][:, 4, 0]
+    my_length = lax.dynamic_slice_in_dim(targets, my_slot, 1, 0)
+    hat_two, inverse_two, _ = norm_forward(first_sum, norm_gain[1], norm_bias[1])
+    hat_three, inverse_three, _ = norm_forward(second_sum, norm_gain[2], norm_bias[2])
 
     hidden_pre = dot(third_low, w_up)
     hidden_act, gelu_back = jax.vjp(jax.nn.gelu, hidden_pre)

time: 1070 us -> 924 us (0.86)
  waiting for transfers between devices: 636 us -> 533 us
  Pallas kernels: 33.9 us -> 125 us
  blocking collectives: 153 us -> 102 us
  local copies, waits for them, and re-layouts: 59.9 us -> 31.7 us
  starting transfers between devices: 46.4 us -> 27.8 us
  matrix products: 67.3 us -> 48.7 us
    pallas_call x2 -> x1, Pallas kernels: 12.4 us -> 104 us  [forward_call(): pl.pallas_call(forward_kernel, in_specs=[smem] * 3 + [vmem] * 3 + [any_sp...]
    all_to_all x9 -> x5, waiting for transfers between devices: 67 us -> 14.6 us  [swap(): return lax.all_to_all(blocks, axis, split_axis=0, concat_axis=0, tiled=True)]
    all_to_all x3 -> x1, blocking collectives: 50 us -> 25.3 us  [swap(): return lax.all_to_all(blocks, axis, split_axis=0, concat_axis=0, tiled=True)]
    reduce_scatter x7 -> x5, waiting for transfers between devices: 129 us -> 107 us  [scatter_seq(): lax.psum_scatter(partial.astype(BF16), 'seq', scatter_dimension=0, tiled=...]
    all_gather x1 -> x0, blocking collectives: 20.6 us -> none  [gather_seq(): return lax.all_gather(rows, 'seq', axis=0, tiled=True)]
    all_gather x6 -> x2, waiting for transfers between devices: 46.2 us -> 25.7 us  [gather_seq(): return lax.all_gather(rows, 'seq', axis=0, tiled=True)]
    dot_general x21 -> x16, matrix products: 67.3 us -> 48.7 us  [dot(): lax.dot_general(left, right, (contract, ((), ())), preferred_element_type...]
    all_to_all x9 -> x5, starting transfers between devices: 45 us -> 26.7 us  [swap(): return lax.all_to_all(blocks, axis, split_axis=0, concat_axis=0, tiled=True)]
  transfers between devices with their start and end apart: 31 -> 20, of which waited for: 22 -> 17; matrix products, arithmetic and copies ran while one was open for 12% -> 8% of each run, Pallas kernels for 1% -> 1%
where the time goes in v2:
time: 924 us; the launch traced here: 911 us
  waiting for transfers between devices  533 us (58%)
  Pallas kernels  125 us (14%)
  blocking collectives  102 us (11%)
  matrix products  48.7 us (5%)
  local copies, waits for them, and re-layouts  31.7 us (3%)
  starting transfers between devices  27.8 us (3%)
  other arithmetic  26.6 us (3%)
  between operations  16.1 us (2%)
    reduce_scatter x3, waiting for transfers between devices, finish_rows(): lax.psum_scatter(grad.astype(BF16), 'ctx', scatter_dimension=0, tiled=True)  210 us
    reduce_scatter x4, waiting for transfers between devices, finish_columns(): lax.psum_scatter(blocks.reshape(ctx_count * seq_count * share, columns),...  118 us
    reduce_scatter x5, waiting for transfers between devices, scatter_seq(): lax.psum_scatter(partial.astype(BF16), 'seq', scatter_dimension=0, tiled=...  107 us
    pallas_call x1, Pallas kernels, forward_call(): pl.pallas_call(forward_kernel, in_specs=[smem] * 3 + [vmem] * 3 + [any_sp...  104 us
    reduce_scatter x1, waiting for transfers between devices, fast_device(): lax.psum_scatter(dkv, 'ctx', scatter_dimension=0, tiled=True)  57.6 us
    dot_general x16, matrix products, dot(): lax.dot_general(left, right, (contract, ((), ())), preferred_element_type...  48.7 us
    psum x1, blocking collectives, fast_device(): norm_sum = lax.psum(norm_terms, ('seq', 'ctx'))  38.6 us
    pmax x1, blocking collectives, fast_device(): peaks = lax.pmax(jnp.stack([peak_self, peak_cross]), ('seq', 'ctx'))  38.3 us
  transfers between devices with their start and end apart: 20, of which 17 were waited for; matrix products, arithmetic and copies ran while one was open for 8% of the time, Pallas kernels for 1%

profile of v2, /device:TPU:29, one launch (start us, length us, event | category | flops | bytes accessed | tf_op | source)
XLA Modules:
  0.0 911.1 jit_solution(8233912257694525218)
XLA Ops:
  16.6 103.6 %forward.1 = (bf16[512,1024]{1,0:T(8,128)(2,1)S(1)}, bf16[512,1024]{1,0:T(8,128)(2,1)}, bf16[512,1024]{1,0:T(8,128)(2,1)}, bf16[512,1024]{1,0:T(8,128)(2,1)}, bf...) custom-call(s32[8,2]{1,0:T(8,128)S(1)} %copy.47.table_ref, ...), custom_call_target="tpu_custom_call" | custom-call | tf_op jit(solution)/shard_map/forward/pallas_call | solution.py:1329
  120.3 4.3 fusion.52
  124.7 6.3 fusion.6
  132.3 3.4 convolution_convert_fusion.6
  135.8 7.1 convolution_convert_fusion.7
  143.3 1.6 slice_reduce_fusion
  146.3 14.2 %reduce-scatter.16.cloned.1.call-done = bf16[128,1024]{1,0:T(8,128)(2,1)} async-done(((bf16[512,1024]{1,0:T(8,128)(2,1)}), bf16[128,1024]{1,0:T(8,128)(2,1)}) %reduce-scatter.16.cloned.1.call-update) | async-done | bytes 262160 | tf_op jit(solution)/shard_map/reduce_scatter | solution.py:1356
  160.5 1.7 fusion.36
  162.2 26.5 %reduce-scatter.14.cloned.1.call-done = bf16[128,1024]{1,0:T(8,128)(2,1)} async-done(((bf16[512,1024]{1,0:T(8,128)(2,1)}), bf16[128,1024]{1,0:T(8,128)(2,1)}) %reduce-scatter.14.cloned.1.call-update) | async-done | bytes 262160 | tf_op jit(solution)/shard_map/reduce_scatter | solution.py:1356
  188.7 2.5 fusion.47
  191.6 16.9 %all-gather.3.cloned.1.call-done = bf16[512,1024]{1,0:T(8,128)(2,1)} async-done(((bf16[128,1024]{1,0:T(8,128)(2,1)}), bf16[512,1024]{1,0:T(8,128)(2,1)}) %all-gather.3.cloned.1.call-update) | async-done | bytes 1048592 | tf_op jit(solution)/shard_map/all_gather | solution.py:1352
  208.5 1.7 convolution_convert_fusion.13
  211.1 9.3 %cross_backward.1 = (bf16[4,128,256]{2,1,0:T(8,128)(2,1)S(1)}, bf16[4,256,512]{2,1,0:T(8,128)(2,1)S(1)}) custom-call(s32[4]{0:T(128)S(1)} %get-tuple-element.83.limit_ref, bf16[4,128,256]{2,1,0:T(8,128)(2,1)S(1)} %bitcast.186, bf16[4,256,512]{2,1,0:T(8,128)(2,1)S(1)} %copy-done.6, bf16[4,128,256]{2,1,0:T(8,128)(2,1)S(1)} %bitcast.188), custom_call_target="tpu_custom_call" | custom-call | tf_op jit(solution)/shard_map/cross_backward/pallas_call | solution.py:730
  223.9 23.5 %reduce-scatter.18.cloned.1.call-done = bf16[128,1024]{1,0:T(8,128)(2,1)} async-done(((bf16[512,1024]{1,0:T(8,128)(2,1)}), bf16[128,1024]{1,0:T(8,128)(2,1)}) %reduce-scatter.18.cloned.1.call-update) | async-done | bytes 262160 | tf_op jit(solution)/shard_map/reduce_scatter | solution.py:1356
  248.6 2.2 fusion.45
  250.9 1.8 convolution_convert_fusion.9
  253.7 57.6 %reduce-scatter.22.cloned.1.call-done = bf16[128,512]{1,0:T(8,128)(2,1)} async-done(((bf16[1024,512]{1,0:T(8,128)(2,1)}), bf16[128,512]{1,0:T(8,128)(2,1)}) %reduce-scatter.22.cloned.1.call-update) | async-done | bytes 131088 | tf_op jit(solution)/shard_map/reduce_scatter | solution.py:1511
  315.1 4.3 convolution_convert_fusion.1
  319.5 2.3 copy.60
  324.3 8.8 all-gather.5.cloned.1.call-done
  333.1 2.5 convolution_convert_fusion.10
  335.7 7.1 convolution_convert_fusion
  345.5 5.4 all-to-all-start
  352.5 7.3 all-to-all-done
  359.8 12.1 %self_backward.1 = (bf16[1024,128]{1,0:T(8,128)(2,1)S(1)}, bf16[2,1024,128]{2,1,0:T(8,128)(2,1)S(1)}) custom-call(s32[1]{0:T(128)} %bitcast.10.length_ref, s32[1024,1]{1,0:T(8,128)S(1)} %add.157.row_ref, s32[1,1024]{1,0:T(1,128)S(1)} %add.148.col_ref, bf16[1,1024,128]{2,1,0:T(8,128)(2,1)S(1)} %slice.72.q_ref, bf16[2,1024,128]{2,1,0:T(8,128)(2,1)S(1)} %slice.73.kv_ref, ...), custom_call_target="tpu_custom_call" | custom-call | tf_op jit(solution)/shard_map/self_backward/pallas_call | solution.py:627
  372.0 25.3 %all_to_all.30 = bf16[8,384,128]{2,1,0:T(8,128)(2,1)S(1)} all-to-all(bf16[8,384,128]{2,1,0:T(8,128)(2,1)S(1)} %bitcast.196), channel_id=1, replica_groups=mesh['seq'=4,'ctx'=8] {'ctx'}, dimensions={0} | all-to-all | bytes 1572864 | tf_op jit(solution)/shard_map/all_to_all | solution.py:1362
  398.4 3.4 convolution_convert_fusion.4
  402.7 38.3 %pmax.7 = f32[2,16]{1,0:T(2,128)S(1)} all-reduce(f32[2,16]{1,0:T(2,128)S(1)} %pad_maximum_fusion.3), channel_id=1, replica_groups=mesh['seq'=4,'ctx'=8] {'seq','ctx'}, use_global_device_ids=true, to_apply=%region_32.33 | all-reduce | flops 32 | bytes 256 | tf_op jit(solution)/shard_map/pmax | solution.py:1488
  444.2 2.0 convert_element_type.196
  446.8 1.8 fusion.8
  450.0 5.9 all-to-all-start.3
  456.1 3.4 all-to-all-done.3
  459.6 3.1 reduce-scatter.32.cloned.1.call-done
  462.7 5.7 all-to-all-start.4
  468.4 58.7 %reduce-scatter.34.cloned.1.call-done = bf16[32,1024]{1,0:T(8,128)(2,1)} async-done(((bf16[256,1024]{1,0:T(8,128)(2,1)}), bf16[32,1024]{1,0:T(8,128)(2,1)}) %reduce-scatter.34.cloned.1.call-update) | async-done | bytes 65552 | tf_op jit(solution)/shard_map/reduce_scatter | solution.py:1376
  528.6 92.1 %reduce-scatter.36.cloned.1.call-done = bf16[128,2048]{1,0:T(8,128)(2,1)} async-done(((bf16[1024,2048]{1,0:T(8,128)(2,1)}), bf16[128,2048]{1,0:T(8,128)(2,1)}) %reduce-scatter.36.cloned.1.call-update) | async-done | bytes 524304 | tf_op jit(solution)/shard_map/reduce_scatter | solution.py:1384
  620.7 4.1 all-to-all-start.5
  625.6 18.9 %reduce-scatter.24.cloned.1.call-done = bf16[32,1024]{1,0:T(8,128)(2,1)} async-done(((bf16[128,1024]{1,0:T(8,128)(2,1)}), bf16[32,1024]{1,0:T(8,128)(2,1)}) %reduce-scatter.24.cloned.1.call-update) | async-done | bytes 65552 | tf_op jit(solution)/shard_map/reduce_scatter | solution.py:1356
  647.2 59.3 %reduce-scatter.28.cloned.1.call-done = bf16[32,1024]{1,0:T(8,128)(2,1)} async-done(((bf16[256,1024]{1,0:T(8,128)(2,1)}), bf16[32,1024]{1,0:T(8,128)(2,1)}) %reduce-scatter.28.cloned.1.call-update) | async-done | bytes 65552 | tf_op jit(solution)/shard_map/reduce_scatter | solution.py:1376
  708.0 91.9 %reduce-scatter.38.cloned.1.call-done = bf16[256,1024]{1,0:T(8,128)(2,1)} async-done(((bf16[2048,1024]{1,0:T(8,128)(2,1)}), bf16[256,1024]{1,0:T(8,128)(2,1)}) %reduce-scatter.38.cloned.1.call-update) | async-done | bytes 524304 | tf_op jit(solution)/shard_map/reduce_scatter | solution.py:1376
  799.8 2.1 convert_element_type.195
  802.8 1.6 copy.63
  804.3 23.7 %reduce-scatter.20.cloned.1.call-done = bf16[128,1024]{1,0:T(8,128)(2,1)} async-done(((bf16[512,1024]{1,0:T(8,128)(2,1)}), bf16[128,1024]{1,0:T(8,128)(2,1)}) %reduce-scatter.20.cloned.1.call-update) | async-done | bytes 262160 | tf_op jit(solution)/shard_map/reduce_scatter | solution.py:1356
  829.3 38.6 %psum.7 = f32[6,1024]{1,0:T(8,128)S(1)} all-reduce(f32[6,1024]{1,0:T(8,128)S(1)} %stack.38), channel_id=1, replica_groups=mesh['seq'=4,'ctx'=8] {'seq','ctx'}, use_global_device_ids=true, to_apply=%region_31.32 | all-reduce | flops 6144 | bytes 49152 | tf_op jit(solution)/shard_map/psum | solution.py:1530
  868.0 2.0 fusion.25
  870.0 22.9 %reduce-scatter.26.cloned.1.call-done = bf16[128,768]{1,0:T(8,128)(2,1)} async-done(((bf16[1024,768]{1,0:T(8,128)(2,1)}), bf16[128,768]{1,0:T(8,128)(2,1)}) %reduce-scatter.26.cloned.1.call-update) | async-done | bytes 196624 | tf_op jit(solution)/shard_map/reduce_scatter | solution.py:1384
  892.9 5.5 all-to-all-start.2
  899.1 3.9 all-to-all-done.2
  (195 shorter events, 46.7 us)
Async XLA Ops:
  7.2 153.3 %reduce-scatter.16.cloned.1.call-start = ((), (), s32[]{:S(2)}) async-start(), calls=%async_computation.20 | async-start | bytes 1310720 | tf_op jit(solution)/shard_map/reduce_scatter | solution.py:1356
  16.6 103.7 %copy-start.38 = (bf16[2048,1024]{1,0:T(8,128)(2,1)S(1)}, bf16[2048,1024]{1,0:T(8,128)(2,1)}, u32[]{:S(2)}) copy-start(bf16[2048,1024]{1,0:T(8,128)(2,1)} %param.28) | copy-start | bytes 12582916
  120.2 4.4 copy-start.11
  120.3 4.4 copy-start.13
  120.3 4.4 copy-start.17
  120.3 4.4 copy-start.19
  120.3 4.4 copy-start.25
  120.3 4.4 copy-start.39
  120.3 4.4 copy-start.41
  135.7 53.0 %reduce-scatter.14.cloned.1.call-start = ((), (), s32[]{:S(2)}) async-start(), calls=%async_computation.19 | async-start | bytes 1310720 | tf_op jit(solution)/shard_map/reduce_scatter | solution.py:1356
  135.8 7.2 copy-start.35
  135.8 10.5 %copy-start.23 = (f32[3,1024]{1,0:T(4,128)S(1)}, f32[3,1024]{1,0:T(4,128)}, u32[]{:S(2)}) copy-start(f32[3,1024]{1,0:T(4,128)} %gain_ref.1) | copy-start | bytes 36868
  142.9 45.8 %copy-start.5 = (bf16[1,128,1024]{2,1,0:T(8,128)(2,1)S(1)}, bf16[1,128,1024]{2,1,0:T(8,128)(2,1)}, u32[]{:S(2)}) copy-start(bf16[1,128,1024]{2,1,0:T(8,128)(2,1)} %cotangent_ref.1) | copy-start | bytes 786436
  142.9 65.6 %copy-start.8 = (bf16[256,1024]{1,0:T(8,128)(2,1)S(1)}, bf16[256,1024]{1,0:T(8,128)(2,1)}, u32[]{:S(2)}) copy-start(bf16[256,1024]{1,0:T(8,128)(2,1)} %co_ref.1) | copy-start | bytes 1572868
  142.9 67.3 %copy-start.6 = (bf16[4,256,512]{2,1,0:T(8,128)(2,1)S(1)}, bf16[4,256,512]{2,1,0:T(8,128)(2,1)}, u32[]{:S(2)}) copy-start(bf16[4,256,512]{2,1,0:T(8,128)(2,1)} %get-tuple-element.42.kv_ref) | copy-start | bytes 3145732
  142.9 65.5 %all-gather.3.cloned.1.call-start = ((), (), s32[]{:S(2)}) async-start(), calls=%async_computation.21 | async-start | bytes 1310720 | tf_op jit(solution)/shard_map/all_gather | solution.py:1352
  191.2 56.1 %reduce-scatter.18.cloned.1.call-start = ((), (), s32[]{:S(2)}) async-start(), calls=%async_computation.22 | async-start | bytes 1310720 | tf_op jit(solution)/shard_map/reduce_scatter | solution.py:1356
  220.5 26.8 %copy-start.27 = (f32[2,128,1024]{2,1,0:T(8,128)S(1)}, f32[2,128,1024]{2,1,0:T(8,128)}, u32[]{:S(2)}) copy-start(f32[2,128,1024]{2,1,0:T(8,128)} %get-tuple-element.36) | copy-start | bytes 3145732
  222.6 28.3 %copy-start.16 = (bf16[4,128,256]{2,1,0:T(8,128)(2,1)S(1)}, bf16[4,128,256]{2,1,0:T(8,128)(2,1)}, u32[]{:S(2)}) copy-start(bf16[4,128,256]{2,1,0:T(8,128)(2,1)} %copy-done.15) | copy-start | bytes 786436
  222.6 88.6 %reduce-scatter.22.cloned.1.call-start = ((), (), s32[]{:S(2)}) async-start(), calls=%async_computation.25 | async-start | bytes 1179648 | tf_op jit(solution)/shard_map/reduce_scatter | solution.py:1511
  223.8 87.5 %copy-start.18 = (bf16[128,1024]{1,0:T(8,128)(2,1)S(1)}, bf16[128,1024]{1,0:T(8,128)(2,1)}, u32[]{:S(2)}) copy-start(bf16[128,1024]{1,0:T(8,128)(2,1)} %copy-done.17) | copy-start | bytes 786436
  223.8 109.3 %all-gather.5.cloned.1.call-start = ((), (), s32[]{:S(2)}) async-start(), calls=%async_computation.23 | async-start | bytes 1310720 | tf_op jit(solution)/shard_map/all_gather | solution.py:1352
  250.9 199.1 %reduce-scatter.30.cloned.1.call-start = ((), (), s32[]{:S(2)}) async-start(), calls=%async_computation.29 | async-start | bytes 589824 | tf_op jit(solution)/shard_map/reduce_scatter | solution.py:1384
  250.9 62.9 %copy-start.14 = (bf16[512,256]{1,0:T(8,128)(2,1)S(1)}, bf16[512,256]{1,0:T(8,128)(2,1)}, u32[]{:S(2)}) copy-start(bf16[512,256]{1,0:T(8,128)(2,1)} %copy-done.13) | copy-start | bytes 786436
  250.9 62.9 %copy-start.31 = (bf16[512,1024]{1,0:T(8,128)(2,1)S(1)}, bf16[512,1024]{1,0:T(8,128)(2,1)}, u32[]{:S(2)}) copy-start(bf16[512,1024]{1,0:T(8,128)(2,1)} %all-gather.3.cloned.1.call-done) | copy-start | bytes 3145732
  253.6 209.1 %reduce-scatter.32.cloned.1.call-start = ((), (), s32[]{:S(2)}) async-start(), calls=%async_computation.30 | async-start | bytes 1179648 | tf_op jit(solution)/shard_map/reduce_scatter | solution.py:1384
  313.7 213.3 %reduce-scatter.34.cloned.1.call-start = ((), (), s32[]{:S(2)}) async-start(), calls=%async_computation.31 | async-start | bytes 589824 | tf_op jit(solution)/shard_map/reduce_scatter | solution.py:1376
  315.1 305.6 %reduce-scatter.36.cloned.1.call-start = ((), (), s32[]{:S(2)}) async-start(), calls=%async_computation.32 | async-start | bytes 4718592 | tf_op jit(solution)/shard_map/reduce_scatter | solution.py:1384
  321.7 11.3 %copy-start.12 = (bf16[512,256]{1,0:T(8,128)(2,1)S(1)}, bf16[512,256]{1,0:T(8,128)(2,1)}, u32[]{:S(2)}) copy-start(bf16[512,256]{1,0:T(8,128)(2,1)} %copy-done.11) | copy-start | bytes 786436
  321.8 13.9 %copy-start.40 = (bf16[512,1024]{1,0:T(8,128)(2,1)S(1)}, bf16[512,1024]{1,0:T(8,128)(2,1)}, u32[]{:S(2)}) copy-start(bf16[512,1024]{1,0:T(8,128)(2,1)} %get-tuple-element.39) | copy-start | bytes 3145732
  321.8 322.7 %reduce-scatter.24.cloned.1.call-start = ((), (), s32[]{:S(2)}) async-start(), calls=%async_computation.26 | async-start | bytes 327680 | tf_op jit(solution)/shard_map/reduce_scatter | solution.py:1356
  324.2 382.3 %reduce-scatter.28.cloned.1.call-start = ((), (), s32[]{:S(2)}) async-start(), calls=%async_computation.28 | async-start | bytes 589824 | tf_op jit(solution)/shard_map/reduce_scatter | solution.py:1376
  335.6 464.2 %reduce-scatter.38.cloned.1.call-start = ((), (), s32[]{:S(2)}) async-start(), calls=%async_computation.33 | async-start | bytes 4718592 | tf_op jit(solution)/shard_map/reduce_scatter | solution.py:1376
  345.5 14.3 %all-to-all-start = ((bf16[8,128,128]{2,1,0:T(8,128)(2,1)}), bf16[8,128,128]{2,1,0:T(8,128)(2,1)S(1)}, u32[]{:S(2)}, u32[]{:S(2)}) async-start(bf16[8,128,128]{2,1,0:T(8,128)(2,1)} %bitcast.12), calls=%async_computation.3 | async-start | bytes 524288 | tf_op jit(solution)/shard_map/all_to_all | solution.py:1362
  350.9 477.1 %reduce-scatter.20.cloned.1.call-start = ((), (), s32[]{:S(2)}) async-start(), calls=%async_computation.24 | async-start | bytes 1310720 | tf_op jit(solution)/shard_map/reduce_scatter | solution.py:1356
  398.0 43.0 %copy-start.1 = (bf16[1,128,1024]{2,1,0:T(8,128)(2,1)S(1)}, bf16[1,128,1024]{2,1,0:T(8,128)(2,1)}, u32[]{:S(2)}) copy-start(bf16[1,128,1024]{2,1,0:T(8,128)(2,1)} %tokens_ref.1) | copy-start | bytes 786436
  398.0 43.1 %copy-start.37 = (f32[2,16]{1,0:T(2,128)S(1)}, f32[2,16]{1,0:T(2,128)}, u32[]{:S(2)}) copy-start(f32[2,16]{1,0:T(2,128)} %param.31) | copy-start | bytes 388
  398.1 43.1 %copy-start.26 = (bf16[512,1024]{1,0:T(8,128)(2,1)S(1)}, bf16[512,1024]{1,0:T(8,128)(2,1)}, u32[]{:S(2)}) copy-start(bf16[512,1024]{1,0:T(8,128)(2,1)} %copy-done.25) | copy-start | bytes 3145732
  401.9 491.0 %reduce-scatter.26.cloned.1.call-start = ((), (), s32[]{:S(2)}) async-start(), calls=%async_computation.27 | async-start | bytes 1769472 | tf_op jit(solution)/shard_map/reduce_scatter | solution.py:1384
  441.0 2.5 copy-start.36
  442.2 2.0 copy-start.28
  442.2 4.3 copy-start.3
  442.3 4.3 copy-start.29
  450.0 9.6 %all-to-all-start.3 = ((bf16[4,32,256]{2,1,0:T(8,128)(2,1)}), bf16[4,32,256]{2,1,0:T(8,128)(2,1)S(1)}, u32[]{:S(2)}, u32[]{:S(2)}) async-start(bf16[4,32,256]{2,1,0:T(8,128)(2,1)} %bitcast.211), calls=%async_computation.12 | async-start | bytes 131072 | tf_op jit(solution)/shard_map/all_to_all | solution.py:1362
  462.7 65.9 %all-to-all-start.4 = ((bf16[4,32,512]{2,1,0:T(8,128)(2,1)}), bf16[4,32,512]{2,1,0:T(8,128)(2,1)S(1)}, u32[]{:S(2)}, u32[]{:S(2)}) async-start(bf16[4,32,512]{2,1,0:T(8,128)(2,1)} %bitcast.209), calls=%async_computation.14 | async-start | bytes 262144 | tf_op jit(solution)/shard_map/all_to_all | solution.py:1362
  620.7 181.2 %all-to-all-start.5 = ((bf16[4,32,2048]{2,1,0:T(8,128)(2,1)}), bf16[4,32,2048]{2,1,0:T(8,128)(2,1)S(1)}, u32[]{:S(2)}, u32[]{:S(2)}) async-start(bf16[4,32,2048]{2,1,0:T(8,128)(2,1)} %bitcast.205), calls=%async_computation.17 | async-start | bytes 1048576 | tf_op jit(solution)/shard_map/all_to_all | solution.py:1362
  647.2 220.9 %copy-start.30 = (f32[128,1024]{1,0:T(8,128)S(1)}, f32[128,1024]{1,0:T(8,128)}, u32[]{:S(2)}) copy-start(f32[128,1024]{1,0:T(8,128)} %get-tuple-element.73) | copy-start | bytes 1572868
  892.9 10.0 %all-to-all-start.2 = ((bf16[4,32,768]{2,1,0:T(8,128)(2,1)}), bf16[4,32,768]{2,1,0:T(8,128)(2,1)S(1)}, u32[]{:S(2)}, u32[]{:S(2)}) async-start(bf16[4,32,768]{2,1,0:T(8,128)(2,1)} %bitcast.208), calls=%async_computation.9 | async-start | bytes 393216 | tf_op jit(solution)/shard_map/all_to_all | solution.py:1362
  (15 other events, 15.3 us)
Sparse Core Ops, SparseCore 0:
  135.8 24.5 reduce-scatter.15
  163.7 24.8 reduce-scatter.13
  191.3 17.1 all-gather.2
  222.8 24.5 reduce-scatter.17
  251.5 59.6 reduce-scatter.21
  313.3 19.7 all-gather.4
  336.4 59.4 reduce-scatter.29
  400.3 62.3 reduce-scatter.31
  466.0 61.0 reduce-scatter.33
  531.0 89.6 reduce-scatter.35
  623.8 20.6 reduce-scatter.23
  648.0 58.4 reduce-scatter.27
  710.1 89.6 reduce-scatter.37
  802.4 25.5 reduce-scatter.19
  831.3 61.6 reduce-scatter.25

commit v3 on v2

--- a/solution.py
+++ b/solution.py
@@ -537,216 +537,6 @@
         jnp.sum(grad * hat, axis=0),
         jnp.sum(grad, axis=0),
     )
-
-
-def self_forward_kernel(length_ref, row_ref, col_ref, q_ref, kv_ref, mix_ref, peak_ref):
-    length = length_ref[0]
-    row_pos = row_ref[...]
-    col_pos = col_ref[...]
-    allowed = (col_pos <= row_pos) & (col_pos < length)
-    valid = row_pos < length
-
-    @pl.when(pl.program_id(0) == 0)
-    def _():
-        peak_ref[...] = jnp.full_like(peak_ref, masked_score)
-
-    for head in range(q_ref.shape[-1] // HD):
-        cut = slice(head * HD, (head + 1) * HD)
-        scores = dot(q_ref[0, :, cut], kv_ref[0, :, cut], NT) * SCALE
-        scores = jnp.where(allowed, scores, masked_score)
-        top = jnp.max(scores, axis=-1, keepdims=True)
-        expos = jnp.exp(scores - top)
-        probs = expos * (1.0 / jnp.sum(expos, axis=-1, keepdims=True))
-        mix_ref[:, cut] = dot(probs.astype(BF16), kv_ref[1, :, cut]).astype(BF16)
-        peak = jnp.max(jnp.where(valid, top, masked_score), axis=0, keepdims=True)
-        peak_ref[head : head + 1, :] = jnp.maximum(
-            peak_ref[head : head + 1, :], jnp.broadcast_to(peak, (1, 128))
-        )
-
-
-def self_forward(qkv, positions, length):
-    count, width = qkv.shape[1:]
-    step = min(256, count)
-    return pl.pallas_call(
-        self_forward_kernel,
-        grid=(count // step,),
-        in_specs=[
-            pl.BlockSpec(memory_space=pltpu.SMEM),
-            pl.BlockSpec((step, 1), lambda i: (i, 0)),
-            pl.BlockSpec((1, count), lambda i: (0, 0)),
-            pl.BlockSpec((1, step, width), lambda i: (0, i, 0)),
-            pl.BlockSpec((2, count, width), lambda i: (0, 0, 0)),
-        ],
-        out_specs=[
-            pl.BlockSpec((step, width), lambda i: (i, 0)),
-            pl.BlockSpec((8, 128), lambda i: (0, 0)),
-        ],
-        out_shape=[
-            jax.ShapeDtypeStruct((count, width), BF16),
-            jax.ShapeDtypeStruct((8, 128), F32),
-        ],
-        compiler_params=pltpu.CompilerParams(vmem_limit_bytes=48 * 2**20),
-        name="self_forward",
-    )(length, positions[:, None], positions[None, :], qkv[0][None], qkv[1:])
-
-
-def self_backward_kernel(length_ref, row_ref, col_ref, q_ref, kv_ref, g_ref, dq_ref, dkv_ref, acc):
-    length = length_ref[0]
-    row_pos = row_ref[...]
-    col_pos = col_ref[...]
-    allowed = (col_pos <= row_pos) & (col_pos < length)
-
-    @pl.when(pl.program_id(0) == 0)
-    def _():
-        acc[...] = jnp.zeros_like(acc)
-
-    for head in range(q_ref.shape[-1] // HD):
-        cut = slice(head * HD, (head + 1) * HD)
-        query, grad = q_ref[0, :, cut], g_ref[:, cut]
-        scores = dot(query, kv_ref[0, :, cut], NT) * SCALE
-        scores = jnp.where(allowed, scores, masked_score)
-        top = jnp.max(scores, axis=-1, keepdims=True)
-        expos = jnp.exp(scores - top)
-        probs = expos * (1.0 / jnp.sum(expos, axis=-1, keepdims=True))
-        dprobs = dot(grad, kv_ref[1, :, cut], NT)
-        delta = jnp.sum(probs * dprobs, axis=-1, keepdims=True)
-        dscores = (probs * (dprobs - delta)).astype(BF16)
-        dq_ref[:, cut] = (dot(dscores, kv_ref[0, :, cut]) * SCALE).astype(BF16)
-        acc[0, :, cut] += dot(dscores, query, TN)
-        acc[1, :, cut] += dot(probs.astype(BF16), grad, TN)
-
-    @pl.when(pl.program_id(0) == pl.num_programs(0) - 1)
-    def _():
-        dkv_ref[0] = (acc[0] * SCALE).astype(BF16)
-        dkv_ref[1] = acc[1].astype(BF16)
-
-
-def self_backward(qkv, positions, length, grad):
-    count, width = qkv.shape[1:]
-    step = min(256, count)
-    dq, dkv = pl.pallas_call(
-        self_backward_kernel,
-        grid=(count // step,),
-        in_specs=[
-            pl.BlockSpec(memory_space=pltpu.SMEM),
-            pl.BlockSpec((step, 1), lambda i: (i, 0)),
-            pl.BlockSpec((1, count), lambda i: (0, 0)),
-            pl.BlockSpec((1, step, width), lambda i: (0, i, 0)),
-            pl.BlockSpec((2, count, width), lambda i: (0, 0, 0)),
-            pl.BlockSpec((step, width), lambda i: (i, 0)),
-        ],
-        out_specs=[
-            pl.BlockSpec((step, width), lambda i: (i, 0)),
-            pl.BlockSpec((2, count, width), lambda i: (0, 0, 0)),
-        ],
-        out_shape=[
-            jax.ShapeDtypeStruct((count, width), BF16),
-            jax.ShapeDtypeStruct((2, count, width), BF16),
-        ],
-        scratch_shapes=[pltpu.VMEM((2, count, width), F32)],
-        compiler_params=pltpu.CompilerParams(vmem_limit_bytes=48 * 2**20),
-        name="self_backward",
-    )(length, positions[:, None], positions[None, :], qkv[0][None], qkv[1:], grad)
-    return jnp.concatenate([dq[None], dkv], axis=0)
-
-
-def cross_forward_kernel(limit_ref, target_ref, row_ref, q_ref, kv_ref, mix_ref, peak_ref):
-    slot = pl.program_id(0)
-    width = q_ref.shape[-1]
-    keys = kv_ref.shape[1]
-    live = lax.broadcasted_iota(jnp.int32, (1, keys), 1) < limit_ref[slot]
-    valid = row_ref[...] < target_ref[slot]
-
-    @pl.when(slot == 0)
-    def _():
-        peak_ref[...] = jnp.full_like(peak_ref, masked_score)
-
-    for head in range(width // HD):
-        cut = slice(head * HD, (head + 1) * HD)
-        vcut = slice(width + head * HD, width + (head + 1) * HD)
-        scores = dot(q_ref[0, :, cut], kv_ref[0, :, cut], NT) * SCALE
-        scores = jnp.where(live, scores, masked_score)
-        top = jnp.max(scores, axis=-1, keepdims=True)
-        expos = jnp.exp(scores - top)
-        probs = expos * (1.0 / jnp.sum(expos, axis=-1, keepdims=True))
-        mix_ref[0, :, cut] = dot(probs.astype(BF16), kv_ref[0, :, vcut]).astype(BF16)
-        peak = jnp.max(jnp.where(valid, top, masked_score), axis=0, keepdims=True)
-        peak_ref[head : head + 1, :] = jnp.maximum(
-            peak_ref[head : head + 1, :], jnp.broadcast_to(peak, (1, 128))
-        )
-
-
-def cross_forward(query, kv, own_positions, target_lengths, source_lengths):
-    slots, rows, width = query.shape
-    keys = kv.shape[1]
-    return pl.pallas_call(
-        cross_forward_kernel,
-        grid=(slots,),
-        in_specs=[
-            pl.BlockSpec(memory_space=pltpu.SMEM),
-            pl.BlockSpec(memory_space=pltpu.SMEM),
-            pl.BlockSpec((rows, 1), lambda i: (0, 0)),
-            pl.BlockSpec((1, rows, width), lambda i: (i, 0, 0)),
-            pl.BlockSpec((1, keys, 2 * width), lambda i: (i, 0, 0)),
-        ],
-        out_specs=[
-            pl.BlockSpec((1, rows, width), lambda i: (i, 0, 0)),
-            pl.BlockSpec((8, 128), lambda i: (0, 0)),
-        ],
-        out_shape=[
-            jax.ShapeDtypeStruct((slots, rows, width), BF16),
-            jax.ShapeDtypeStruct((8, 128), F32),
-        ],
-        compiler_params=pltpu.CompilerParams(vmem_limit_bytes=48 * 2**20),
-        name="cross_forward",
-    )(source_lengths, target_lengths, own_positions[:, None], query, kv)
-
-
-def cross_backward_kernel(limit_ref, q_ref, kv_ref, g_ref, dq_ref, dkv_ref):
-    slot = pl.program_id(0)
-    width = q_ref.shape[-1]
-    keys = kv_ref.shape[1]
-    live = lax.broadcasted_iota(jnp.int32, (1, keys), 1) < limit_ref[slot]
-    for head in range(width // HD):
-        cut = slice(head * HD, (head + 1) * HD)
-        vcut = slice(width + head * HD, width + (head + 1) * HD)
-        query, grad = q_ref[0, :, cut], g_ref[0, :, cut]
-        scores = dot(query, kv_ref[0, :, cut], NT) * SCALE
-        scores = jnp.where(live, scores, masked_score)
-        top = jnp.max(scores, axis=-1, keepdims=True)
-        expos = jnp.exp(scores - top)
-        probs = expos * (1.0 / jnp.sum(expos, axis=-1, keepdims=True))
-        dprobs = dot(grad, kv_ref[0, :, vcut], NT)
-        delta = jnp.sum(probs * dprobs, axis=-1, keepdims=True)
-        dscores = (probs * (dprobs - delta)).astype(BF16)
-        dq_ref[0, :, cut] = (dot(dscores, kv_ref[0, :, cut]) * SCALE).astype(BF16)
-        dkv_ref[0, :, cut] = (dot(dscores, query, TN) * SCALE).astype(BF16)
-        dkv_ref[0, :, vcut] = dot(probs.astype(BF16), grad, TN).astype(BF16)
-
-
-def cross_backward(query, kv, source_lengths, grad):
-    slots, rows, width = query.shape
-    keys = kv.shape[1]
-    return pl.pallas_call(
-        cross_backward_kernel,
-        grid=(slots,),
-        in_specs=[
-            pl.BlockSpec(memory_space=pltpu.SMEM),
-            pl.BlockSpec((1, rows, width), lambda i: (i, 0, 0)),
-            pl.BlockSpec((1, keys, 2 * width), lambda i: (i, 0, 0)),
-            pl.BlockSpec((1, rows, width), lambda i: (i, 0, 0)),
-        ],
-        out_specs=[
-            pl.BlockSpec((1, rows, width), lambda i: (i, 0, 0)),
-            pl.BlockSpec((1, keys, 2 * width), lambda i: (i, 0, 0)),
-        ],
-        out_shape=[
-            jax.ShapeDtypeStruct((slots, rows, width), BF16),
-            jax.ShapeDtypeStruct((slots, keys, 2 * width), BF16),
-        ],
-        compiler_params=pltpu.CompilerParams(vmem_limit_bytes=48 * 2**20),
-        name="cross_backward",
-    )(source_lengths, query, kv, grad)
 
 
 MESH = pl.DeviceIdType.MESH
@@ -1348,47 +1138,716 @@
     return dict(zip(shapes, made))
 
 
-def gather_seq(rows):
-    return lax.all_gather(rows, "seq", axis=0, tiled=True)
-
-
-def scatter_seq(partial):
-    return lax.psum_scatter(
-        partial.astype(BF16), "seq", scatter_dimension=0, tiled=True
-    ).astype(F32)
-
-
-def swap(blocks, axis):
-    return lax.all_to_all(blocks, axis, split_axis=0, concat_axis=0, tiled=True)
-
-
-def columns_of(weight, parts):
-    seq_count = lax.axis_size("seq")
-    rows, columns = weight.shape
-    width = columns // (parts * seq_count)
-    blocks = weight.reshape(rows, parts, seq_count, width).transpose(2, 0, 1, 3)
-    return swap(blocks.reshape(seq_count, rows, parts * width), "seq").reshape(
-        seq_count * rows, parts * width
-    )
-
-
-def finish_rows(grad):
-    return lax.psum_scatter(grad.astype(BF16), "ctx", scatter_dimension=0, tiled=True).astype(F32)
-
-
-def finish_columns(grad, parts):
-    seq_count, ctx_count = lax.axis_size("seq"), lax.axis_size("ctx")
-    rows, columns = grad.shape
-    share = rows // (seq_count * ctx_count)
-    blocks = grad.astype(BF16).reshape(seq_count, ctx_count, share, columns).transpose(1, 0, 2, 3)
-    own = lax.psum_scatter(
-        blocks.reshape(ctx_count * seq_count * share, columns),
-        "ctx",
-        scatter_dimension=0,
-        tiled=True,
-    ).reshape(seq_count, share, columns)
-    taken = swap(own, "seq").reshape(seq_count, share, parts, columns // parts)
-    return taken.transpose(1, 2, 0, 3).reshape(share, seq_count * columns).astype(F32)
+class Sum:
+    def __init__(self, links, place, full, into, away, result, lead=False, own=None):
+        self.links, self.place, self.full, self.own = links, place, full, own
+        self.into, self.away, self.result, self.lead = into, away, result, lead
+        self.base = links.slots(7)
+
+    def target(self, turn):
+        return lax.rem(self.place.z + 1 + turn, 4)
+
+    def start(self, turns=(0, 1, 2, 3)):
+        p = self.place
+        for turn in turns:
+            to = self.target(turn)
+            src = self.full.at[to, 1 - p.y] if self.lead else self.full.at[:, to, 1 - p.y]
+            self.links.push(self.base + turn, src, self.into.at[to], (p.s, p.pair))
+
+    def turn(self, turns=(0, 1, 2, 3)):
+        p, links, into = self.place, self.links, self.into
+        for turn in turns:
+            to = self.target(turn)
+            links.take(self.base + turn, into.at[to], (p.s, p.pair))
+
+            def add(a, carry):
+                if self.own is not None:
+                    mine = self.own[to, a] if self.lead else self.own[a, to]
+                else:
+                    mine = self.full[to, p.y, a] if self.lead else self.full[a, to, p.y]
+                into[to, a] = (mine.astype(F32) + into[to, a].astype(F32)).astype(BF16)
+                return carry
+
+            lax.fori_loop(0, into.shape[1], add, 0)
+            if turn < 3:
+                links.push(
+                    self.base + 4 + turn, into.at[to], self.away.at[turn], (p.s, to * 2 + p.y)
+                )
+
+    def finish(self):
+        p, links, into, away = self.place, self.links, self.into, self.away
+        for turn in range(3):
+            came = lax.rem(p.z + 3 - turn, 4) * 2 + p.y
+            links.take(self.base + 4 + turn, away.at[turn], (p.s, came))
+
+        def add(a, carry):
+            total = into[p.z, a].astype(F32) + away[0, a].astype(F32)
+            total = total + (away[1, a].astype(F32) + away[2, a].astype(F32))
+            self.result[a] = total.astype(BF16)
+            return carry
+
+        lax.fori_loop(0, into.shape[1], add, 0)
+
+
+class Exchange:
+    def __init__(self, links, place, result, taken):
+        self.links, self.place, self.result, self.taken = links, place, result, taken
+        self.base = links.slots(3)
+        self.others = (place.far, place.opp, place.sib)
+
+    def start(self):
+        p = self.place
+        for step, other in enumerate(self.others):
+            self.links.push(
+                self.base + step,
+                self.result.at[pl.ds(other, 1)],
+                self.taken.at[pl.ds(p.s, 1)],
+                (other, p.c),
+            )
+        self.taken[pl.ds(p.s, 1)] = self.result[pl.ds(p.s, 1)]
+
+    def finish(self):
+        for step, other in enumerate(self.others):
+            self.links.take(
+                self.base + step, self.taken.at[pl.ds(other, 1)], (other, self.place.c)
+            )
+
+
+def norm_terms_of(values):
+    centered = values - jnp.mean(values, axis=-1, keepdims=True)
+    spread = jnp.mean(centered * centered, axis=-1, keepdims=True)
+    inverse = lax.rsqrt(spread + norm_eps)
+    return centered * inverse, inverse
+
+
+def backward_body(r):
+    place, links = Place(), Links(r.send_sem, r.recv_sem, r.local_sem)
+    p = place
+    rows = r.tokens.shape[1]
+    half = rows // 2
+    width = r.w_cq.shape[1]
+    source_rows = r.source.shape[0] // 4
+    keys = r.kvs.shape[1]
+    pair_width = r.heads.shape[2]
+    held, groups = width // HD, width // pair_width
+    depth = r.first.shape[1]
+    step = rows // PIECES
+    share = depth // 4
+
+    loads = {}
+    for name in r.loaded:
+        loads[name] = pltpu.make_async_copy(
+            getattr(r, name + "_hbm"), getattr(r, name), r.load_sem.at[len(loads)]
+        )
+        loads[name].start()
+
+    def need(*wanted):
+        for name in wanted:
+            loads.pop(name).wait()
+
+    place.greet()
+    down = Sum(links, place, r.down_full, r.down_into, r.down_away, r.down_result, True, r.down_own)
+    up = Sum(links, place, r.up_full, r.up_into, r.up_away, r.up_result, False, r.up_own)
+    own_down = links.save(r.down_full.at[:, p.y], r.down_own)
+    own_up = links.save(r.up_full.at[:, :, p.y], r.up_own)
+    links.saves = []
+    for turn in (0, 1):
+        up.start((turn,))
+        down.start((turn,))
+
+    r.peaks_ctx[pl.ds(p.c, 1)] = r.peak[...][None]
+    peak_base = links.slots(STEPS)
+    own_peak = r.peaks_ctx.at[pl.ds(p.c, 1)]
+    for hop in range(1, STEPS):
+        links.push(peak_base + hop, own_peak, own_peak, (p.s, lax.rem(p.c + hop, STEPS)))
+
+    own_rows = row_positions(r.table, p.c, half)
+    r.norms[...] = jnp.zeros_like(r.norms)
+
+    def add_norms(index, gain, bias):
+        r.norms[index : index + 1] += gain[None]
+        r.norms[index + 3 : index + 4] += bias[None]
+
+    get_cross = Gather(links, place, r.cross_branch, rows, PIECES)
+
+    def after_third(piece, total):
+        cut = slice(piece * step, (piece + 1) * step)
+        hat, inverse = norm_terms_of(r.sums[1, cut])
+        back, gain, bias = norm_backward(total, hat, inverse, r.gain[2:3])
+        add_norms(2, gain, bias)
+        valid = own_rows[cut] < r.target[0]
+        value = jnp.where(valid, r.cotangent[0, cut].astype(F32), 0.0) + back
+        r.grad_sum[cut] = value
+        r.cross_branch[rows_at(p.s * rows + piece * step, step)] = value.astype(BF16)
+        get_cross.start(piece)
+
+    def stored(ref):
+        return lambda block, piece: ref[rows_at(block * rows + piece * step, step)].astype(F32)
+
+    need("sums")
+    Reduce(links, place, r.rs_out.at[0], r.rs_in.at[0], rows, PIECES).run(
+        stored(r.grad_third), after_third
+    )
+    for hop in range(1, STEPS):
+        other = lax.rem(p.c + STEPS - hop, STEPS)
+        links.take(peak_base + hop, r.peaks_ctx.at[pl.ds(other, 1)], (p.s, other))
+    best = []
+    for group in range(groups):
+        tile = r.peaks_ctx[group]
+        for owner in range(group + groups, STEPS, groups):
+            tile = jnp.maximum(tile, r.peaks_ctx[owner])
+        best.append(tile)
+    everyone = best[0]
+    for tile in best[1:]:
+        everyone = jnp.maximum(everyone, tile)
+    mine = jnp.concatenate([tile[0:2] for tile in best] + [everyone[2 : 2 + held]], axis=0)
+    r.peaks_seq[pl.ds(p.s, 1)] = mine[None]
+    peak_seq = links.slots(3)
+    own_peak = r.peaks_seq.at[pl.ds(p.s, 1)]
+    for hop, other in enumerate((p.far, p.opp, p.sib)):
+        links.push(peak_seq + hop, own_peak, own_peak, (other, p.c))
+
+    for piece in range(PIECES):
+        get_cross.forward(piece)
+    need("w_co", "cross", "query", "kvs", "w_cq", "second")
+    for piece in range(PIECES):
+        get_cross.finish(piece)
+
+    def cross_back(slot, carry):
+        at = rows_at(slot * rows, rows)
+        grad_rows = dot(r.cross_branch[at], r.w_co[...], NT).astype(BF16)
+        live = lax.broadcasted_iota(jnp.int32, (1, keys), 1) < r.lens[pl.ds(slot, 1)][0, 4:5, 0:1]
+        for head in range(held):
+            cut = slice(head * HD, (head + 1) * HD)
+            vcut = slice(width + head * HD, width + (head + 1) * HD)
+            asked, grad = r.query[at, cut], grad_rows[:, cut]
+            scores = dot(asked, r.kvs[slot, :, cut], NT) * SCALE
+            probs, _ = softmax_rows(jnp.where(live, scores, masked_score))
+            dprobs = dot(grad, r.kvs[slot, :, vcut], NT)
+            delta = jnp.sum(probs * dprobs, axis=-1, keepdims=True)
+            dscores = (probs * (dprobs - delta)).astype(BF16)
+            r.dquery[at, cut] = (dot(dscores, r.kvs[slot, :, cut]) * SCALE).astype(BF16)
+            shape = (4, 2, source_rows, HD)
+            r.dkv_full[slot, :, :, :, cut] = (
+                (dot(dscores, asked, TN) * SCALE).astype(BF16).reshape(shape)
+            )
+            r.dkv_full[slot, :, :, :, vcut] = (
+                dot(probs.astype(BF16), grad, TN).astype(BF16).reshape(shape)
+            )
+        return carry
+
+    lax.fori_loop(0, 4, cross_back, 0)
+    dkv = Sum(links, place, r.dkv_full, r.dkv_into, r.dkv_away, r.dkv_result)
+    dkv.start()
+
+    own_down.wait()
+    own_up.wait()
+    up.turn((0,))
+    down.turn((0,))
+    up.start((2,))
+    down.start((2,))
+
+    get_self = Gather(links, place, r.self_branch, rows, PIECES)
+
+    def after_second(piece, total):
+        cut = slice(piece * step, (piece + 1) * step)
+        hat, inverse = norm_terms_of(r.sums[0, cut])
+        back, gain, bias = norm_backward(total, hat, inverse, r.gain[1:2])
+        add_norms(1, gain, bias)
+        value = r.grad_sum[cut] + back
+        r.grad_sum[cut] = value
+        r.self_branch[rows_at(p.s * rows + piece * step, step)] = value.astype(BF16)
+        get_self.start(piece)
+
+    Reduce(links, place, r.rs_out.at[1], r.rs_in.at[1], rows, PIECES).run(
+        lambda block, piece: dot(
+            r.dquery[rows_at(block * rows + piece * step, step)], r.w_cq[...], NT
+        ),
+        after_second,
+    )
+
+    def row_grad(left, right, full):
+        def one(part, carry):
+            lanes = lanes_at(part * 128, 128)
+            value = dot(left[:, lanes], right[...], TN).astype(BF16)
+            full[pl.ds(part * 2, 2)] = value.reshape((2, 2) + full.shape[2:])
+            return carry
+
+        lax.fori_loop(0, left.shape[1] // 128, one, 0)
+
+    def column_grad(left, right, full):
+        def one(block, carry):
+            lanes = lanes_at(block * share, share)
+            value = dot(left[:, lanes], right(), TN).astype(BF16)
+            full[pl.ds(block, 1)] = value.reshape((1,) + full.shape[1:])
+            return carry
+
+        lax.fori_loop(0, 4, one, 0)
+
+    row_grad(r.cross, r.cross_branch, r.co_full)
+    for piece in range(PIECES):
+        get_self.forward(piece)
+    column_grad(r.second, lambda: r.dquery[...], r.cq_full)
+    for piece in range(PIECES):
+        get_self.finish(piece)
+
+    need("w_out", "heads", "mix")
+
+    def mix_back(slot, carry):
+        value = dot(r.self_branch[rows_at(slot * rows, rows)], r.w_out[...], NT).astype(BF16)
+        for group in range(groups):
+            r.gsent[slot * groups + group] = value[:, group * pair_width : (group + 1) * pair_width]
+        return carry
+
+    lax.fori_loop(0, 4, mix_back, 0)
+    a2a = links.slots(STEPS)
+    mine_rows = rows_at(p.c * rows, rows)
+    for hop in range(1, STEPS):
+        other = lax.rem(p.c + hop, STEPS)
+        links.push(a2a + hop, r.gsent.at[other], r.gheads.at[mine_rows], (p.s, other))
+    r.gheads[mine_rows] = r.gsent[p.c]
+    for owner in range(STEPS):
+        r.columns[:, owner * rows : (owner + 1) * rows] = column_positions(r.table, owner, half)
+    row_grad(r.mix, r.self_branch, r.so_full)
+    dkv.turn()
+    up.turn((1,))
+    down.turn((1,))
+    up.start((3,))
+    down.start((3,))
+    co = Sum(links, place, r.co_full, r.co_into, r.co_away, r.co_result, True)
+    cq = Sum(links, place, r.cq_full, r.cq_into, r.cq_away, r.cq_result)
+    so = Sum(links, place, r.so_full, r.so_into, r.so_away, r.so_result, True)
+    for hop in range(1, STEPS):
+        other = lax.rem(p.c + STEPS - hop, STEPS)
+        links.take(a2a + hop, r.gheads.at[rows_at(other * rows, rows)], (p.s, other))
+
+    my_slot, my_group = lax.div(p.c, groups), lax.rem(p.c, groups)
+    length = r.lens[pl.ds(my_slot, 1)][0, 0:1, 0:1]
+    slot_rows = rows_at(my_slot * rows, rows)
+    group_lanes = lanes_at(my_group * pair_width, pair_width)
+    back_q, back_kv = links.slots(STEPS), links.slots(STEPS)
+    r.acc[...] = jnp.zeros_like(r.acc)
+
+    def q_copy(owner):
+        at = rows_at(owner * rows, rows)
+        return links.copy(
+            back_q + p.c, r.dq_own.at[at], r.dproj.at[0, slot_rows, group_lanes], (p.s, owner)
+        )
+
+    def kv_copy(owner):
+        at = rows_at(owner * rows, rows)
+        return links.copy(
+            back_kv + p.c,
+            r.dkv_own.at[:, at],
+            r.dproj.at[pl.ds(1, 2), slot_rows, group_lanes],
+            (p.s, owner),
+        )
+
+    def attend_back(block, carry):
+        at = rows_at(block * 2 * rows, 2 * rows)
+        row_pos = jnp.concatenate(
+            [
+                row_positions(r.table, 2 * block, half),
+                row_positions(r.table, 2 * block + 1, half),
+            ],
+            axis=0,
+        )
+        col_pos = r.columns[...]
+        allowed = (col_pos <= row_pos) & (col_pos < length)
+        for head in range(pair_width // HD):
+            cut = slice(head * HD, (head + 1) * HD)
+            asked, grad = r.heads[0, at, cut], r.gheads[at, cut]
+            scores = dot(asked, r.heads[1, :, cut], NT) * SCALE
+            probs, _ = softmax_rows(jnp.where(allowed, scores, masked_score))
+            dprobs = dot(grad, r.heads[2, :, cut], NT)
+            delta = jnp.sum(probs * dprobs, axis=-1, keepdims=True)
+            dscores = (probs * (dprobs - delta)).astype(BF16)
+            r.dq_own[at, cut] = (dot(dscores, r.heads[1, :, cut]) * SCALE).astype(BF16)
+            r.acc[0, :, cut] += dot(dscores, asked, TN)
+            r.acc[1, :, cut] += dot(probs.astype(BF16), grad, TN)
+        return carry
+
+    for block in range(STEPS // 2):
+        attend_back(block, 0)
+        for owner in (2 * block, 2 * block + 1):
+            pl.when(p.c != owner)(q_copy(owner).start)
+    for owner in range(STEPS):
+        at = rows_at(owner * rows, rows)
+        r.dkv_own[0, at] = (r.acc[0, at] * SCALE).astype(BF16)
+        r.dkv_own[1, at] = r.acc[1, at].astype(BF16)
+        pl.when(p.c != owner)(kv_copy(owner).start)
+    r.dproj[0, slot_rows, group_lanes] = r.dq_own[mine_rows]
+    r.dproj[pl.ds(1, 2), slot_rows, group_lanes] = r.dkv_own[:, mine_rows]
+
+    co.start()
+    cq.start()
+    so.start()
+    need("w_ckv", "source")
+    dkv.finish()
+    r.dsource[...] = r.dkv_result[...].reshape(4 * source_rows, 2 * width)
+    column_grad(r.source, lambda: r.dsource[...], r.ckv_full)
+    ckv = Sum(links, place, r.ckv_full, r.ckv_into, r.ckv_away, r.ckv_result)
+    ckv.start()
+
+    def after_output(piece, total):
+        cut = slice(piece * step, (piece + 1) * step)
+        valid = own_rows[cut] < r.target[0]
+        r.output[cut] = jnp.where(valid, r.sums[1, cut] + total, 0.0).astype(BF16)
+
+    Reduce(links, place, r.rs_out.at[2], r.rs_in.at[2], rows, PIECES).run(
+        stored(r.third_part), after_output
+    )
+
+    def after_encoder(piece, total):
+        r.grad_source[...] = total
+
+    Reduce(links, place, r.enc_out, r.enc_in, source_rows).run(
+        lambda block, piece: dot(
+            r.dsource[rows_at(block * source_rows, source_rows)], r.w_ckv[...], NT
+        ),
+        after_encoder,
+    )
+
+    need("w_qkv", "first")
+    for owner in range(STEPS):
+
+        @pl.when(p.c != owner)
+        def _():
+            at = pl.ds((owner // groups) * rows, rows)
+            lane = lanes_at((owner % groups) * pair_width, pair_width)
+            links.take(back_q + owner, r.dproj.at[0, at, lane], (p.s, owner))
+            links.take(back_kv + owner, r.dproj.at[pl.ds(1, 2), at, lane], (p.s, owner))
+
+    def first_partial(block, piece):
+        at = rows_at(block * rows + piece * step, step)
+        total = dot(r.dproj[0, at], r.w_qkv[:, :width], NT)
+        total += dot(r.dproj[1, at], r.w_qkv[:, width : 2 * width], NT)
+        return total + dot(r.dproj[2, at], r.w_qkv[:, 2 * width :], NT)
+
+    def after_first(piece, total):
+        cut = slice(piece * step, (piece + 1) * step)
+        hat, inverse = norm_terms_of(r.tokens[0, cut].astype(F32))
+        back, gain, bias = norm_backward(total, hat, inverse, r.gain[0:1])
+        add_norms(0, gain, bias)
+        r.grad_inputs[cut] = r.grad_sum[cut] + back
+
+    def qkv_grad(block, carry):
+        lanes = lanes_at(block * share, share)
+        left = r.first[:, lanes]
+        for part in range(3):
+            value = dot(left, r.dproj[part], TN).astype(BF16)
+            r.qkv_full[pl.ds(block, 1), :, :, :, part * width : (part + 1) * width] = value.reshape(
+                (1,) + r.qkv_full.shape[1:4] + (width,)
+            )
+        return carry
+
+    lax.fori_loop(0, 4, qkv_grad, 0)
+    qkv = Sum(links, place, r.qkv_full, r.qkv_into, r.qkv_away, r.qkv_result)
+    qkv.start()
+    Reduce(links, place, r.rs_out.at[3], r.rs_in.at[3], rows, PIECES).run(first_partial, after_first)
+
+    norm_seq, norm_ctx = links.slots(3), links.slots(STEPS)
+    others = (p.far, p.opp, p.sib)
+    for hop, other in enumerate(others):
+        links.push(
+            norm_seq + hop,
+            r.norms.at[:, lanes_at(other * share, share)],
+            r.norms_seq.at[pl.ds(p.s, 1)].at[0],
+            (other, p.c),
+        )
+    up.turn((2,))
+    down.turn((2,))
+    total = r.norms[:, lanes_at(p.s * share, share)]
+    for hop, other in enumerate(others):
+        links.take(norm_seq + hop, r.norms_seq.at[pl.ds(other, 1)].at[0], (other, p.c))
+        total = total + r.norms_seq[pl.ds(other, 1)][0]
+    r.norms_ctx[pl.ds(p.c, 1)] = total[None]
+    own_norms = r.norms_ctx.at[pl.ds(p.c, 1)]
+    for hop in range(1, STEPS):
+        links.push(norm_ctx + hop, own_norms, own_norms, (p.s, lax.rem(p.c + hop, STEPS)))
+    up.turn((3,))
+    down.turn((3,))
+    for job in (co, cq, so, ckv, qkv):
+        job.turn()
+    sums = {}
+    up.finish()
+    sums["up"] = Exchange(links, place, r.up_result, r.up_taken)
+    sums["up"].start()
+    down.finish()
+    links.save(r.down_result, r.down_hbm)
+    for job in (co, so):
+        job.finish()
+    for name, job in (("cq", cq), ("ckv", ckv), ("qkv", qkv)):
+        job.finish()
+        sums[name] = Exchange(links, place, getattr(r, name + "_result"), getattr(r, name + "_taken"))
+        sums[name].start()
+    for hop in range(1, STEPS):
+        other = lax.rem(p.c + STEPS - hop, STEPS)
+        links.take(norm_ctx + hop, r.norms_ctx.at[pl.ds(other, 1)], (p.s, other))
+    total = r.norms_ctx[0]
+    for owner in range(1, STEPS):
+        total = total + r.norms_ctx[owner]
+    r.norm_sum[...] = total
+    for hop, other in enumerate(others):
+        links.take(peak_seq + hop, r.peaks_seq.at[pl.ds(other, 1)], (other, p.c))
+    for job in sums.values():
+        job.finish()
+    for owner in range(STEPS):
+        pl.when(p.c != owner)(q_copy(owner).wait_send)
+        pl.when(p.c != owner)(kv_copy(owner).wait_send)
+    links.finish()
+
+
+def backward_call(kept, given):
+    rows, depth = given["tokens"].shape[1:]
+    width = kept["w_cq"].shape[1]
+    source_rows = kept["source"].shape[0] // 4
+    keys = kept["kvs"].shape[1]
+    share = depth // 32
+    hidden = kept["w_up"].shape[1]
+    any_space = pl.BlockSpec(memory_space=pl.ANY)
+    vmem = pl.BlockSpec(memory_space=pltpu.VMEM)
+    smem = pl.BlockSpec(memory_space=pltpu.SMEM)
+    inputs = dict(
+        table=(smem, given["table"]),
+        target=(smem, given["target"]),
+        tokens=(vmem, given["tokens"]),
+        cotangent=(vmem, given["cotangent"]),
+        gain=(vmem, given["gain"]),
+        peak=(vmem, kept["peak"]),
+        lens=(vmem, kept["lens"]),
+        grad_third=(vmem, given["grad_third"]),
+        third_part=(vmem, given["third_part"]),
+        up_full=(any_space, given["grad_up"].reshape(4, 4, 2, share, hidden)),
+        down_full=(any_space, given["grad_down"].reshape(4, 2, hidden // (8 * share), share, depth)),
+    )
+    loaded = dict(
+        sums=kept["sums"],
+        w_co=given["cross_out"],
+        cross=kept["cross"],
+        query=kept["query"],
+        kvs=kept["kvs"],
+        w_cq=kept["w_cq"],
+        second=kept["second"],
+        w_out=given["self_out"],
+        heads=kept["heads"],
+        mix=kept["mix"],
+        w_ckv=kept["w_ckv"],
+        source=kept["source"],
+        w_qkv=kept["w_qkv"],
+        first=kept["first"],
+    )
+    for name, value in loaded.items():
+        inputs[name + "_hbm"] = (any_space, value)
+    outs = dict(
+        output=((rows, depth), BF16),
+        grad_inputs=((rows, depth), F32),
+        grad_source=((source_rows, depth), F32),
+        down_hbm=((hidden // (8 * share), share, depth), BF16),
+        co_result=((1, share, depth), BF16),
+        so_result=((1, share, depth), BF16),
+        up_taken=((4, share, hidden), BF16),
+        cq_taken=((4, share, width), BF16),
+        ckv_taken=((4, share, 2 * width), BF16),
+        qkv_taken=((4, share, 3 * width), BF16),
+        norm_sum=((8, depth // 4), F32),
+        peaks_seq=((4, 8, 128), F32),
+    )
+    down_blocks = hidden // (8 * share)
+    scratch = {name: (value.shape, value.dtype) for name, value in loaded.items()}
+    scratch |= dict(
+        down_own=((4, down_blocks, share, depth), BF16),
+        down_into=((4, down_blocks, share, depth), BF16),
+        down_away=((3, down_blocks, share, depth), BF16),
+        down_result=((down_blocks, share, depth), BF16),
+        up_own=((4, 4, share, hidden), BF16),
+        up_into=((4, 4, share, hidden), BF16),
+        up_away=((3, 4, share, hidden), BF16),
+        up_result=((4, share, hidden), BF16),
+        peaks_ctx=((8, 8, 128), F32),
+        norms=((8, depth), F32),
+        norms_seq=((4, 8, depth // 4), F32),
+        norms_ctx=((8, 8, depth // 4), F32),
+        cross_branch=((4 * rows, depth), BF16),
+        self_branch=((4 * rows, depth), BF16),
+        grad_sum=((rows, depth), F32),
+        rs_out=((4, 3, rows, depth), BF16),
+        rs_in=((4, 3, rows, depth), BF16),
+        enc_out=((3, source_rows, depth), BF16),
+        enc_in=((3, source_rows, depth), BF16),
+        dquery=((4 * rows, width), BF16),
+        dsource=((4 * source_rows, 2 * width), BF16),
+        gsent=((8, rows, 128), BF16),
+        gheads=((8 * rows, 128), BF16),
+        columns=((1, 8 * rows), jnp.int32),
+        acc=((2, 8 * rows, 128), F32),
+        dq_own=((8 * rows, 128), BF16),
+        dkv_own=((2, 8 * rows, 128), BF16),
+        dproj=((3, 4 * rows, width), BF16),
+    )
+    for name in ("co", "so"):
+        scratch[name + "_full"] = ((4, 2, 1, share, depth), BF16)
+        scratch[name + "_into"] = ((4, 1, share, depth), BF16)
+        scratch[name + "_away"] = ((3, 1, share, depth), BF16)
+    for name, columns, r in (
+        ("cq", width, share),
+        ("ckv", 2 * width, share),
+        ("qkv", 3 * width, share),
+        ("dkv", 2 * width, source_rows),
+    ):
+        scratch[name + "_full"] = ((4, 4, 2, r, columns), BF16)
+        scratch[name + "_into"] = ((4, 4, r, columns), BF16)
+        scratch[name + "_away"] = ((3, 4, r, columns), BF16)
+        scratch[name + "_result"] = ((4, r, columns), BF16)
+    sems = dict(send_sem=224, recv_sem=224, local_sem=4, load_sem=len(loaded))
+    names = list(inputs) + list(outs) + list(scratch) + list(sems)
+
+    def kernel(*refs):
+        held = dict(zip(names, refs), loaded=tuple(loaded))
+        backward_body(type("Refs", (), held))
+
+    made = pl.pallas_call(
+        kernel,
+        in_specs=[spec for spec, _ in inputs.values()],
+        out_specs=[any_space if name == "down_hbm" else vmem for name in outs],
+        out_shape=[jax.ShapeDtypeStruct(*shape) for shape in outs.values()],
+        scratch_shapes=[pltpu.VMEM(*shape) for shape in scratch.values()]
+        + [pltpu.SemaphoreType.DMA((count,)) for count in sems.values()],
+        compiler_params=pltpu.CompilerParams(
+            collective_id=1, has_side_effects=True, vmem_limit_bytes=60 * 2**20
+        ),
+        name="backward",
+    )(*[value for _, value in inputs.values()])
+    return dict(zip(outs, made))
+
+
+def finish_kernel(
+    clip_ref,
+    peaks_ref,
+    norm_ref,
+    qkv_w,
+    cq_w,
+    ckv_w,
+    output_ref,
+    inputs_ref,
+    source_ref,
+    down_ref,
+    co_ref,
+    so_ref,
+    up_ref,
+    cq_ref,
+    ckv_ref,
+    qkv_ref,
+    output_out,
+    inputs_out,
+    source_out,
+    qkv_out,
+    so_out,
+    cq_out,
+    ckv_out,
+    co_out,
+    up_out,
+    down_out,
+    gain_out,
+    bias_out,
+    self_out,
+    cross_out,
+):
+    output_out[0] = output_ref[...]
+    inputs_out[0] = inputs_ref[...]
+    source_out[0] = source_ref[...]
+    share = so_out.shape[0]
+    so_out[...] = so_ref[0].astype(F32)
+    co_out[...] = co_ref[0].astype(F32)
+    for block in range(down_ref.shape[0]):
+        down_out[block * share : (block + 1) * share] = down_ref[block].astype(F32)
+
+    def columns(out, taken, parts):
+        whole, width = out.shape[1] // parts, out.shape[1] // (4 * parts)
+        for owner in range(4):
+            for part in range(parts):
+                at = part * whole + owner * width
+                out[:, at : at + width] = taken[owner, :, part * width : (part + 1) * width].astype(
+                    F32
+                )
+
+    columns(up_out, up_ref, 1)
+    columns(cq_out, cq_ref, 1)
+    columns(ckv_out, ckv_ref, 2)
+    columns(qkv_out, qkv_ref, 3)
+    spread = gain_out.shape[1]
+    turned = pltpu.roll(norm_ref[...], norm_ref.shape[1] - lax.axis_index("ctx") * spread, 1)
+    gain_out[...] = turned[0:3, :spread]
+    bias_out[...] = turned[3:6, :spread]
+    lane = lax.broadcasted_iota(jnp.int32, (1, 128), 1)
+    held = peaks_ref.shape[1] // 2
+    for owner in range(4):
+        for two in range(held // 2):
+            head = owner * held + two * 2
+            at = slice(head * HD, head * HD + 128)
+            for kind, jobs in (
+                (0, ((self_out, qkv_w, 0, 0), (self_out, qkv_w, H * HD, H * HD))),
+                (1, ((cross_out, cq_w, 0, 0), (cross_out, ckv_w, 0, H * HD))),
+            ):
+                top = [peaks_ref[owner, kind * held + two * 2 + i : kind * held + two * 2 + i + 1] for i in (0, 1)]
+                limit = [clip_ref[kind, head + i] for i in (0, 1)]
+                limits = jnp.where(lane < HD, limit[0], limit[1])
+                tops = jnp.where(lane < HD, top[0], top[1])
+                factor = jnp.sqrt(limits / jnp.maximum(tops, limits))
+                for out, weight, start, goal in jobs:
+                    out[:, goal + head * HD : goal + head * HD + 128] = (
+                        weight[:, start + head * HD : start + head * HD + 128].astype(F32) * factor
+                    ).astype(BF16)
+
+
+def finish_call(made, given):
+    rows, depth = given["tokens"].shape[1:]
+    hidden = given["mlp_up"].shape[1]
+    source_rows, share = made["grad_source"].shape[0], made["so_result"].shape[1]
+    columns = H * HD
+    weight_rows = given["self_qkv"].shape[0]
+    shapes = [
+        ((1, rows, depth), BF16),
+        ((1, rows, depth), F32),
+        ((1, source_rows, depth), F32),
+        ((share, 3 * columns), F32),
+        ((share, depth), F32),
+        ((share, columns), F32),
+        ((share, 2 * columns), F32),
+        ((share, depth), F32),
+        ((share, hidden), F32),
+        ((hidden // 32, depth), F32),
+        ((3, share), F32),
+        ((3, share), F32),
+        ((weight_rows, 2 * columns), BF16),
+        ((weight_rows, 2 * columns), BF16),
+    ]
+    vmem = pl.BlockSpec(memory_space=pltpu.VMEM)
+    return pl.pallas_call(
+        finish_kernel,
+        in_specs=[pl.BlockSpec(memory_space=pltpu.SMEM)] + [vmem] * 15,
+        out_specs=[vmem] * len(shapes),
+        out_shape=[jax.ShapeDtypeStruct(*shape) for shape in shapes],
+        compiler_params=pltpu.CompilerParams(vmem_limit_bytes=48 * 2**20),
+        name="finish",
+    )(
+        given["clip"],
+        made["peaks_seq"],
+        made["norm_sum"],
+        given["self_qkv"],
+        given["cross_q"],
+        given["cross_kv"],
+        made["output"],
+        made["grad_inputs"],
+        made["grad_source"],
+        made["down_hbm"],
+        made["co_result"],
+        made["so_result"],
+        made["up_taken"],
+        made["cq_taken"],
+        made["ckv_taken"],
+        made["qkv_taken"],
+    )
 
 
 def fast_device(
@@ -1409,39 +1868,6 @@
     norm_bias,
     clip_limit,
 ):
-    rows = tokens.shape[1]
-    source_rows = encoder_states.shape[1]
-    seq_count, ctx_count = lax.axis_size("seq"), lax.axis_size("ctx")
-    seq_index, ctx_index = lax.axis_index("seq"), lax.axis_index("ctx")
-    held, pair = H // seq_count, H // ctx_count
-    groups = held // pair
-    own_width, pair_width = held * HD, pair * HD
-    width = H * HD
-    half = rows // 2
-    all_positions = (
-        block_table[:, :, None] * half + jnp.arange(half, dtype=jnp.int32)[None, None, :]
-    ).reshape(-1)
-    own_positions = lax.dynamic_slice_in_dim(all_positions, ctx_index * rows, rows, 0)
-    valid_rows = (own_positions < target_lengths[0])[:, None]
-    my_slot = ctx_index // groups
-
-    inputs = tokens[0].astype(F32)
-    hat_one, inverse_one, _ = norm_forward(inputs, norm_gain[0], norm_bias[0])
-    grad_rows = jnp.where(valid_rows, cotangent[0].astype(F32), 0.0)
-
-    def to_heads(blocks, parts):
-        blocks = blocks.reshape(seq_count, rows, parts, groups, pair_width)
-        blocks = blocks.transpose(0, 3, 2, 1, 4).reshape(ctx_count, parts * rows, pair_width)
-        taken = swap(blocks, "ctx").reshape(ctx_count, parts, rows, pair_width)
-        return taken.transpose(1, 0, 2, 3).reshape(parts, ctx_count * rows, pair_width)
-
-    def to_rows(heads):
-        parts = heads.shape[0]
-        blocks = heads.reshape(parts, ctx_count, rows, pair_width).transpose(1, 0, 2, 3)
-        taken = swap(blocks.reshape(ctx_count, parts * rows, pair_width), "ctx")
-        taken = taken.reshape(seq_count, groups, parts, rows, pair_width).transpose(0, 3, 2, 1, 4)
-        return taken.reshape(seq_count * rows, parts * own_width)
-
     kept = forward_call(
         block_table,
         target_lengths,
@@ -1458,107 +1884,33 @@
         norm_gain,
         norm_bias,
     )
-    first_low, second_low, third_low = kept["first"], kept["second"], kept["third"]
-    mlp_branch, source_low = kept["branch"], kept["source"]
-    w_qkv, w_cq, w_ckv, w_up = kept["w_qkv"], kept["w_cq"], kept["w_ckv"], kept["w_up"]
-    qkv, self_low, cross_kvs, cross_low = kept["heads"], kept["mix"], kept["kvs"], kept["cross"]
-    cross_query = kept["query"].reshape(seq_count, rows, own_width)
-    first_sum, second_sum = kept["sums"][0], kept["sums"][1]
-    self_peak, cross_peak = kept["peak"], kept["peak"][2:]
-    targets, sources = kept["lens"][:, 0, 0], kept["lens"][:, 4, 0]
-    my_length = lax.dynamic_slice_in_dim(targets, my_slot, 1, 0)
-    hat_two, inverse_two, _ = norm_forward(first_sum, norm_gain[1], norm_bias[1])
-    hat_three, inverse_three, _ = norm_forward(second_sum, norm_gain[2], norm_bias[2])
-
+    third_low, mlp_branch, w_up = kept["third"], kept["branch"], kept["w_up"]
     hidden_pre = dot(third_low, w_up)
     hidden_act, gelu_back = jax.vjp(jax.nn.gelu, hidden_pre)
     hidden_low = hidden_act.astype(BF16)
-    third_sum = second_sum + scatter_seq(dot(hidden_low, mlp_down))
-    output_rows = jnp.where(valid_rows, third_sum, 0.0).astype(BF16)
-
-    peak_self = lax.dynamic_update_slice_in_dim(
-        jnp.full((H,), masked_score, F32),
-        self_peak[:pair, 0],
-        seq_index * held + (ctx_index % groups) * pair,
-        0,
-    )
-    peak_cross = lax.dynamic_update_slice_in_dim(
-        jnp.full((H,), masked_score, F32), cross_peak[:held, 0], seq_index * held, 0
-    )
-    peaks = lax.pmax(jnp.stack([peak_self, peak_cross]), ("seq", "ctx"))
-
-    grad_down = dot(hidden_low, mlp_branch, TN)
     grad_pre = gelu_back(dot(mlp_branch, mlp_down, NT))[0].astype(BF16)
-    grad_up = dot(third_low, grad_pre, TN)
-    back_three, gain_three, bias_three = norm_backward(
-        scatter_seq(dot(grad_pre, w_up, NT)), hat_three, inverse_three, norm_gain[2]
-    )
-    up_shard, down_shard = finish_columns(grad_up, 1), finish_rows(grad_down)
-
-    grad_second = grad_rows + back_three
-    cross_branch = gather_seq(grad_second.astype(BF16))
-    grad_co = dot(cross_low, cross_branch, TN)
-    cross_grad = dot(cross_branch, cross_out, NT).astype(BF16)
-    dquery, dkv = cross_backward(
-        cross_query, cross_kvs, sources, cross_grad.reshape(seq_count, rows, own_width)
-    )
-    dquery = dquery.reshape(seq_count * rows, own_width)
-    dkv = (
-        dkv.reshape(seq_count, ctx_count, source_rows, 2 * own_width)
-        .transpose(1, 0, 2, 3)
-        .reshape(ctx_count * seq_count * source_rows, 2 * own_width)
-    )
-    grad_source_kv = lax.psum_scatter(dkv, "ctx", scatter_dimension=0, tiled=True)
-    grad_cq = dot(second_low, dquery, TN)
-    grad_ckv = dot(source_low, grad_source_kv, TN)
-    grad_source = scatter_seq(dot(grad_source_kv, w_ckv, NT))
-    back_two, gain_two, bias_two = norm_backward(
-        scatter_seq(dot(dquery, w_cq, NT)), hat_two, inverse_two, norm_gain[1]
-    )
-    grad_first = grad_second + back_two
-    self_branch = gather_seq(grad_first.astype(BF16))
-    grad_so = dot(self_low, self_branch, TN)
-    self_grad = to_heads(dot(self_branch, self_out, NT).astype(BF16), 1)[0]
-    grad_projected = to_rows(self_backward(qkv, all_positions, my_length, self_grad))
-    grad_qkv = dot(first_low, grad_projected, TN)
-    back_one, gain_one, bias_one = norm_backward(
-        scatter_seq(dot(grad_projected, w_qkv, NT)), hat_one, inverse_one, norm_gain[0]
-    )
-    grad_inputs = grad_first + back_one
-
-    norm_terms = jnp.stack([gain_one, gain_two, gain_three, bias_one, bias_two, bias_three])
-    norm_sum = lax.psum(norm_terms, ("seq", "ctx"))
-    norm_share = width // (seq_count * ctx_count)
-    norm_shard = lax.dynamic_slice_in_dim(
-        norm_sum, (seq_index * ctx_count + ctx_index) * norm_share, norm_share, 1
-    )
-
-    factors = jnp.sqrt(clip_limit / jnp.maximum(peaks, clip_limit))
-    columns = jnp.repeat(factors, HD, axis=1)
-    qkv_wide = self_qkv.astype(F32)
-    clipped_self = jnp.concatenate(
-        [qkv_wide[:, :width] * columns[0], qkv_wide[:, width : 2 * width] * columns[0]], axis=1
-    ).astype(BF16)
-    clipped_cross = jnp.concatenate(
-        [cross_q.astype(F32) * columns[1], cross_kv[:, :width].astype(F32) * columns[1]], axis=1
-    ).astype(BF16)
-    return (
-        output_rows[None],
-        grad_inputs[None],
-        grad_source[None],
-        finish_columns(grad_qkv, 3),
-        finish_rows(grad_so),
-        finish_columns(grad_cq, 1),
-        finish_columns(grad_ckv, 2),
-        finish_rows(grad_co),
-        up_shard,
-        down_shard,
-        norm_shard[:3],
-        norm_shard[3:],
-        clipped_self,
-        clipped_cross,
-        peaks,
-    )
+    given = dict(
+        table=block_table,
+        target=target_lengths,
+        tokens=tokens,
+        cotangent=cotangent,
+        gain=norm_gain,
+        grad_third=dot(grad_pre, w_up, NT).astype(BF16),
+        third_part=dot(hidden_low, mlp_down).astype(BF16),
+        grad_up=dot(third_low, grad_pre, TN).astype(BF16),
+        grad_down=dot(hidden_low, mlp_branch, TN).astype(BF16),
+        cross_out=cross_out,
+        self_out=self_out,
+        self_qkv=self_qkv,
+        cross_q=cross_q,
+        cross_kv=cross_kv,
+        mlp_up=mlp_up,
+        clip=clip_limit,
+    )
+    made = backward_call(kept, given)
+    held = H // 4
+    tops = made["peaks_seq"][:, :, 0].reshape(4, 2, held).transpose(1, 0, 2).reshape(2, H)
+    return (*finish_call(made, given), tops)
 
 
 def solution(mesh):

time: 924 us -> 419 us (0.45)
  waiting for transfers between devices: 533 us -> 0 us
  Pallas kernels: 125 us -> 362 us
  blocking collectives: 102 us -> 0 us
  starting transfers between devices: 27.8 us -> 0 us
  other arithmetic: 26.6 us -> 0 us
  matrix products: 48.7 us -> 26.3 us
  between operations: 16.1 us -> 2.43 us
  local copies, waits for them, and re-layouts: 31.7 us -> 20.4 us
    reduce_scatter x13 -> x0, waiting for transfers between devices: 492 us -> none  [the longest x3 210 us: finish_rows(): lax.psum_scatter(grad.astype(BF16), 'ctx', scatter_dimension=0, tiled=True)]
    pallas_call x2, Pallas kernels: 21.4 us -> 259 us  [the longest x1 255 us: backward_call(): pl.pallas_call(kernel, in_specs=[spec for spec, _ in inputs.values()], ou...]
    psum x1 -> x0, blocking collectives: 38.6 us -> none  [fast_device(): norm_sum = lax.psum(norm_terms, ('seq', 'ctx'))]
    pmax x1 -> x0, blocking collectives: 38.3 us -> none  [fast_device(): peaks = lax.pmax(jnp.stack([peak_self, peak_cross]), ('seq', 'ctx'))]
    all_to_all x5 -> x0, starting transfers between devices: 26.7 us -> none  [swap(): return lax.all_to_all(blocks, axis, split_axis=0, concat_axis=0, tiled=True)]
    all_gather x2 -> x0, waiting for transfers between devices: 25.7 us -> none  [gather_seq(): return lax.all_gather(rows, 'seq', axis=0, tiled=True)]
    all_to_all x1 -> x0, blocking collectives: 25.3 us -> none  [swap(): return lax.all_to_all(blocks, axis, split_axis=0, concat_axis=0, tiled=True)]
    dot_general x16 -> x6, matrix products: 48.7 us -> 26.3 us  [dot(): lax.dot_general(left, right, (contract, ((), ())), preferred_element_type...]
  transfers between devices with their start and end apart: 20 -> 0, of which waited for: 17 -> 0; matrix products, arithmetic and copies ran while one was open for 8% -> 0% of each run, Pallas kernels for 1% -> 0%
where the time goes in v3:
time: 419 us; the launch traced here: 412 us
  Pallas kernels  362 us (86%)
  matrix products  26.3 us (6%)
  local copies, waits for them, and re-layouts  20.4 us (5%)
    pallas_call x1, Pallas kernels, backward_call(): pl.pallas_call(kernel, in_specs=[spec for spec, _ in inputs.values()], ou...  255 us
    pallas_call x1, Pallas kernels, forward_call(): pl.pallas_call(forward_kernel, in_specs=[smem] * 3 + [vmem] * 3 + [any_sp...  104 us
    dot_general x6, matrix products, dot(): lax.dot_general(left, right, (contract, ((), ())), preferred_element_type...  26.3 us
    unnamed x77, local copies, waits for them, and re-layouts  18.9 us

profile of v3, /device:TPU:29, one launch (start us, length us, event | category | flops | bytes accessed | tf_op | source)
XLA Modules:
  0.0 411.5 jit_solution(6445913654231152903)
XLA Ops:
  1.9 0.8 copy.35.table_ref.refs_0_
  2.7 1.0 copy-done.2
  3.7 1.0 copy-done.3
  4.8 1.0 copy-done.4
  5.8 0.9 copy-done.6
  6.8 0.9 copy-done.7
  7.7 0.8 copy-done.22
  8.6 0.7 copy-done.27
  9.3 0.7 copy-done.29
  10.0 103.7 %forward.1 = (bf16[512,1024]{1,0:T(8,128)(2,1)S(1)}, bf16[512,1024]{1,0:T(8,128)(2,1)}, bf16[512,1024]{1,0:T(8,128)(2,1)}, bf16[512,1024]{1,0:T(8,128)(2,1)}, bf...) custom-call(s32[8,2]{1,0:T(8,128)S(1)} %copy.35.table_ref.refs_0_, ...), custom_call_target="tpu_custom_call" | custom-call | tf_op jit(solution)/shard_map/forward/pallas_call | solution.py:1119
  113.7 0.0 copy-start.8
  113.7 0.0 copy-start.9
  113.7 0.0 copy-start.13
  113.7 0.0 copy-start.14
  113.7 0.0 copy-start.15
  113.8 0.0 copy-start.16
  113.8 0.0 copy-start.17
  113.8 0.0 copy-start.30
  113.8 0.0 copy-start.32
  113.8 4.5 %fusion.7 = f32[512,2048]{1,0:T(8,128)S(1)} fusion(bf16[512,1024]{1,0:T(8,128)(2,1)} %get-tuple-element.60, bf16[2048,1024]{1,0:T(8,128)(2,1)S(1)} %copy-done.34), kind=kOutput, calls=%fused_computation.15 | convolution fusion | flops 2147483648 | bytes 9437184 | tf_op jit(solution)/shard_map/dot_general | solution.py:516
  118.4 0.0 copy-done.8
  118.4 0.0 copy-done.9
  118.4 0.0 copy-done.13
  118.4 0.0 copy-done.14
  118.4 0.0 copy-done.15
  118.4 0.0 copy-done.16
  118.5 5.4 %fusion.6 = (bf16[512,2048]{1,0:T(8,128)(2,1)S(1)}, f32[512,2048]{1,0:T(8,128)S(1)}) fusion(f32[512,2048]{1,0:T(8,128)S(1)} %fusion.7, bf16[512,1024]{1,0:T(8,128)(2,1)S(1)} %copy-done.37, bf16[1024,2048]{1,0:T(8,128)(2,1)S(1)} %copy-done.35), kind=kOutput, calls=%fused_computation.8 | convolution fusion | flops 2168455168 | bytes 15728640 | tf_op jit(solution)/shard_map/dot_general | solution.py:516
  123.9 3.3 convolution_convert_fusion.3.refs_7_
  127.3 4.4 %convolution_convert_fusion.1 = bf16[1024,2048]{1,0:T(8,128)(2,1)} fusion(bf16[512,1024]{1,0:T(8,128)(2,1)S(1)} %copy-done.37, bf16[512,2048]{1,0:T(8,128)(2,1)S(1)} %get-tuple-element.101), kind=kOutput, calls=%fused_computation.11 | convolution fusion | flops 2149580800 | bytes 7340032 | tf_op jit(solution)/shard_map/dot_general | solution.py:516
  131.6 3.7 convolution_convert_fusion.2.refs_8_
  135.3 5.0 %convolution_convert_fusion = bf16[2048,1024]{1,0:T(8,128)(2,1)} fusion(bf16[512,1024]{1,0:T(8,128)(2,1)S(1)} %copy-done.36, f32[512,2048]{1,0:T(8,128)S(1)} %get-tuple-element.102), kind=kOutput, calls=%fused_computation.10 | convolution fusion | flops 2159017984 | bytes 9437184 | tf_op jit(solution)/shard_map/dot_general | solution.py:516
  140.3 255.3 %backward.1 = (bf16[128,1024]{1,0:T(8,128)(2,1)}, f32[128,1024]{1,0:T(8,128)}, f32[32,1024]{1,0:T(8,128)}, bf16[8,32,1024]{2,1,0:T(8,128)(2,1)}, bf16[1,32,1024]...) custom-call(s32[8,2]{1,0:T(8,128)} %copy-done.28, ...), custom_call_target="tpu_custom_call" | custom-call | tf_op jit(solution)/shard_map/backward/pallas_call | solution.py:1709
  395.7 0.8 slice_reduce_fusion
  396.5 0.1 reshape_squeeze.3
  396.6 0.6 reshape.41
  397.2 1.0 copy-done.10
  398.3 1.0 copy-done.11
  399.3 1.0 copy-done.12
  400.4 0.9 copy-done.18
  401.3 0.9 copy-done.19
  402.2 0.9 copy-done.20
  403.1 0.9 copy-done.21
  404.0 0.8 copy-done.23
  404.9 0.8 copy-done.24
  405.7 0.8 copy-done.25
  406.6 0.7 copy-done.26
  407.3 0.7 copy-done.31
  408.0 3.3 finish.1
  (42 shorter events, 0.1 us)
Async XLA Ops:
  2.7 1.0 copy-start.2
  3.7 1.0 copy-start.3
  4.8 1.0 copy-start.4
  5.8 0.9 copy-start.6
  6.8 0.9 copy-start.7
  7.7 0.8 copy-start.22
  8.6 0.7 copy-start.27
  9.3 0.7 copy-start.29
  10.0 103.7 %copy-start.28 = (s32[8,2]{1,0:T(8,128)}, s32[8,2]{1,0:T(8,128)S(1)}, u32[]{:S(2)}) copy-start(s32[8,2]{1,0:T(8,128)S(1)} %copy.35.table_ref.refs_0_) | copy-start | bytes 196
  10.0 103.8 %copy-start.34 = (bf16[2048,1024]{1,0:T(8,128)(2,1)S(1)}, bf16[2048,1024]{1,0:T(8,128)(2,1)}, u32[]{:S(2)}) copy-start(bf16[2048,1024]{1,0:T(8,128)(2,1)} %param.28) | copy-start | bytes 12582916
  113.7 4.7 %copy-start.8 = (bf16[512,1024]{1,0:T(8,128)(2,1)}, bf16[512,1024]{1,0:T(8,128)(2,1)S(1)}, u32[]{:S(2)}) copy-start(bf16[512,1024]{1,0:T(8,128)(2,1)S(1)} %get-tuple-element.74.refs_24_) | copy-start | bytes 3145732
  113.7 4.7 %copy-start.9 = (bf16[3,1024,128]{2,1,0:T(8,128)(2,1)}, bf16[3,1024,128]{2,1,0:T(8,128)(2,1)S(1)}, u32[]{:S(2)}) copy-start(bf16[3,1024,128]{2,1,0:T(8,128)(2,1)S(1)} %get-tuple-element.69.refs_19_) | copy-start | bytes 2359300
  113.7 4.7 %copy-start.13 = (bf16[1024,256]{1,0:T(8,128)(2,1)}, bf16[1024,256]{1,0:T(8,128)(2,1)S(1)}, u32[]{:S(2)}) copy-start(bf16[1024,256]{1,0:T(8,128)(2,1)S(1)} %get-tuple-element.67.refs_16_) | copy-start | bytes 1572868
  113.7 4.7 %copy-start.14 = (bf16[128,1024]{1,0:T(8,128)(2,1)}, bf16[128,1024]{1,0:T(8,128)(2,1)S(1)}, u32[]{:S(2)}) copy-start(bf16[128,1024]{1,0:T(8,128)(2,1)S(1)} %get-tuple-element.72.refs_22_) | copy-start | bytes 786436
  113.7 4.7 %copy-start.15 = (bf16[512,256]{1,0:T(8,128)(2,1)}, bf16[512,256]{1,0:T(8,128)(2,1)S(1)}, u32[]{:S(2)}) copy-start(bf16[512,256]{1,0:T(8,128)(2,1)S(1)} %get-tuple-element.70.refs_20_) | copy-start | bytes 786436
  113.8 4.7 %copy-start.16 = (bf16[512,256]{1,0:T(8,128)(2,1)}, bf16[512,256]{1,0:T(8,128)(2,1)S(1)}, u32[]{:S(2)}) copy-start(bf16[512,256]{1,0:T(8,128)(2,1)S(1)} %get-tuple-element.65.refs_14_) | copy-start | bytes 786436
  113.8 4.7 %copy-start.17 = (bf16[512,256]{1,0:T(8,128)(2,1)}, bf16[512,256]{1,0:T(8,128)(2,1)S(1)}, u32[]{:S(2)}) copy-start(bf16[512,256]{1,0:T(8,128)(2,1)S(1)} %get-tuple-element.64.refs_13_) | copy-start | bytes 786436
  113.8 4.7 %copy-start.30 = (s32[4,8,128]{2,1,0:T(8,128)}, s32[4,8,128]{2,1,0:T(8,128)S(1)}, u32[]{:S(2)}) copy-start(s32[4,8,128]{2,1,0:T(8,128)S(1)} %get-tuple-element.59.refs_6_) | copy-start | bytes 49156
  113.8 4.7 %copy-start.32 = (f32[8,128]{1,0:T(8,128)}, f32[8,128]{1,0:T(8,128)S(1)}, u32[]{:S(2)}) copy-start(f32[8,128]{1,0:T(8,128)S(1)} %get-tuple-element.58.refs_5_) | copy-start | bytes 12292
  113.8 4.7 %copy-start.35 = (bf16[1024,2048]{1,0:T(8,128)(2,1)S(1)}, bf16[1024,2048]{1,0:T(8,128)(2,1)}, u32[]{:S(2)}) copy-start(bf16[1024,2048]{1,0:T(8,128)(2,1)} %get-tuple-element.62) | copy-start | bytes 12582916
  113.8 4.7 %copy-start.37 = (bf16[512,1024]{1,0:T(8,128)(2,1)S(1)}, bf16[512,1024]{1,0:T(8,128)(2,1)}, u32[]{:S(2)}) copy-start(bf16[512,1024]{1,0:T(8,128)(2,1)} %get-tuple-element.61) | copy-start | bytes 3145732
  131.6 3.7 copy-start.36
  140.3 256.9 %copy-start = (bf16[256,3072]{1,0:T(8,128)(2,1)S(1)}, bf16[256,3072]{1,0:T(8,128)(2,1)}, u32[]{:S(2)}) copy-start(bf16[256,3072]{1,0:T(8,128)(2,1)} %qkv_w.1) | copy-start | bytes 4718596
  140.3 256.9 %copy-start.1 = (bf16[256,2048]{1,0:T(8,128)(2,1)S(1)}, bf16[256,2048]{1,0:T(8,128)(2,1)}, u32[]{:S(2)}) copy-start(bf16[256,2048]{1,0:T(8,128)(2,1)} %ckv_w.1) | copy-start | bytes 3145732
  140.3 256.9 %copy-start.5 = (bf16[256,1024]{1,0:T(8,128)(2,1)S(1)}, bf16[256,1024]{1,0:T(8,128)(2,1)}, u32[]{:S(2)}) copy-start(bf16[256,1024]{1,0:T(8,128)(2,1)} %cq_w.1) | copy-start | bytes 1572868
  140.3 256.9 %copy-start.33 = (f32[2,16]{1,0:T(2,128)S(1)}, f32[2,16]{1,0:T(2,128)}, u32[]{:S(2)}) copy-start(f32[2,16]{1,0:T(2,128)} %clip_ref.1) | copy-start | bytes 388
  397.2 1.0 copy-start.10
  398.3 1.0 copy-start.11
  399.3 1.0 copy-start.12
  400.4 0.9 copy-start.18
  401.3 0.9 copy-start.19
  402.2 0.9 copy-start.20
  403.1 0.9 copy-start.21
  404.0 0.8 copy-start.23
  404.9 0.8 copy-start.24
  405.7 0.8 copy-start.25
  406.6 0.7 copy-start.26
  407.3 0.7 copy-start.31
